TPU v7x, 32 devices: a whole 2x2x4 slice. The times are simulated.
32 devices in a mesh: ctx: 8 (over y, x, core), tp: 4 (over z).
Axes of the slice: x: 2, y: 2, z: 4, core: 2. Of those that a mesh axis runs over, the one named last changes fastest.
Arguments:
- hidden_in: bfloat16 [2, 4096, 2048], P(None, 'ctx'), may hold values from -6 to 6
- seq_lengths: int32 [2, 3], replicated, may hold values from 1 to 2048, 4096 in all within a row
- token_order: int32 [2, 4096], replicated, may hold values from 0 to 4095, each once within a row
- attn_gain: float32 [2048], replicated, may hold values from 0.5 to 1.5
- w_query: bfloat16 [2048, 2048], P('ctx', 'tp'), may hold values from -0.125 to 0.125
- w_key: bfloat16 [2048, 1024], P('ctx', 'tp'), may hold values from -0.125 to 0.125
- w_value: bfloat16 [2048, 1024], P('ctx', 'tp'), may hold values from -0.125 to 0.125
- query_gain: float32 [128], replicated, may hold values from 0.5 to 1.5
- key_gain: float32 [128], replicated, may hold values from 0.5 to 1.5
- w_out: bfloat16 [2048, 2048], P('tp', 'ctx'), may hold values from -1 to 1
- mlp_gain: float32 [2048], replicated, may hold values from 0.5 to 1.5
- w_gate: bfloat16 [2048, 6144], P('ctx', 'tp'), may hold values from -0.125 to 0.125
- w_up: bfloat16 [2048, 6144], P('ctx', 'tp'), may hold values from -0.125 to 0.125
- w_down: bfloat16 [6144, 2048], P('tp', 'ctx'), may hold values from -0.078125 to 0.078125
- cotangent: bfloat16 [2, 4096, 2048], P(None, 'ctx'), may hold values from -6 to 6
Outputs:
- layer_out: bfloat16 [2, 4096, 2048], P(None, 'ctx')
- grad_input: float32 [2, 4096, 2048], P(None, 'ctx')
- grad_attn_gain: float32 [2048], P('ctx')
- grad_query: float32 [2048, 2048], P('ctx', 'tp')
- grad_key: float32 [2048, 1024], P('ctx', 'tp')
- grad_value: float32 [2048, 1024], P('ctx', 'tp')
- grad_query_gain: float32 [128], replicated
- grad_key_gain: float32 [128], replicated
- grad_out: float32 [2048, 2048], P('tp', 'ctx')
- grad_mlp_gain: float32 [2048], P('ctx')
- grad_gate: float32 [2048, 6144], P('ctx', 'tp')
- grad_up: float32 [2048, 6144], P('ctx', 'tp')
- grad_down: float32 [6144, 2048], P('tp', 'ctx')
Inputs may be any that keep to these rules, and one draw needn't show every extreme that they name: `seq_lengths`: the 3 lengths of a micro-batch, packed in this order, fill its 4096 positions; the longest is exactly 2048. `token_order`: each row is a permutation of the packed positions; slots are dealt to the indices of ctx in runs of 512.
All inputs are finite; a program needn't handle non-finite values.
Results may differ from a plain program's by a relative error of at most 0.024.
Values may be sent and summed in bfloat16 or wider, within the bound.
A program may use at most 128 MiB of HBM per device.

v0:
```python
import math

import jax
import jax.numpy as jnp
from jax import lax
from jax.sharding import PartitionSpec as P

EPSILON = 1e-06
THETA = 1000000.0
MASKED = -1e30


def layout(lengths_row, order_row):
    seq_ends = jnp.cumsum(lengths_row)
    seq_starts = seq_ends - lengths_row
    segment = jnp.sum((order_row[:, None] >= seq_ends[None, :]).astype(jnp.int32), axis=1)
    matches = segment[:, None] == jnp.arange(lengths_row.shape[0], dtype=jnp.int32)[None, :]
    offset = jnp.sum(jnp.where(matches, seq_starts[None, :], 0), axis=1)
    return (segment, order_row - offset)


def angles_of(position, head_size):
    inverse = jnp.exp(
        jnp.arange(head_size // 2, dtype=jnp.float32) * (-2.0 * math.log(THETA) / head_size)
    )
    return position.astype(jnp.float32)[:, None] * inverse[None, :]


def rotate(values, cosine, sine_part):
    half_size = values.shape[-1] // 2
    front_part = values[..., :half_size]
    back_part = values[..., half_size:]
    return jnp.concatenate(
        [front_part * cosine - back_part * sine_part, back_part * cosine + front_part * sine_part],
        axis=-1,
    )


def unrotate(grads, cosine, sine_part):
    half_size = grads.shape[-1] // 2
    front_part = grads[..., :half_size]
    back_part = grads[..., half_size:]
    return jnp.concatenate(
        [front_part * cosine + back_part * sine_part, back_part * cosine - front_part * sine_part],
        axis=-1,
    )


def norm_back(grad_rows, normalized, inverse_rms, gain_vec):
    scaled = grad_rows * gain_vec
    return inverse_rms * (
        scaled - normalized * jnp.mean(scaled * normalized, axis=-1, keepdims=True)
    )


def contract_rows(left_side, right_side):
    return lax.dot_general(
        left_side, right_side, (((0,), (0,)), ((), ())), preferred_element_type=jnp.float32
    )


def times_transpose(left_side, right_side):
    return lax.dot_general(
        left_side, right_side, (((1,), (1,)), ((), ())), preferred_element_type=jnp.float32
    )


def split_blocks(key_all, value_all, segment_all, packed_all, head_size):
    total_rows = key_all.shape[0]
    block_rows = min(1024, total_rows)
    block_count = total_rows // block_rows
    key_heads = key_all.shape[1] // head_size
    return (
        key_all.reshape(block_count, block_rows, key_heads, head_size),
        value_all.reshape(block_count, block_rows, key_heads, head_size),
        segment_all.reshape(block_count, block_rows),
        packed_all.reshape(block_count, block_rows),
    )


def block_scores(query_grouped, pieces, segment_own, packed_own):
    score_scale = query_grouped.shape[-1] ** (-0.5)
    scores = (
        jnp.einsum("qngd,knd->ngqk", query_grouped, pieces[0], preferred_element_type=jnp.float32)
        * score_scale
    )
    allowed = (segment_own[:, None] == pieces[2][None, :]) & (
        pieces[3][None, :] <= packed_own[:, None]
    )
    return jnp.where(allowed[None, None], scores, MASKED)


def attend_forward(query_grouped, blocks, segment_own, packed_own):
    tok_rows, key_heads, group_size, head_size = query_grouped.shape

    def value_step(carry, pieces):
        peak_score, mass_sum, running = carry
        scores = block_scores(query_grouped, pieces, segment_own, packed_own)
        new_peak = jnp.maximum(peak_score, jnp.max(scores, axis=-1))
        factor = jnp.exp(peak_score - new_peak)
        expo = jnp.exp(scores - new_peak[..., None])
        mass_sum = mass_sum * factor + jnp.sum(expo, axis=-1)
        running = running * jnp.transpose(factor, (2, 0, 1))[..., None]
        running = running + jnp.einsum(
            "ngqk,knd->qngd",
            expo.astype(jnp.bfloat16),
            pieces[1],
            preferred_element_type=jnp.float32,
        )
        return ((new_peak, mass_sum, running), None)

    start_peak = jnp.full((key_heads, group_size, tok_rows), MASKED, jnp.float32)
    start = (start_peak, jnp.zeros_like(start_peak), jnp.zeros(query_grouped.shape, jnp.float32))
    (peak_score, mass_sum, running), unused = lax.scan(value_step, start, blocks)
    log_mass = peak_score + jnp.log(mass_sum)
    mixed_full = running / jnp.transpose(mass_sum, (2, 0, 1))[..., None]
    mixed = mixed_full.reshape(tok_rows, key_heads * group_size * head_size).astype(jnp.bfloat16)
    return (mixed, mixed_full, log_mass)


def attend_backward(
    query_grouped, grad_grouped, mixed_full, blocks, log_mass, segment_own, packed_own
):
    score_scale = query_grouped.shape[-1] ** (-0.5)
    row_dot = jnp.transpose(
        jnp.sum(grad_grouped.astype(jnp.float32) * mixed_full, axis=-1), (1, 2, 0)
    )

    def grad_step(carry, pieces):
        scores = block_scores(query_grouped, pieces, segment_own, packed_own)
        probs = jnp.exp(scores - log_mass[..., None])
        grad_probs = jnp.einsum(
            "qngd,knd->ngqk", grad_grouped, pieces[1], preferred_element_type=jnp.float32
        )
        grad_scores = (probs * (grad_probs - row_dot[..., None])).astype(jnp.bfloat16)
        carry = carry + jnp.einsum(
            "ngqk,knd->qngd", grad_scores, pieces[0], preferred_element_type=jnp.float32
        )
        grad_key = (
            jnp.einsum(
                "ngqk,qngd->knd", grad_scores, query_grouped, preferred_element_type=jnp.float32
            )
            * score_scale
        )
        grad_value = jnp.einsum(
            "ngqk,qngd->knd",
            probs.astype(jnp.bfloat16),
            grad_grouped,
            preferred_element_type=jnp.float32,
        )
        return (carry, (grad_key, grad_value))

    grad_query, (grad_keys, grad_values) = lax.scan(
        grad_step, jnp.zeros(query_grouped.shape, jnp.float32), blocks
    )
    total_rows = grad_keys.shape[0] * grad_keys.shape[1]
    return (
        grad_query * score_scale,
        grad_keys.reshape(total_rows, -1),
        grad_values.reshape(total_rows, -1),
    )


def on_device(
    hidden_in,
    seq_lengths,
    token_order,
    attn_gain,
    w_query,
    w_key,
    w_value,
    query_gain,
    key_gain,
    w_out,
    mlp_gain,
    w_gate,
    w_up,
    w_down,
    cotangent,
):
    micro_count = hidden_in.shape[0]
    tok_rows = hidden_in.shape[1]
    width = hidden_in.shape[2]
    head_size = query_gain.shape[0]
    ctx_rank = lax.axis_index("ctx")
    own_start = ctx_rank * tok_rows
    acc_query = jnp.zeros((width, w_query.shape[1]), jnp.float32)
    acc_key = jnp.zeros((width, w_key.shape[1]), jnp.float32)
    acc_value = jnp.zeros((width, w_value.shape[1]), jnp.float32)
    acc_gate = jnp.zeros((width, w_gate.shape[1]), jnp.float32)
    acc_up = jnp.zeros((width, w_up.shape[1]), jnp.float32)
    acc_out = jnp.zeros((w_out.shape[0], width), jnp.float32)
    acc_down = jnp.zeros((w_down.shape[0], width), jnp.float32)
    acc_attn_gain = jnp.zeros((width,), jnp.float32)
    acc_mlp_gain = jnp.zeros((width,), jnp.float32)
    acc_query_gain = jnp.zeros((head_size,), jnp.float32)
    acc_key_gain = jnp.zeros((head_size,), jnp.float32)
    outputs = []
    input_grads = []
    for micro_batch in range(micro_count):
        full_rows = (
            lax.all_gather(w_query, "ctx", axis=0, tiled=True),
            lax.all_gather(w_key, "ctx", axis=0, tiled=True),
            lax.all_gather(w_value, "ctx", axis=0, tiled=True),
            lax.all_gather(w_gate, "ctx", axis=0, tiled=True),
            lax.all_gather(w_up, "ctx", axis=0, tiled=True),
        )
        full_cols = (
            lax.all_gather(w_out, "ctx", axis=1, tiled=True),
            lax.all_gather(w_down, "ctx", axis=1, tiled=True),
        )
        query_w, key_w, value_w, gate_w, up_w = full_rows
        out_w, down_w = full_cols
        packed_all = token_order[micro_batch]
        segment_all, position_all = layout(seq_lengths[micro_batch], packed_all)
        segment_own = lax.dynamic_slice_in_dim(segment_all, own_start, tok_rows)
        packed_own = lax.dynamic_slice_in_dim(packed_all, own_start, tok_rows)
        position_own = lax.dynamic_slice_in_dim(position_all, own_start, tok_rows)
        angles = angles_of(position_own, head_size)
        cosine = jnp.cos(angles)[:, None, :]
        sine_part = jnp.sin(angles)[:, None, :]
        inputs = hidden_in[micro_batch].astype(jnp.float32)
        inv_one = lax.rsqrt(jnp.mean(inputs * inputs, axis=-1, keepdims=True) + EPSILON)
        unit_one = inputs * inv_one
        normed = (unit_one * attn_gain).astype(jnp.bfloat16)
        query_raw = jnp.dot(normed, query_w, preferred_element_type=jnp.float32).reshape(
            tok_rows, -1, head_size
        )
        key_raw = jnp.dot(normed, key_w, preferred_element_type=jnp.float32).reshape(
            tok_rows, -1, head_size
        )
        value_rows = jnp.dot(normed, value_w, preferred_element_type=jnp.float32).astype(
            jnp.bfloat16
        )
        query_inv = lax.rsqrt(jnp.mean(query_raw * query_raw, axis=-1, keepdims=True) + EPSILON)
        query_unit = query_raw * query_inv
        query_rot = rotate(query_unit * query_gain, cosine, sine_part).astype(jnp.bfloat16)
        key_inv = lax.rsqrt(jnp.mean(key_raw * key_raw, axis=-1, keepdims=True) + EPSILON)
        key_unit = key_raw * key_inv
        key_rot = rotate(key_unit * key_gain, cosine, sine_part).astype(jnp.bfloat16)
        key_heads = key_rot.shape[1]
        query_heads = query_rot.shape[1]
        key_all, value_all = (
            lax.all_gather(
                key_rot.reshape(tok_rows, key_heads * head_size), "ctx", axis=0, tiled=True
            ),
            lax.all_gather(value_rows, "ctx", axis=0, tiled=True),
        )
        blocks = split_blocks(key_all, value_all, segment_all, packed_all, head_size)
        query_grouped = query_rot.reshape(tok_rows, key_heads, query_heads // key_heads, head_size)
        mixed, mixed_full, log_mass = attend_forward(query_grouped, blocks, segment_own, packed_own)
        middle = inputs + lax.psum(
            jnp.dot(mixed, out_w, preferred_element_type=jnp.float32).astype(jnp.bfloat16), "tp"
        ).astype(jnp.float32)
        inv_two = lax.rsqrt(jnp.mean(middle * middle, axis=-1, keepdims=True) + EPSILON)
        unit_two = middle * inv_two
        normed_two = (unit_two * mlp_gain).astype(jnp.bfloat16)
        gate_raw = jnp.dot(normed_two, gate_w, preferred_element_type=jnp.float32)
        up_raw = jnp.dot(normed_two, up_w, preferred_element_type=jnp.float32)
        gate_sigmoid = jax.nn.sigmoid(gate_raw)
        hidden = (gate_raw * gate_sigmoid * up_raw).astype(jnp.bfloat16)
        down_term = jnp.dot(hidden, down_w, preferred_element_type=jnp.float32)
        layer_rows = middle + lax.psum(down_term.astype(jnp.bfloat16), "tp").astype(jnp.float32)
        outputs.append(layer_rows.astype(jnp.bfloat16))
        grad_rows = cotangent[micro_batch]
        acc_down = acc_down + contract_rows(hidden, grad_rows)
        grad_hidden = times_transpose(grad_rows, down_w)
        grad_up_raw = (grad_hidden * gate_raw * gate_sigmoid).astype(jnp.bfloat16)
        grad_gate_raw = (
            grad_hidden * up_raw * gate_sigmoid * (1.0 + gate_raw * (1.0 - gate_sigmoid))
        ).astype(jnp.bfloat16)
        acc_gate = acc_gate + contract_rows(normed_two, grad_gate_raw)
        acc_up = acc_up + contract_rows(normed_two, grad_up_raw)
        grad_normed_two = lax.psum(
            (times_transpose(grad_gate_raw, gate_w) + times_transpose(grad_up_raw, up_w)).astype(
                jnp.bfloat16
            ),
            "tp",
        ).astype(jnp.float32)
        acc_mlp_gain = acc_mlp_gain + jnp.sum(grad_normed_two * unit_two, axis=0)
        grad_middle = grad_rows.astype(jnp.float32) + norm_back(
            grad_normed_two, unit_two, inv_two, mlp_gain
        )
        grad_middle_low = grad_middle.astype(jnp.bfloat16)
        acc_out = acc_out + contract_rows(mixed, grad_middle_low)
        grad_mixed = times_transpose(grad_middle_low, out_w).astype(jnp.bfloat16)
        grad_grouped = grad_mixed.reshape(query_grouped.shape)
        grad_query_rot, grad_key_all, grad_value_all = attend_backward(
            query_grouped, grad_grouped, mixed_full, blocks, log_mass, segment_own, packed_own
        )
        grad_key_own, grad_value_own = (
            lax.psum_scatter(
                grad_key_all.astype(jnp.bfloat16), "ctx", scatter_dimension=0, tiled=True
            ).astype(jnp.float32),
            lax.psum_scatter(
                grad_value_all.astype(jnp.bfloat16), "ctx", scatter_dimension=0, tiled=True
            ).astype(jnp.float32),
        )
        grad_value_low = grad_value_own.astype(jnp.bfloat16)
        grad_query_normed = unrotate(
            grad_query_rot.reshape(tok_rows, query_heads, head_size), cosine, sine_part
        )
        acc_query_gain = acc_query_gain + jnp.sum(grad_query_normed * query_unit, axis=(0, 1))
        grad_query_low = (
            norm_back(grad_query_normed, query_unit, query_inv, query_gain)
            .astype(jnp.bfloat16)
            .reshape(tok_rows, -1)
        )
        grad_key_normed = unrotate(
            grad_key_own.reshape(tok_rows, key_heads, head_size), cosine, sine_part
        )
        acc_key_gain = acc_key_gain + jnp.sum(grad_key_normed * key_unit, axis=(0, 1))
        grad_key_low = (
            norm_back(grad_key_normed, key_unit, key_inv, key_gain)
            .astype(jnp.bfloat16)
            .reshape(tok_rows, -1)
        )
        acc_query = acc_query + contract_rows(normed, grad_query_low)
        acc_key = acc_key + contract_rows(normed, grad_key_low)
        acc_value = acc_value + contract_rows(normed, grad_value_low)
        grad_partial = (
            times_transpose(grad_query_low, query_w)
            + times_transpose(grad_key_low, key_w)
            + times_transpose(grad_value_low, value_w)
        )
        grad_normed = lax.psum(grad_partial.astype(jnp.bfloat16), "tp").astype(jnp.float32)
        acc_attn_gain = acc_attn_gain + jnp.sum(grad_normed * unit_one, axis=0)
        input_grads.append(grad_middle + norm_back(grad_normed, unit_one, inv_one, attn_gain))
    sum_query_gain, sum_key_gain = lax.psum((acc_query_gain, acc_key_gain), ("ctx", "tp"))
    rows_out = (
        lax.psum_scatter(
            acc_query.astype(jnp.bfloat16), "ctx", scatter_dimension=0, tiled=True
        ).astype(jnp.float32),
        lax.psum_scatter(
            acc_key.astype(jnp.bfloat16), "ctx", scatter_dimension=0, tiled=True
        ).astype(jnp.float32),
        lax.psum_scatter(
            acc_value.astype(jnp.bfloat16), "ctx", scatter_dimension=0, tiled=True
        ).astype(jnp.float32),
        lax.psum_scatter(
            acc_gate.astype(jnp.bfloat16), "ctx", scatter_dimension=0, tiled=True
        ).astype(jnp.float32),
        lax.psum_scatter(
            acc_up.astype(jnp.bfloat16), "ctx", scatter_dimension=0, tiled=True
        ).astype(jnp.float32),
        lax.psum_scatter(
            acc_attn_gain.astype(jnp.bfloat16), "ctx", scatter_dimension=0, tiled=True
        ).astype(jnp.float32),
        lax.psum_scatter(
            acc_mlp_gain.astype(jnp.bfloat16), "ctx", scatter_dimension=0, tiled=True
        ).astype(jnp.float32),
    )
    cols_out = (
        lax.psum_scatter(
            acc_out.astype(jnp.bfloat16), "ctx", scatter_dimension=1, tiled=True
        ).astype(jnp.float32),
        lax.psum_scatter(
            acc_down.astype(jnp.bfloat16), "ctx", scatter_dimension=1, tiled=True
        ).astype(jnp.float32),
    )
    return (
        jnp.stack(outputs),
        jnp.stack(input_grads),
        rows_out[5],
        rows_out[0],
        rows_out[1],
        rows_out[2],
        sum_query_gain,
        sum_key_gain,
        cols_out[0],
        rows_out[6],
        rows_out[3],
        rows_out[4],
        cols_out[1],
    )


def solution(mesh):
    in_specs = (
        P(None, "ctx", None),
        P(),
        P(),
        P(),
        P("ctx", "tp"),
        P("ctx", "tp"),
        P("ctx", "tp"),
        P(),
        P(),
        P("tp", "ctx"),
        P(),
        P("ctx", "tp"),
        P("ctx", "tp"),
        P("tp", "ctx"),
        P(None, "ctx", None),
    )
    out_specs = (
        P(None, "ctx", None),
        P(None, "ctx", None),
        P("ctx"),
        P("ctx", "tp"),
        P("ctx", "tp"),
        P("ctx", "tp"),
        P(),
        P(),
        P("tp", "ctx"),
        P("ctx"),
        P("ctx", "tp"),
        P("ctx", "tp"),
        P("tp", "ctx"),
    )
    return jax.shard_map(
        on_device, mesh=mesh, in_specs=in_specs, out_specs=out_specs, check_vma=False
    )
```

profile of v0, /device:TPU:0, one launch (start us, length us, event | category | flops | bytes accessed | tf_op | source)
XLA Modules:
  0.0 1873.9 jit_solution(1908469111895912264)
XLA Ops:
  17.0 19.1 %all-gather.12.cloned.1.call-done = bf16[2048,256]{1,0:T(8,128)(2,1)} async-done(((bf16[256,256]{1,0:T(8,128)(2,1)}), bf16[2048,256]{1,0:T(8,128)(2,1)}) %all-gather.12.cloned.1.call-update) | async-done | bytes 1048592 | tf_op jit(solution)/shard_map/all_gather | solution.py:203
  43.5 18.1 all-gather.18.cloned.1.call-done
  70.6 20.8 %all-gather.16.cloned.1.call-done = bf16[2048,512]{1,0:T(8,128)(2,1)} async-done(((bf16[256,512]{1,0:T(8,128)(2,1)}), bf16[2048,512]{1,0:T(8,128)(2,1)}) %all-gather.16.cloned.1.call-update) | async-done | bytes 2097168 | tf_op jit(solution)/shard_map/all_gather | solution.py:202
  104.4 17.3 all-gather.30.cloned.1.call-done
  125.8 26.0 %all-gather.32.cloned.1.call-done = bf16[4096,256]{1,0:T(8,128)(2,1)} async-done(((bf16[512,256]{1,0:T(8,128)(2,1)}), bf16[4096,256]{1,0:T(8,128)(2,1)}) %all-gather.32.cloned.1.call-update) | async-done | bytes 2097168 | tf_op jit(solution)/shard_map/all_gather | solution.py:247
  155.8 80.8 %while.61 = (s32[]{:T(128)}, f32[2,2,512]{2,1,0:T(2,128)S(1)}, f32[2,2,512]{2,1,0:T(2,128)S(1)}, f32[512,2,2,128]{0,3,2,1:T(8,128)}, s32[512]{0:T(512)S(1)}, /*i...) while((s32[]{:T(128)}, f32[2,2,512]{2,1,0:T(2,128)S(1)}, ...), condition=%wide.region_22.23_spmd.clone, body=%wide.region_19.22_spmd.clone.sunk | while | flops 1099182080 | bytes 33190044 | solution.py:114
  156.7 6.0 fusion.350
  169.0 6.8 fusion.354
  176.6 6.0 fusion.350
  188.9 7.2 fusion.354
  197.0 6.0 fusion.350
  209.3 7.1 fusion.354
  217.2 6.0 fusion.350
  229.5 7.1 fusion.354
  245.2 76.9 %while.60 = (s32[]{:T(128)}, f32[2,2,512]{2,1,0:T(2,128)S(1)}, f32[2,2,512]{2,1,0:T(2,128)S(1)}, f32[512,2,2,128]{0,3,2,1:T(8,128)S(1)}, s32[512]{0:T(512)S(1)},...) while((s32[]{:T(128)}, f32[2,2,512]{2,1,0:T(2,128)S(1)}, ...), condition=%wide.region_9.10_spmd.clone, body=%wide.region_6.9_spmd.clone.sunk | while | flops 1099182080 | bytes 33190044 | solution.py:114
  246.6 6.0 fusion.342
  265.7 6.0 fusion.342
  333.3 153.7 %all-reduce.15.cloned.1.call-done = (bf16[512,2048]{1,0:T(8,128)(2,1)}, bf16[512,2048]{1,0:T(8,128)(2,1)}) async-done(((bf16[512,2048]{1,0:T(8,128)(2,1)}, bf16[512,2048]{1,0:T(8,128)(2,1)}), (bf16[512,2048]{1,0:T(8,128)(2,1)}, bf16[512,2048]{1,0:T(8,128)(2,1)})) %all-reduce.15.cloned.1.call-update) | async-done | bytes 4194320 | tf_op jit(solution)/shard_map/psum | solution.py:252
  497.0 36.5 %all-gather.24.cloned.1.call-done = bf16[2048,1536]{1,0:T(8,128)(2,1)} async-done(((bf16[256,1536]{1,0:T(8,128)(2,1)}), bf16[2048,1536]{1,0:T(8,128)(2,1)}) %all-gather.24.cloned.1.call-update) | async-done | bytes 6291472 | tf_op jit(solution)/shard_map/all_gather | solution.py:205
  533.5 8.5 fusion.207
  542.0 39.1 %all-gather.26.cloned.1.call-done = bf16[2048,1536]{1,0:T(8,128)(2,1)} async-done(((bf16[256,1536]{1,0:T(8,128)(2,1)}), bf16[2048,1536]{1,0:T(8,128)(2,1)}) %all-gather.26.cloned.1.call-update) | async-done | bytes 6291472 | tf_op jit(solution)/shard_map/all_gather | solution.py:206
  581.1 8.6 fusion.208
  600.0 29.6 %all-gather.28.cloned.1.call-done = bf16[1536,2048]{1,0:T(8,128)(2,1)} async-done(((bf16[1536,256]{1,0:T(8,128)(2,1)}), bf16[1536,2048]{1,0:T(8,128)(2,1)}) %all-gather.28.cloned.1.call-update) | async-done | bytes 6291472 | tf_op jit(solution)/shard_map/all_gather | solution.py:210
  629.7 11.4 multiply_convert_fusion.2
  642.3 8.3 fusion.212
  650.6 7.7 multiply_convert_fusion.4
  658.4 6.7 fusion.209
  665.1 7.4 add_convert_fusion.6
  677.9 154.8 %all-reduce.13.cloned.1.call-done = (bf16[512,2048]{1,0:T(8,128)(2,1)}, bf16[512,2048]{1,0:T(8,128)(2,1)}) async-done(((bf16[512,2048]{1,0:T(8,128)(2,1)}, bf16[512,2048]{1,0:T(8,128)(2,1)}), (bf16[512,2048]{1,0:T(8,128)(2,1)}, bf16[512,2048]{1,0:T(8,128)(2,1)})) %all-reduce.13.cloned.1.call-update) | async-done | bytes 4194320 | tf_op jit(solution)/shard_map/psum | solution.py:274
  832.8 6.8 fusion.130
  839.9 7.8 fusion.129
  855.3 82.4 %while.63 = (s32[]{:T(128)}, f32[512,2,2,128]{0,3,2,1:T(8,128)S(1)}, bf16[4,1024,2,128]{3,1,2,0:T(8,128)(2,1)}, bf16[4,1024,2,128]{3,1,2,0:T(8,128)(2,1)}, bf16[...) while((s32[]{:T(128)}, ...), condition=%wide.region_41.42_spmd.clone, body=%wide.region_40.41_spmd.clone.sunk | while | flops 2707685376 | bytes 134271296 | solution.py:153
  951.7 82.7 %while.62 = (s32[]{:T(128)}, f32[512,2,2,128]{0,3,2,1:T(8,128)S(1)}, bf16[4,1024,2,128]{3,1,2,0:T(8,128)(2,1)}, bf16[4,1024,2,128]{3,1,2,0:T(8,128)(2,1)}, bf16[...) while((s32[]{:T(128)}, ...), condition=%wide.region_30.31_spmd.clone, body=%wide.region_29.30_spmd.clone.sunk | while | flops 2707685376 | bytes 134271296 | solution.py:153
  1068.6 11.7 reduce-scatter.12.cloned.1.call-done
  1087.9 36.7 %reduce-scatter.14.cloned.1.call-done = bf16[512,256]{1,0:T(8,128)(2,1)} async-done(((bf16[4096,256]{1,0:T(8,128)(2,1)}), bf16[512,256]{1,0:T(8,128)(2,1)}) %reduce-scatter.14.cloned.1.call-update) | async-done | bytes 262160 | tf_op jit(solution)/shard_map/reduce_scatter | solution.py:295
  1127.3 42.7 %reduce-scatter.18.cloned.1.call-done = bf16[512,256]{1,0:T(8,128)(2,1)} async-done(((bf16[4096,256]{1,0:T(8,128)(2,1)}), bf16[512,256]{1,0:T(8,128)(2,1)}) %reduce-scatter.18.cloned.1.call-update) | async-done | bytes 262160 | tf_op jit(solution)/shard_map/reduce_scatter | solution.py:295
  1202.8 7.2 add_convert_fusion
  1210.5 8.1 convolution_convert_fusion
  1218.5 7.5 convolution_convert_fusion.2
  1239.9 19.5 %reduce-scatter.26.cloned.1.call-done = bf16[512,256]{1,0:T(8,128)(2,1)} async-done(((bf16[512,2048]{1,0:T(8,128)(2,1)}), bf16[512,256]{1,0:T(8,128)(2,1)}) %reduce-scatter.26.cloned.1.call-update) | async-done | bytes 262160 | tf_op jit(solution)/shard_map/reduce_scatter | solution.py:354
  1261.1 39.2 %all-reduce.2 = (f32[128]{0:T(128)}, f32[128]{0:T(128)}) all-reduce(f32[128]{0:T(128)S(1)} %add.306, f32[128]{0:T(128)S(1)} %add.307), channel_id=1, replica_groups=mesh['ctx'=8,'tp'=4] {'ctx','tp'}, use_global_device_ids=true, to_apply=%region_56.57 | all-reduce | flops 256 | bytes 2048 | tf_op jit(solution)/shard_map/psum | solution.py:329
  1302.0 35.9 %reduce-scatter.24.cloned.1.call-done = bf16[256,256]{1,0:T(8,128)(2,1)} async-done(((bf16[2048,256]{1,0:T(8,128)(2,1)}), bf16[256,256]{1,0:T(8,128)(2,1)}) %reduce-scatter.24.cloned.1.call-update) | async-done | bytes 131088 | tf_op jit(solution)/shard_map/reduce_scatter | solution.py:337
  1339.5 64.1 %reduce-scatter.28.cloned.1.call-done = bf16[256,1536]{1,0:T(8,128)(2,1)} async-done(((bf16[2048,1536]{1,0:T(8,128)(2,1)}), bf16[256,1536]{1,0:T(8,128)(2,1)}) %reduce-scatter.28.cloned.1.call-update) | async-done | bytes 786448 | tf_op jit(solution)/shard_map/reduce_scatter | solution.py:340
  1406.1 63.1 %reduce-scatter.30.cloned.1.call-done = bf16[256,1536]{1,0:T(8,128)(2,1)} async-done(((bf16[2048,1536]{1,0:T(8,128)(2,1)}), bf16[256,1536]{1,0:T(8,128)(2,1)}) %reduce-scatter.30.cloned.1.call-update) | async-done | bytes 786448 | tf_op jit(solution)/shard_map/reduce_scatter | solution.py:343
  1471.6 62.6 %reduce-scatter.32.cloned.1.call-done = bf16[1536,256]{1,0:T(8,128)(2,1)} async-done(((bf16[1536,2048]{1,0:T(8,128)(2,1)}), bf16[1536,256]{1,0:T(8,128)(2,1)}) %reduce-scatter.32.cloned.1.call-update) | async-done | bytes 786448 | tf_op jit(solution)/shard_map/reduce_scatter | solution.py:357
  1536.6 293.6 %all-reduce.11.cloned.1.call-done = (bf16[512,2048]{1,0:T(8,128)(2,1)}, bf16[512,2048]{1,0:T(8,128)(2,1)}, bf16[512,2048]{1,0:T(8,128)(2,1)}, bf16[512,2048]{1,0:T(8,128)(2,1)}) async-done(((bf16[512,2048]{1,0:T(8,128)(2,1)}, bf16[512,2048]{1,0:T(8,128)(2,1)}, bf16[512,2048]{1,0:T(8,128)(2,1)}, bf16[512,2048]{1,0:T(8,128)(2,1)}), (bf16[512,2048]{1,0:T(8,128)(2,1)}, bf16[512,2048]{1,0:T(8,128)(2,1)}, ...) | async-done | bytes 8388624 | tf_op jit(solution)/shard_map/psum | solution.py:263
  1835.1 14.1 all-reduce.3
  1850.5 10.3 fusion.126
  (620 shorter events, 486.8 us)
Async XLA Ops:
  7.2 30.5 %copy-start.90 = (f32[2048]{0:T(1024)S(1)}, f32[2048]{0:T(1024)}, u32[]{:S(2)}) copy-start(f32[2048]{0:T(1024)} %param.26) | copy-start | bytes 24580
  7.2 29.0 %all-gather.12.cloned.1.call-start = ((), (), s32[]{:S(2)}) async-start(), calls=%async_computation.11 | async-start | bytes 1179648 | tf_op jit(solution)/shard_map/all_gather | solution.py:203
  7.9 53.6 %all-gather.18.cloned.1.call-start = ((), (), s32[]{:S(2)}) async-start(), calls=%async_computation.14 | async-start | bytes 1179648 | tf_op jit(solution)/shard_map/all_gather | solution.py:204
  8.7 82.7 %all-gather.16.cloned.1.call-start = ((), (), s32[]{:S(2)}) async-start(), calls=%async_computation.13 | async-start | bytes 2359296 | tf_op jit(solution)/shard_map/all_gather | solution.py:202
  9.4 112.2 %all-gather.30.cloned.1.call-start = ((), (), s32[]{:S(2)}) async-start(), calls=%async_computation.20 | async-start | bytes 2359296 | tf_op jit(solution)/shard_map/all_gather | solution.py:244
  16.0 79.3 %copy-start.92 = (f32[512]{0:T(512)}, f32[512]{0:T(512)S(1)}, u32[]{:S(2)}) copy-start(f32[512]{0:T(512)S(1)} %add_rsqrt_fusion.7) | copy-start | bytes 6148
  16.0 83.1 %copy-start.94 = (f32[512]{0:T(512)}, f32[512]{0:T(512)S(1)}, u32[]{:S(2)}) copy-start(f32[512]{0:T(512)S(1)} %add_rsqrt_fusion.5) | copy-start | bytes 6148
  17.0 85.2 %copy-start.44 = (f32[512,64]{0,1:T(8,128)}, f32[512,64]{0,1:T(8,128)S(1)}, u32[]{:S(2)}) copy-start(f32[512,64]{0,1:T(8,128)S(1)} %get-tuple-element.851) | copy-start | bytes 393220
  17.0 85.2 %copy-start.46 = (f32[512,64]{0,1:T(8,128)}, f32[512,64]{0,1:T(8,128)S(1)}, u32[]{:S(2)}) copy-start(f32[512,64]{0,1:T(8,128)S(1)} %get-tuple-element.852) | copy-start | bytes 393220
  17.0 86.0 %copy-start.48 = (f32[512,64]{0,1:T(8,128)}, f32[512,64]{0,1:T(8,128)S(1)}, u32[]{:S(2)}) copy-start(f32[512,64]{0,1:T(8,128)S(1)} %get-tuple-element.839) | copy-start | bytes 393220
  17.0 86.0 %copy-start.50 = (f32[512,64]{0,1:T(8,128)}, f32[512,64]{0,1:T(8,128)S(1)}, u32[]{:S(2)}) copy-start(f32[512,64]{0,1:T(8,128)S(1)} %get-tuple-element.840) | copy-start | bytes 393220
  41.5 23.5 %copy-start.84 = (f32[512,2]{0,1:T(2,128)}, f32[512,2]{0,1:T(2,128)S(1)}, u32[]{:S(2)}) copy-start(f32[512,2]{0,1:T(2,128)S(1)} %get-tuple-element.869) | copy-start | bytes 12292
  41.5 23.5 %copy-start.86 = (f32[512,2]{0,1:T(2,128)}, f32[512,2]{0,1:T(2,128)S(1)}, u32[]{:S(2)}) copy-start(f32[512,2]{0,1:T(2,128)S(1)} %get-tuple-element.870) | copy-start | bytes 12292
  43.4 108.4 %all-gather.32.cloned.1.call-start = ((), (), s32[]{:S(2)}) async-start(), calls=%async_computation.21 | async-start | bytes 2359296 | tf_op jit(solution)/shard_map/all_gather | solution.py:247
  65.0 171.7 %all-gather.14.cloned.1.call-start = ((), (), s32[]{:S(2)}) async-start(), calls=%async_computation.12 | async-start | bytes 2359296 | tf_op jit(solution)/shard_map/all_gather | solution.py:244
  66.1 175.0 %all-gather.20.cloned.1.call-start = ((), (), s32[]{:S(2)}) async-start(), calls=%async_computation.15 | async-start | bytes 2359296 | tf_op jit(solution)/shard_map/all_gather | solution.py:247
  69.2 255.1 %all-gather.22.cloned.1.call-start = ((), (), s32[]{:S(2)}) async-start(), calls=%async_computation.16 | async-start | bytes 2359296 | tf_op jit(solution)/shard_map/all_gather | solution.py:209
  70.0 417.1 %all-reduce.15.cloned.1.call-start = ((), (), s32[]{:S(2)}) async-start(), calls=%async_computation.35 | async-start | bytes 8388608 | tf_op jit(solution)/shard_map/psum | solution.py:252
  331.4 202.1 %all-gather.24.cloned.1.call-start = ((), (), s32[]{:S(2)}) async-start(), calls=%async_computation.17 | async-start | bytes 7077888 | tf_op jit(solution)/shard_map/all_gather | solution.py:205
  332.0 249.1 %all-gather.26.cloned.1.call-start = ((), (), s32[]{:S(2)}) async-start(), calls=%async_computation.18 | async-start | bytes 7077888 | tf_op jit(solution)/shard_map/all_gather | solution.py:206
  332.7 297.0 %all-gather.28.cloned.1.call-start = ((), (), s32[]{:S(2)}) async-start(), calls=%async_computation.19 | async-start | bytes 7077888 | tf_op jit(solution)/shard_map/all_gather | solution.py:210
  333.3 499.5 %all-reduce.13.cloned.1.call-start = ((), (), s32[]{:S(2)}) async-start(), calls=%async_computation.34 | async-start | bytes 8388608 | tf_op jit(solution)/shard_map/psum | solution.py:274
  581.1 8.6 copy-start.55
  581.1 8.6 copy-start.101
  581.1 13.7 slice-start
  650.6 21.9 %slice-start.2 = ((s8[6291456]{0:T(1024)(128)(4,1)}), s8[2097152]{0:T(1024)(128)(4,1)S(1)}, s32[]{:S(2)}) async-start(s8[6291456]{0:T(1024)(128)(4,1)} %bitcast.671), calls=%async_computation.38 | async-start | bytes 4194304
  658.3 14.2 copy-start.103
  658.3 14.2 slice-start.3
  677.2 390.2 %reduce-scatter.16.cloned.1.call-start = ((), (), s32[]{:S(2)}) async-start(), calls=%async_computation.24 | async-start | bytes 2359296 | tf_op jit(solution)/shard_map/reduce_scatter | solution.py:292
  839.9 9.9 copy-start.30
  839.9 9.9 copy-start.39
  943.1 137.2 %reduce-scatter.12.cloned.1.call-start = ((), (), s32[]{:S(2)}) async-start(), calls=%async_computation.22 | async-start | bytes 2359296 | tf_op jit(solution)/shard_map/reduce_scatter | solution.py:292
  1039.8 84.9 %reduce-scatter.14.cloned.1.call-start = ((), (), s32[]{:S(2)}) async-start(), calls=%async_computation.23 | async-start | bytes 2359296 | tf_op jit(solution)/shard_map/reduce_scatter | solution.py:295
  1045.7 124.3 %reduce-scatter.18.cloned.1.call-start = ((), (), s32[]{:S(2)}) async-start(), calls=%async_computation.25 | async-start | bytes 2359296 | tf_op jit(solution)/shard_map/reduce_scatter | solution.py:295
  1051.2 186.8 %reduce-scatter.20.cloned.1.call-start = ((), (), s32[]{:S(2)}) async-start(), calls=%async_computation.26 | async-start | bytes 2359296 | tf_op jit(solution)/shard_map/reduce_scatter | solution.py:331
  1060.9 198.5 %reduce-scatter.26.cloned.1.call-start = ((), (), s32[]{:S(2)}) async-start(), calls=%async_computation.29 | async-start | bytes 2359296 | tf_op jit(solution)/shard_map/reduce_scatter | solution.py:354
  1067.3 16.2 copy-start.36
  1067.3 16.2 copy-start.87
  1067.3 16.2 copy-start.97
  1067.3 16.4 copy-start.34
  1067.3 16.4 copy-start.85
  1067.4 233.0 %reduce-scatter.22.cloned.1.call-start = ((), (), s32[]{:S(2)}) async-start(), calls=%async_computation.27 | async-start | bytes 1179648 | tf_op jit(solution)/shard_map/reduce_scatter | solution.py:334
  1087.9 250.0 %reduce-scatter.24.cloned.1.call-start = ((), (), s32[]{:S(2)}) async-start(), calls=%async_computation.28 | async-start | bytes 1179648 | tf_op jit(solution)/shard_map/reduce_scatter | solution.py:337
  1173.7 229.9 %reduce-scatter.28.cloned.1.call-start = ((), (), s32[]{:S(2)}) async-start(), calls=%async_computation.30 | async-start | bytes 7077888 | tf_op jit(solution)/shard_map/reduce_scatter | solution.py:340
  1185.4 283.8 %reduce-scatter.30.cloned.1.call-start = ((), (), s32[]{:S(2)}) async-start(), calls=%async_computation.31 | async-start | bytes 7077888 | tf_op jit(solution)/shard_map/reduce_scatter | solution.py:343
  1197.0 337.2 %reduce-scatter.32.cloned.1.call-start = ((), (), s32[]{:S(2)}) async-start(), calls=%async_computation.32 | async-start | bytes 7077888 | tf_op jit(solution)/shard_map/reduce_scatter | solution.py:357
  1210.0 620.2 %all-reduce.11.cloned.1.call-start = ((), (), s32[]{:S(2)}) async-start(), calls=%async_computation.33 | async-start | bytes 16777216 | tf_op jit(solution)/shard_map/psum | solution.py:263
  1830.2 20.3 %copy-start.19 = (bf16[512,2048]{1,0:T(8,128)(2,1)S(1)}, bf16[512,2048]{1,0:T(8,128)(2,1)}, u32[]{:S(2)}) copy-start(bf16[512,2048]{1,0:T(8,128)(2,1)} %get-tuple-element.789) | copy-start | bytes 6291460
  (116 other events, 533.2 us)
Sparse Core Ops, SparseCore 0:
  9.9 26.1 all-gather.11
  38.0 23.4 all-gather.17
  63.4 27.8 all-gather.15
  93.7 27.8 all-gather.29
  123.9 27.8 all-gather.31
  154.2 27.8 all-gather.13
  184.6 27.8 all-gather.19
  214.4 28.1 all-gather.21
  331.5 155.4 all-reduce.14
  488.9 44.5 all-gather.23
  535.5 45.5 all-gather.25
  583.0 46.6 all-gather.27
  677.4 155.3 all-reduce.12
  943.2 40.2 reduce-scatter.15
  1039.9 40.3 reduce-scatter.11
  1083.4 41.1 reduce-scatter.13
  1128.7 41.2 reduce-scatter.17
  1173.1 41.2 reduce-scatter.19
  1218.0 41.2 reduce-scatter.25
  1262.3 36.0 reduce-scatter.21
  1301.7 36.1 reduce-scatter.23
  1341.9 61.7 reduce-scatter.27
  1407.4 61.7 reduce-scatter.29
  1472.4 61.7 reduce-scatter.31
  1537.3 292.8 all-reduce.10
where the time goes:
time: 1880 us; the launch traced here: 1870 us
  waiting for transfers between devices  1150 us (61%)
  matrix products  412 us (22%)
  other arithmetic  124 us (7%)
  local copies, waits for them, and re-layouts  114 us (6%)
  blocking collectives  53.3 us (3%)
    psum x1, waiting for transfers between devices, on_device(): lax.psum(down_term.astype(jnp.bfloat16), 'tp').astype(jnp.float32)  294 us
    psum x1, waiting for transfers between devices, on_device(): lax.psum((times_transpose(grad_gate_raw, gate_w) + times_transpose(grad_u...  155 us
    psum x1, waiting for transfers between devices, on_device(): lax.psum(jnp.dot(mixed, out_w, preferred_element_type=jnp.float32).astype...  154 us
    reduce_scatter x2, waiting for transfers between devices, on_device(): lax.psum_scatter(grad_value_all.astype(jnp.bfloat16), 'ctx', scatter_dime...  79.5 us
    dot_general x16, matrix products, block_scores(): jnp.einsum('qngd,knd->ngqk', query_grouped, pieces[0], preferred_element_...  66.8 us
    reduce_scatter x1, waiting for transfers between devices, on_device(): lax.psum_scatter(acc_gate.astype(jnp.bfloat16), 'ctx', scatter_dimension=...  64.1 us
    reduce_scatter x1, waiting for transfers between devices, on_device(): lax.psum_scatter(acc_up.astype(jnp.bfloat16), 'ctx', scatter_dimension=0,...  63.1 us
    reduce_scatter x1, waiting for transfers between devices, on_device(): lax.psum_scatter(acc_down.astype(jnp.bfloat16), 'ctx', scatter_dimension=...  62.6 us
  transfers between devices with their start and end apart: 25, of which 19 were waited for; matrix products, arithmetic and copies ran while one was open for 24% of the time, Pallas kernels for 0%

commit v1 on v0

v1 whole, which is shorter than its diff:
```python
import functools
import math

import jax
import jax.numpy as jnp
from jax import lax
from jax.experimental import pallas as pl
from jax.experimental.pallas import tpu as pltpu
from jax.sharding import PartitionSpec as P

EPSILON = 1e-06
THETA = 1000000.0
F32 = jnp.float32
BF16 = jnp.bfloat16
MESH = pl.DeviceIdType.MESH
VMEM = pltpu.VMEM
ANY = pl.ANY
LOG2E = math.log2(math.e)
SUB = 64
QROWS = 128
CHUNKS = 16
LAG = 2


def params(megabytes, collective=None):
    if collective is None:
        return pltpu.CompilerParams(vmem_limit_bytes=megabytes << 20)
    return pltpu.CompilerParams(
        vmem_limit_bytes=megabytes << 20, collective_id=collective, has_side_effects=True
    )


def nt(left_side, right_side):
    return lax.dot_general(
        left_side, right_side, (((1,), (1,)), ((), ())), preferred_element_type=F32
    )


def tn(left_side, right_side):
    return lax.dot_general(
        left_side, right_side, (((0,), (0,)), ((), ())), preferred_element_type=F32
    )


def nn(left_side, right_side):
    return jnp.dot(left_side, right_side, preferred_element_type=F32)


def whole(shape):
    return pl.BlockSpec(shape, lambda *ids: (0,) * len(shape))


def gather_kernel(count, n_ctx, *refs):
    sources, results, sems = refs[:count], refs[count : 2 * count], refs[2 * count :]
    own_sem, send_sem, recv_sem, pass_sem, take_sem = sems
    me = lax.axis_index("ctx")
    column = lax.axis_index("tp")
    chip, core = me // 2, lax.rem(me, 2)
    chips = n_ctx // 2
    partner = chip * 2 + 1 - core

    def peer(d):
        return jnp.bitwise_xor(chip, d) * 2 + core

    barrier = pltpu.get_barrier_semaphore()
    pl.semaphore_signal(barrier, inc=1, device_id=(partner, column), device_id_type=MESH)
    for d in range(1, chips):
        pl.semaphore_signal(barrier, inc=1, device_id=(peer(d), column), device_id_type=MESH)
    pl.semaphore_wait(barrier, chips)

    def rows_of(array, owner):
        rows = sources[array].shape[0]
        return results[array].at[pl.ds(pl.multiple_of(owner * rows, rows), rows)]

    def across(array, d):
        return pltpu.make_async_remote_copy(
            src_ref=sources[array],
            dst_ref=rows_of(array, me),
            send_sem=send_sem.at[array, d],
            recv_sem=recv_sem.at[array, d],
            device_id=(peer(d), column),
            device_id_type=MESH,
        )

    def passed(array, d):
        owner = peer(d)
        return pltpu.make_async_remote_copy(
            src_ref=sources[array] if d == 0 else rows_of(array, owner),
            dst_ref=rows_of(array, owner),
            send_sem=pass_sem.at[array, d],
            recv_sem=take_sem.at[array, d],
            device_id=(partner, column),
            device_id_type=MESH,
        )

    def local(array):
        return pltpu.make_async_copy(sources[array], rows_of(array, me), own_sem.at[array])

    for array in range(count):
        for d in range(1, chips):
            across(array, d).start()
        passed(array, 0).start()
        local(array).start()
    for array in range(count):
        for d in range(1, chips):
            across(array, d).wait_recv()
            passed(array, d).start()
    for array in range(count):
        local(array).wait()
        for d in range(chips):
            if d > 0:
                across(array, d).wait_send()
            passed(array, d).wait_send()
            passed(array, d).wait_recv()


def gather_ctx(arrays, n_ctx, collective):
    count = len(arrays)
    chips = n_ctx // 2
    dma = pltpu.SemaphoreType.DMA
    return pl.pallas_call(
        functools.partial(gather_kernel, count, n_ctx),
        out_shape=[
            jax.ShapeDtypeStruct((n_ctx * a.shape[0], a.shape[1]), a.dtype) for a in arrays
        ],
        in_specs=[pl.BlockSpec(memory_space=ANY)] * count,
        out_specs=[pl.BlockSpec(memory_space=ANY)] * count,
        scratch_shapes=[dma((count,))] + [dma((count, chips))] * 4,
        compiler_params=params(16, collective),
        name="gather_ctx",
    )(*arrays)


def qkv_kernel(heads, kv_heads, x_ref, w_ref, cos_ref, sin_ref, qg_ref, kg_ref, q_ref, kv_ref, raw_ref):
    head = qg_ref.shape[1]
    rows = nn(x_ref[...], w_ref[...])
    cosine, sine = cos_ref[...], sin_ref[...]

    def turn(part, gain):
        unit = part * lax.rsqrt(jnp.mean(part * part, axis=-1, keepdims=True) + EPSILON)
        scaled = unit * gain
        return (scaled * cosine + pltpu.roll(scaled, head // 2, 1) * sine).astype(BF16)

    for h in range(heads):
        part = rows[:, h * head : (h + 1) * head]
        raw_ref[:, h * head : (h + 1) * head] = part
        q_ref[:, h * head : (h + 1) * head] = turn(part, qg_ref[...])
    for n in range(kv_heads):
        at = (heads + 2 * n) * head
        part = rows[:, at : at + head]
        raw_ref[:, (heads + n) * head : (heads + n + 1) * head] = part
        kv_ref[:, 2 * n * head : (2 * n + 1) * head] = turn(part, kg_ref[...])
        kv_ref[:, (2 * n + 1) * head : (2 * n + 2) * head] = rows[:, at + head : at + 2 * head].astype(BF16)


def project_qkv(normed, weight, cosine, sine, query_gain, key_gain, heads, kv_heads):
    total, width = normed.shape
    head = query_gain.shape[1]
    block = 256
    row = lambda cols: pl.BlockSpec((block, cols), lambda i: (i, 0))
    return pl.pallas_call(
        functools.partial(qkv_kernel, heads, kv_heads),
        grid=(total // block,),
        out_shape=[
            jax.ShapeDtypeStruct((total, heads * head), BF16),
            jax.ShapeDtypeStruct((total, 2 * kv_heads * head), BF16),
            jax.ShapeDtypeStruct((total, (heads + kv_heads) * head), F32),
        ],
        in_specs=[
            row(width),
            whole(weight.shape),
            row(head),
            row(head),
            whole((1, head)),
            whole((1, head)),
        ],
        out_specs=[row(heads * head), row(2 * kv_heads * head), row((heads + kv_heads) * head)],
        compiler_params=params(40),
        name="project_qkv",
    )(normed, weight, cosine, sine, query_gain, key_gain)


def heads_to_rows(block, head):
    return jnp.concatenate(
        [block[:, g * head : (g + 1) * head] for g in range(block.shape[1] // head)], axis=0
    )


def rows_to_heads(block, rows):
    return jnp.concatenate(
        [block[g * rows : (g + 1) * rows] for g in range(block.shape[0] // rows)], axis=1
    )


def forward_kernel(head, lo_ref, hi_ref, q_ref, kv_ref, pk_ref, pq_ref, sq_ref, out_ref, mass_ref):
    block = pl.program_id(1)
    runs = kv_ref.shape[0]
    rows = q_ref.shape[0]
    group = q_ref.shape[1] // head
    scale = head ** (-0.5) * LOG2E
    query = heads_to_rows(q_ref[...], head)
    newest = jnp.concatenate([pq_ref[...]] * group, axis=0)
    oldest = jnp.concatenate([sq_ref[...]] * group, axis=0)

    def step(j, carry):
        total, mass = carry
        at = pl.ds(pl.multiple_of(j * SUB, SUB), SUB)
        keys = kv_ref[:, at, :head].reshape(runs * SUB, head)
        values = kv_ref[:, at, head:].reshape(runs * SUB, head)
        packed = pk_ref[j]
        allowed = (packed <= newest) & (packed >= oldest)
        probs = jnp.where(allowed, jnp.exp2(nt(query, keys) * scale), 0.0)
        mass = mass + jnp.sum(probs, axis=1, keepdims=True)
        return total + nn(probs.astype(BF16), values), mass

    start = (jnp.zeros((group * rows, head), F32), jnp.zeros((group * rows, 1), F32))
    total, mass = lax.fori_loop(lo_ref[block], hi_ref[block], step, start)
    out_ref[...] = rows_to_heads(total / mass, rows)
    mass_ref[0] = jnp.broadcast_to(jnp.log2(mass), (group * rows, 128)).T[0:1]


def attend_forward(query, kv, marks, head, kv_heads):
    lo, hi, pk_row, pq_col, sq_col = marks[:5]
    rows, width = query.shape
    runs = kv.shape[0]
    group = width // (kv_heads * head)
    blocks = rows // QROWS
    return pl.pallas_call(
        functools.partial(forward_kernel, head),
        grid_spec=pltpu.PrefetchScalarGridSpec(
            num_scalar_prefetch=2,
            grid=(kv_heads, blocks),
            in_specs=[
                pl.BlockSpec((QROWS, group * head), lambda n, i, *s: (i, n)),
                pl.BlockSpec((runs, rows, 2 * head), lambda n, i, *s: (0, 0, n)),
                whole(pk_row.shape),
                pl.BlockSpec((QROWS, 1), lambda n, i, *s: (i, 0)),
                pl.BlockSpec((QROWS, 1), lambda n, i, *s: (i, 0)),
            ],
            out_specs=[
                pl.BlockSpec((QROWS, group * head), lambda n, i, *s: (i, n)),
                pl.BlockSpec((1, 1, group * QROWS), lambda n, i, *s: (n * blocks + i, 0, 0)),
            ],
        ),
        out_shape=[
            jax.ShapeDtypeStruct((rows, width), F32),
            jax.ShapeDtypeStruct((kv_heads * blocks, 1, group * QROWS), F32),
        ],
        compiler_params=params(40),
        name="attend_forward",
    )(lo, hi, query, kv, pk_row, pq_col, sq_col)


def back(grad, unit, inverse, gain):
    scaled = grad * gain
    return inverse * (scaled - unit * jnp.mean(scaled * unit, axis=-1, keepdims=True))


def unturn(grad, cosine, sine):
    return grad * cosine - pltpu.roll(grad, grad.shape[1] // 2, 1) * sine


def backward_kernel(
    head,
    lo_ref,
    hi_ref,
    q_ref,
    kv_ref,
    pk_ref,
    pq_ref,
    sq_ref,
    g_ref,
    out_ref,
    mass_ref,
    raw_ref,
    cos_ref,
    sin_ref,
    gain_ref,
    dq_ref,
    dkv_ref,
    dgain_ref,
    dk_acc,
    dv_acc,
):
    n, block = pl.program_id(0), pl.program_id(1)
    runs = kv_ref.shape[0]
    rows = q_ref.shape[0]
    group = q_ref.shape[1] // head
    scale = head ** (-0.5)
    query = heads_to_rows(q_ref[...], head)
    grad = heads_to_rows(g_ref[...], head)
    mixed = heads_to_rows(out_ref[...], head)
    row_dot = jnp.sum(grad.astype(F32) * mixed, axis=1, keepdims=True)
    row_dot = jnp.broadcast_to(row_dot, (group * rows, 128)).T[0:1]
    mass = mass_ref[0]
    newest = jnp.concatenate([pq_ref[...]] * group, axis=1)
    oldest = jnp.concatenate([sq_ref[...]] * group, axis=1)

    @pl.when(block == 0)
    def _():
        dk_acc[...] = jnp.zeros_like(dk_acc)
        dv_acc[...] = jnp.zeros_like(dv_acc)

    @pl.when((block == 0) & (n == 0))
    def _():
        dgain_ref[...] = jnp.zeros_like(dgain_ref)

    def step(j, dq):
        at = pl.ds(pl.multiple_of(j * SUB, SUB), SUB)
        keys = kv_ref[:, at, :head].reshape(runs * SUB, head)
        values = kv_ref[:, at, head:].reshape(runs * SUB, head)
        packed = pk_ref[j][:, :1]
        allowed = (packed <= newest) & (packed >= oldest)
        probs = jnp.where(allowed, jnp.exp2(nt(keys, query) * (scale * LOG2E) - mass), 0.0)
        dscores = (probs * (nt(values, grad) - row_dot)).astype(BF16)
        dk_acc[:, at, :] += nn(dscores, query).reshape(runs, SUB, head)
        dv_acc[:, at, :] += nn(probs.astype(BF16), grad).reshape(runs, SUB, head)
        return dq + tn(dscores, keys)

    dq = lax.fori_loop(
        lo_ref[block], hi_ref[block], step, jnp.zeros((group * rows, head), F32)
    )
    dq = dq * scale
    cosine, sine = cos_ref[...], sin_ref[...]
    for g in range(group):
        own = unturn(dq[g * rows : (g + 1) * rows], cosine, sine)
        raw = raw_ref[:, g * head : (g + 1) * head]
        inverse = lax.rsqrt(jnp.mean(raw * raw, axis=-1, keepdims=True) + EPSILON)
        unit = raw * inverse
        dgain_ref[...] += jnp.sum(own * unit, axis=0, keepdims=True)
        dq_ref[:, g * head : (g + 1) * head] = back(own, unit, inverse, gain_ref[...]).astype(BF16)

    @pl.when(block == pl.num_programs(1) - 1)
    def _():
        dkv_ref[:, :, :head] = (dk_acc[...] * scale).astype(BF16)
        dkv_ref[:, :, head:] = dv_acc[...].astype(BF16)


def attend_backward(query, kv, marks, grad, out, mass, raw, cosine, sine, gain, head, kv_heads):
    lo, hi, unused, unused_too, unused_three, pk_col, pq_row, sq_row = marks
    rows, width = query.shape
    runs = kv.shape[0]
    group = width // (kv_heads * head)
    blocks = rows // QROWS
    own = lambda n, i, *s: (i, n)
    return pl.pallas_call(
        functools.partial(backward_kernel, head),
        grid_spec=pltpu.PrefetchScalarGridSpec(
            num_scalar_prefetch=2,
            grid=(kv_heads, blocks),
            in_specs=[
                pl.BlockSpec((QROWS, group * head), own),
                pl.BlockSpec((runs, rows, 2 * head), lambda n, i, *s: (0, 0, n)),
                whole(pk_col.shape),
                pl.BlockSpec((1, QROWS), lambda n, i, *s: (0, i)),
                pl.BlockSpec((1, QROWS), lambda n, i, *s: (0, i)),
                pl.BlockSpec((QROWS, group * head), own),
                pl.BlockSpec((QROWS, group * head), own),
                pl.BlockSpec((1, 1, group * QROWS), lambda n, i, *s: (n * blocks + i, 0, 0)),
                pl.BlockSpec((QROWS, group * head), own),
                pl.BlockSpec((QROWS, head), lambda n, i, *s: (i, 0)),
                pl.BlockSpec((QROWS, head), lambda n, i, *s: (i, 0)),
                whole((1, head)),
            ],
            out_specs=[
                pl.BlockSpec((QROWS, group * head), own),
                pl.BlockSpec((runs, rows, 2 * head), lambda n, i, *s: (0, 0, n)),
                whole((1, head)),
            ],
            scratch_shapes=[VMEM((runs, rows, head), F32)] * 2,
        ),
        out_shape=[
            jax.ShapeDtypeStruct((rows, width), BF16),
            jax.ShapeDtypeStruct(kv.shape, BF16),
            jax.ShapeDtypeStruct((1, head), F32),
        ],
        compiler_params=params(56),
        name="attend_backward",
    )(lo, hi, query, kv, pk_col, pq_row, sq_row, grad, out, mass, raw, cosine, sine, gain)


def key_back_kernel(head, kv_heads, grad_ref, raw_ref, cos_ref, sin_ref, gain_ref, out_ref, dgain_ref):
    cosine, sine = cos_ref[...], sin_ref[...]
    total = jnp.zeros((1, head), F32)
    for n in range(kv_heads):
        at = 2 * n * head
        own = unturn(grad_ref[:, at : at + head].astype(F32), cosine, sine)
        raw = raw_ref[:, n * head : (n + 1) * head]
        inverse = lax.rsqrt(jnp.mean(raw * raw, axis=-1, keepdims=True) + EPSILON)
        unit = raw * inverse
        total = total + jnp.sum(own * unit, axis=0, keepdims=True)
        out_ref[:, at : at + head] = back(own, unit, inverse, gain_ref[...]).astype(BF16)
        out_ref[:, at + head : at + 2 * head] = grad_ref[:, at + head : at + 2 * head]
    dgain_ref[...] = total


def key_back(grad, raw, cosine, sine, gain, kv_heads):
    rows = grad.shape[0]
    head = gain.shape[1]
    keys = pl.BlockSpec((rows, kv_heads * head), lambda i: (0, raw.shape[1] // (kv_heads * head) - 1))
    return pl.pallas_call(
        functools.partial(key_back_kernel, head, kv_heads),
        grid=(1,),
        out_shape=[jax.ShapeDtypeStruct(grad.shape, BF16), jax.ShapeDtypeStruct((1, head), F32)],
        in_specs=[whole(grad.shape), keys, whole((rows, head)), whole((rows, head)), whole((1, head))],
        out_specs=[whole(grad.shape), whole((1, head))],
        compiler_params=params(32),
        name="key_back",
    )(grad, raw, cosine, sine, gain)


def line_scratch(chunks, rows, width):
    dma = pltpu.SemaphoreType.DMA
    buffer = VMEM((chunks, rows, width), BF16)
    return [buffer] * 5 + [dma((2, chunks)), dma((2, chunks))]


def line_sum(n_tp, scratch, produce, consume):
    part, from_left, from_right, to_right, to_left, send_sem, recv_sem = scratch
    chunks = part.shape[0]
    place = lax.axis_index("tp")
    line = lax.axis_index("ctx")
    has_left, has_right = place > 0, place < n_tp - 1
    barrier = pltpu.get_barrier_semaphore()

    @pl.when(has_left)
    def _():
        pl.semaphore_signal(barrier, inc=1, device_id=(line, place - 1), device_id_type=MESH)

    @pl.when(has_right)
    def _():
        pl.semaphore_signal(barrier, inc=1, device_id=(line, place + 1), device_id_type=MESH)

    pl.semaphore_wait(barrier, has_left.astype(jnp.int32) + has_right.astype(jnp.int32))

    def right(c):
        return pltpu.make_async_remote_copy(
            src_ref=to_right.at[c],
            dst_ref=from_left.at[c],
            send_sem=send_sem.at[0, c],
            recv_sem=recv_sem.at[0, c],
            device_id=(line, place + 1),
            device_id_type=MESH,
        )

    def left(c):
        return pltpu.make_async_remote_copy(
            src_ref=to_left.at[c],
            dst_ref=from_right.at[c],
            send_sem=send_sem.at[1, c],
            recv_sem=recv_sem.at[1, c],
            device_id=(line, place - 1),
            device_id_type=MESH,
        )

    def plus(a, b):
        return (a.astype(F32) + b.astype(F32)).astype(BF16)

    late = LAG * jnp.maximum(place, n_tp - 1 - place)

    def step(s, carry):
        c_right = s - LAG * place
        c_left = s - LAG * (n_tp - 1 - place)
        c_out = s - late

        @pl.when(s < chunks)
        def _():
            part[s] = produce(s).astype(BF16)

        @pl.when((c_right >= 0) & (c_right < chunks))
        def _():
            @pl.when(jnp.logical_not(has_left))
            def _():
                to_right[c_right] = part[c_right]

            @pl.when(has_left)
            def _():
                right(c_right).wait_recv()
                to_right[c_right] = plus(part[c_right], from_left[c_right])

            @pl.when(has_right)
            def _():
                right(c_right).start()

        @pl.when((c_left >= 0) & (c_left < chunks))
        def _():
            @pl.when(jnp.logical_not(has_right))
            def _():
                to_left[c_left] = part[c_left]

            @pl.when(has_right)
            def _():
                left(c_left).wait_recv()
                to_left[c_left] = plus(part[c_left], from_right[c_left])

            @pl.when(has_left)
            def _():
                left(c_left).start()

        @pl.when((c_out >= 0) & (c_out < chunks))
        def _():
            @pl.when(has_right)
            def _():
                consume(c_out, to_right[c_out].astype(F32) + from_right[c_out].astype(F32))

            @pl.when(jnp.logical_not(has_right))
            def _():
                consume(c_out, to_right[c_out].astype(F32))

        return carry

    lax.fori_loop(0, chunks + LAG * (n_tp - 1), step, 0)

    def finish(c, carry):
        @pl.when(has_right)
        def _():
            right(c).wait_send()

        @pl.when(has_left)
        def _():
            left(c).wait_send()

        return carry

    lax.fori_loop(0, chunks, finish, 0)


def piece(c, rows):
    return pl.ds(pl.multiple_of(c * rows, rows), rows)


def mean_square(values):
    return jnp.mean(values * values, axis=-1, keepdims=True)


def attn_out_kernel(n_tp, mixed_ref, place_ref, w_ref, x_ref, gain_ref, own_ref, middle_ref, normed_ref, *scratch):
    rows = scratch[0].shape[1]

    def produce(c):
        own = nn(place_ref[piece(c, rows), :], mixed_ref[...].astype(BF16)).astype(BF16)
        own_ref[piece(c, rows), :] = own
        return nt(own, w_ref[...])

    def consume(c, total):
        middle = x_ref[piece(c, rows), :].astype(F32) + total
        middle_ref[piece(c, rows), :] = middle.astype(BF16)
        unit = middle * lax.rsqrt(mean_square(middle) + EPSILON)
        normed_ref[piece(c, rows), :] = (unit * gain_ref[...]).astype(BF16)

    line_sum(n_tp, scratch, produce, consume)


def attn_out(mixed, place, weight, inputs, gain, n_tp, collective):
    rows, width = inputs.shape
    return pl.pallas_call(
        functools.partial(attn_out_kernel, n_tp),
        out_shape=[
            jax.ShapeDtypeStruct(mixed.shape, BF16),
            jax.ShapeDtypeStruct((rows, width), BF16),
            jax.ShapeDtypeStruct((rows, width), BF16),
        ],
        in_specs=[pl.BlockSpec(memory_space=VMEM)] * 5,
        out_specs=[pl.BlockSpec(memory_space=VMEM)] * 3,
        scratch_shapes=line_scratch(CHUNKS, rows // CHUNKS, width),
        compiler_params=params(56, collective),
        name="attn_out",
    )(mixed, place, weight, inputs, gain)


def middle_back_kernel(n_tp, part_ref, g_ref, middle_ref, gain_ref, w_ref, low_ref, mixed_ref, dgain_ref, *scratch):
    rows = scratch[0].shape[1]
    dgain_ref[...] = jnp.zeros_like(dgain_ref)

    def produce(c):
        return part_ref[piece(c, rows), :]

    def consume(c, total):
        middle = middle_ref[piece(c, rows), :].astype(F32)
        inverse = lax.rsqrt(mean_square(middle) + EPSILON)
        unit = middle * inverse
        dgain_ref[...] += jnp.sum(total * unit, axis=0, keepdims=True)
        grad = g_ref[piece(c, rows), :].astype(F32) + back(total, unit, inverse, gain_ref[...])
        low = grad.astype(BF16)
        low_ref[piece(c, rows), :] = low
        mixed_ref[piece(c, rows), :] = nn(low, w_ref[...]).astype(BF16)

    line_sum(n_tp, scratch, produce, consume)


def middle_back(part, grad, middle, gain, weight, n_tp, collective):
    rows, width = grad.shape
    return pl.pallas_call(
        functools.partial(middle_back_kernel, n_tp),
        out_shape=[
            jax.ShapeDtypeStruct((rows, width), BF16),
            jax.ShapeDtypeStruct((rows, weight.shape[1]), BF16),
            jax.ShapeDtypeStruct((1, width), F32),
        ],
        in_specs=[pl.BlockSpec(memory_space=VMEM)] * 5,
        out_specs=[pl.BlockSpec(memory_space=VMEM)] * 3,
        scratch_shapes=line_scratch(CHUNKS, rows // CHUNKS, width),
        compiler_params=params(56, collective),
        name="middle_back",
    )(part, grad, middle, gain, weight)


def input_back_kernel(n_tp, gq_ref, gkv_ref, place_ref, w_ref, x_ref, mid_ref, gain_ref, out_ref, dgain_ref, *scratch):
    rows = scratch[0].shape[1]
    queries = gq_ref.shape[1]
    dgain_ref[...] = jnp.zeros_like(dgain_ref)

    def produce(c):
        place = place_ref[piece(c, rows), :]
        own_q = nn(place, gq_ref[...]).astype(BF16)
        own_kv = nn(place, gkv_ref[...]).astype(BF16)
        return nt(own_q, w_ref[:, :queries]) + nt(own_kv, w_ref[:, queries:])

    def consume(c, total):
        x = x_ref[piece(c, rows), :].astype(F32)
        inverse = lax.rsqrt(mean_square(x) + EPSILON)
        unit = x * inverse
        dgain_ref[...] += jnp.sum(total * unit, axis=0, keepdims=True)
        grad = mid_ref[piece(c, rows), :].astype(F32) + back(total, unit, inverse, gain_ref[...])
        out_ref[piece(c, rows), :] = grad.astype(BF16)

    line_sum(n_tp, scratch, produce, consume)


def input_back(gq, gkv, place, weight, inputs, mid, gain, n_tp, collective):
    rows, width = inputs.shape
    return pl.pallas_call(
        functools.partial(input_back_kernel, n_tp),
        out_shape=[
            jax.ShapeDtypeStruct((rows, width), BF16),
            jax.ShapeDtypeStruct((1, width), F32),
        ],
        in_specs=[pl.BlockSpec(memory_space=VMEM)] * 7,
        out_specs=[pl.BlockSpec(memory_space=VMEM)] * 2,
        scratch_shapes=line_scratch(CHUNKS, rows // CHUNKS, width),
        compiler_params=params(56, collective),
        name="input_back",
    )(gq, gkv, place, weight, inputs, mid, gain)


def mlp_kernel(share, middle_ref, x_ref, g_ref, wg_ref, wu_ref, wd_ref, hid_ref, gg_ref, gu_ref, down_ref, gn_ref, down_acc, gn_acc):
    step = pl.program_id(0)
    gate = nn(x_ref[...], wg_ref[...])
    up = nn(x_ref[...], wu_ref[...])
    grad = nn(g_ref[...], wd_ref[...])
    sigmoid = jax.nn.sigmoid(gate)
    silu = gate * sigmoid
    hidden = (silu * up).astype(BF16)
    g_up = (grad * silu).astype(BF16)
    g_gate = (grad * up * sigmoid * (1.0 + gate * (1.0 - sigmoid))).astype(BF16)
    hid_ref[...] = hidden
    gu_ref[...] = g_up
    gg_ref[...] = g_gate
    down = nt(hidden, wd_ref[...])
    gn = nt(g_gate, wg_ref[...]) + nt(g_up, wu_ref[...])

    @pl.when(step == 0)
    def _():
        down_acc[...] = down + middle_ref[...].astype(F32) * share
        gn_acc[...] = gn

    @pl.when(step > 0)
    def _():
        down_acc[...] += down
        gn_acc[...] += gn

    @pl.when(step == pl.num_programs(0) - 1)
    def _():
        down_ref[...] = down_acc[...].astype(BF16)
        gn_ref[...] = gn_acc[...].astype(BF16)


def mlp(middle, normed, grad, weight, n_tp):
    rows, width = normed.shape
    units = weight.shape[1] // 3
    tile = 256
    tiles = units // tile
    column = lambda at: pl.BlockSpec((width, tile), lambda j: (0, at * tiles + j))
    out = pl.BlockSpec((rows, tile), lambda j: (0, j))
    return pl.pallas_call(
        functools.partial(mlp_kernel, 1.0 / n_tp),
        grid=(tiles,),
        out_shape=[jax.ShapeDtypeStruct((rows, units), BF16)] * 3
        + [jax.ShapeDtypeStruct((rows, width), BF16)] * 2,
        in_specs=[whole((rows, width))] * 3 + [column(0), column(1), column(2)],
        out_specs=[out, out, out, whole((rows, width)), whole((rows, width))],
        scratch_shapes=[VMEM((rows, width), F32)] * 2,
        compiler_params=params(60),
        name="mlp",
    )(middle, normed, grad, weight, weight, weight)


def weight_kernel(starts, parts, *refs):
    out_ref = refs[-1]
    step = pl.program_id(0)
    at = 0
    for index, (lefts, first, last) in enumerate(starts):
        left_refs = [refs[i] for i in lefts]
        right_refs = refs[parts + at : parts + at + len(lefts)]
        at += len(lefts)

        @pl.when((step >= first) & (step < last))
        def _(left_refs=left_refs, right_refs=right_refs):
            total = tn(left_refs[0][...], right_refs[0][...])
            for left_ref, right_ref in zip(left_refs[1:], right_refs[1:]):
                total = total + tn(left_ref[...], right_ref[...])
            out_ref[...] = total.astype(BF16)


def weight_grads(lefts, groups, tile):
    rows, width = lefts[0].shape
    starts, specs, rights, at = [], [], [], 0
    for indices, sides in groups:
        tiles = sides[0].shape[1] // tile
        starts.append((indices, at, at + tiles))
        for side in sides:
            rights.append(side)
            specs.append(
                pl.BlockSpec(
                    (rows, tile), lambda j, at=at, tiles=tiles: (0, jnp.clip(j - at, 0, tiles - 1))
                )
            )
        at += tiles
    return pl.pallas_call(
        functools.partial(weight_kernel, starts, len(lefts)),
        grid=(at,),
        out_shape=jax.ShapeDtypeStruct((width, at * tile), BF16),
        in_specs=[whole((rows, width))] * len(lefts) + specs,
        out_specs=pl.BlockSpec((width, tile), lambda j: (0, j)),
        compiler_params=params(60),
        name="weight_grads",
    )(*lefts, *rights)


def gains_kernel(n_ctx, n_tp, x_ref, out_ref, got, send_sem, recv_sem, line_got, line_send, line_recv):
    me, place = lax.axis_index("ctx"), lax.axis_index("tp")
    barrier = pltpu.get_barrier_semaphore()
    others = [lax.rem(me + d, n_ctx) for d in range(1, n_ctx)]
    members = [lax.rem(place + d, n_tp) for d in range(1, n_tp)]
    for other in others:
        pl.semaphore_signal(barrier, inc=1, device_id=(other, place), device_id_type=MESH)
    for member in members:
        pl.semaphore_signal(barrier, inc=1, device_id=(me, member), device_id_type=MESH)
    pl.semaphore_wait(barrier, n_ctx + n_tp - 2)
    copies = [
        pltpu.make_async_remote_copy(
            src_ref=x_ref.at[other],
            dst_ref=got.at[d],
            send_sem=send_sem.at[d],
            recv_sem=recv_sem.at[d],
            device_id=(other, place),
            device_id_type=MESH,
        )
        for d, other in enumerate(others)
    ]
    for copy in copies:
        copy.start()
    total = x_ref[me]
    for d, copy in enumerate(copies):
        copy.wait()
        total = total + got[d]
    out_ref[...] = total
    copies = [
        pltpu.make_async_remote_copy(
            src_ref=out_ref,
            dst_ref=line_got.at[d],
            send_sem=line_send.at[d],
            recv_sem=line_recv.at[d],
            device_id=(me, member),
            device_id_type=MESH,
        )
        for d, member in enumerate(members)
    ]
    for copy in copies:
        copy.start()
    low = total[4:]
    for d, copy in enumerate(copies):
        copy.wait()
        low = low + line_got[d, 4:, :]
    out_ref[4:, :] = low


def sum_gains(blocks, n_ctx, n_tp, collective):
    dma = pltpu.SemaphoreType.DMA
    return pl.pallas_call(
        functools.partial(gains_kernel, n_ctx, n_tp),
        out_shape=jax.ShapeDtypeStruct((8, 128), F32),
        in_specs=[pl.BlockSpec(memory_space=VMEM)],
        out_specs=pl.BlockSpec(memory_space=VMEM),
        scratch_shapes=[
            VMEM((n_ctx - 1, 8, 128), F32),
            dma((n_ctx - 1,)),
            dma((n_ctx - 1,)),
            VMEM((n_tp - 1, 8, 128), F32),
            dma((n_tp - 1,)),
            dma((n_tp - 1,)),
        ],
        compiler_params=params(16, collective),
        name="sum_gains",
    )(blocks)


def sort_runs(packed_runs):
    place = jnp.sum((packed_runs[:, None, :] < packed_runs[:, :, None]).astype(jnp.int32), axis=2)
    slots = jnp.arange(packed_runs.shape[1], dtype=jnp.int32)
    in_order = jnp.sum(
        jnp.where(place[:, :, None] == slots[None, None, :], packed_runs[:, :, None], 0), axis=1
    )
    return place, in_order


def layout(lengths_row, order_row, rank, n_ctx, head):
    runs = order_row.reshape(n_ctx, -1)
    rows = runs.shape[1]
    place, in_order = sort_runs(runs)
    own_place = lax.dynamic_index_in_dim(place, rank, 0, keepdims=False)
    packed = lax.dynamic_index_in_dim(in_order, rank, 0, keepdims=False)
    starts = jnp.cumsum(lengths_row) - lengths_row
    first = jnp.max(jnp.where(starts[None, :] <= packed[:, None], starts[None, :], 0), axis=1)
    position = packed - first
    inverse = jnp.exp(jnp.arange(head // 2, dtype=F32) * (-2.0 * math.log(THETA) / head))
    angles = position.astype(F32)[:, None] * inverse[None, :]
    cosine, sine = jnp.cos(angles), jnp.sin(angles)
    cosine = jnp.concatenate([cosine, cosine], axis=1)
    sine = jnp.concatenate([-sine, sine], axis=1)
    slots = jnp.arange(rows, dtype=jnp.int32)
    to_slot = (own_place[:, None] == slots[None, :]).astype(BF16)
    to_sorted = (own_place[None, :] == slots[:, None]).astype(BF16)
    blocks = rows // SUB
    grouped = in_order.reshape(n_ctx, blocks, SUB)
    smallest = jnp.min(grouped[:, :, 0], axis=0)
    largest = jnp.max(grouped[:, :, SUB - 1], axis=0)
    oldest = first.reshape(-1, QROWS)[:, 0]
    newest = packed.reshape(-1, QROWS)[:, QROWS - 1]
    lo = jnp.sum((largest[None, :] < oldest[:, None]).astype(jnp.int32), axis=1)
    hi = jnp.sum((smallest[None, :] <= newest[:, None]).astype(jnp.int32), axis=1)
    keys = grouped.transpose(1, 0, 2).reshape(blocks, n_ctx * SUB)
    pk_col = jnp.broadcast_to(keys[:, :, None], (blocks, n_ctx * SUB, 8))
    marks = (
        lo,
        hi,
        keys[:, None, :],
        packed[:, None],
        first[:, None],
        pk_col,
        packed[None, :],
        first[None, :],
    )
    return to_slot, to_sorted, cosine, sine, marks


def on_device(
    n_ctx,
    n_tp,
    hidden_in,
    seq_lengths,
    token_order,
    attn_gain,
    w_query,
    w_key,
    w_value,
    query_gain,
    key_gain,
    w_out,
    mlp_gain,
    w_gate,
    w_up,
    w_down,
    cotangent,
):
    micro_count, rows, width = hidden_in.shape
    head = query_gain.shape[0]
    heads, kv_heads = w_query.shape[1] // head, w_key.shape[1] // head
    rank = lax.axis_index("ctx")
    queries = heads * head
    units = w_gate.shape[1]
    q_gain, k_gain = query_gain[None, :], key_gain[None, :]
    a_gain, m_gain = attn_gain[None, :], mlp_gain[None, :]

    pieces = [w_query]
    for n in range(kv_heads):
        at = slice(n * head, (n + 1) * head)
        pieces += [w_key[:, at], w_value[:, at]]
    qkv_w, out_w = gather_ctx([jnp.concatenate(pieces, axis=1), w_out.T], n_ctx, 0)
    mlp_own = jnp.concatenate([w_gate, w_up, w_down.T], axis=1)
    mlp_own, qkv_w = lax.optimization_barrier((mlp_own, qkv_w))
    mlp_w = lax.all_gather(mlp_own, "ctx", axis=0, tiled=True)

    orders = [layout(seq_lengths[b], token_order[b], rank, n_ctx, head) for b in range(micro_count)]
    inputs = hidden_in.astype(F32)
    inverse = lax.rsqrt(jnp.mean(inputs * inputs, axis=-1, keepdims=True) + EPSILON)
    normed = (inputs * inverse * attn_gain).astype(BF16)
    sorted_normed = [nn(orders[b][1], normed[b]).astype(BF16) for b in range(micro_count)]

    projected = []
    for b in range(micro_count):
        q, kv, raw = project_qkv(
            sorted_normed[b], qkv_w, orders[b][2], orders[b][3], q_gain, k_gain, heads, kv_heads
        )
        (kv_all,) = gather_ctx([kv], n_ctx, 1)
        projected.append((q, kv_all.reshape(n_ctx, rows, -1), raw))

    state = []
    for b in range(micro_count):
        q, kv_all, raw = projected[b]
        mixed_full, mass = attend_forward(q, kv_all, orders[b][4], head, kv_heads)
        mixed, middle, normed_two = attn_out(
            mixed_full, orders[b][0], out_w, hidden_in[b], m_gain, n_tp, 2
        )
        state.append((mixed_full, mass, mixed, middle, normed_two))

    fed = []
    for b in range(micro_count):
        mixed_full, mass, mixed, middle, normed_two = state[b]
        hidden, g_gate, g_up, down, g_n2 = mlp(middle, normed_two, cotangent[b], mlp_w, n_tp)
        g_mid, g_mixed, d_mlp_gain = middle_back(
            g_n2, cotangent[b], middle, m_gain, out_w, n_tp, 3
        )
        fed.append((hidden, g_gate, g_up, down, g_mid, g_mixed, d_mlp_gain))

    both = range(micro_count)
    tile = 512 if units % 512 == 0 else 256
    mlp_grads = weight_grads(
        [state[b][4] for b in both] + [cotangent[b] for b in both],
        [
            (tuple(both), [fed[b][1] for b in both]),
            (tuple(both), [fed[b][2] for b in both]),
            (tuple(micro_count + b for b in both), [fed[b][0] for b in both]),
        ],
        tile,
    )
    mlp_grads = lax.psum_scatter(mlp_grads, "ctx", scatter_dimension=0, tiled=True)

    downs = jnp.stack([fed[b][3] for b in both])
    downs, last = lax.optimization_barrier((downs, fed[-1][5]))
    fed[-1] = fed[-1][:5] + (last,) + fed[-1][6:]
    layer_out = lax.psum(downs, "tp")

    attended = []
    for b in both:
        q, kv_all, raw = projected[b]
        to_slot, to_sorted, cosine, sine, marks = orders[b]
        g_mixed = nn(to_sorted, fed[b][5]).astype(BF16)
        dq, dkv, d_query_gain = attend_backward(
            q, kv_all, marks, g_mixed, state[b][0], state[b][1], raw, cosine, sine, q_gain, head, kv_heads
        )
        dkv = lax.psum_scatter(
            dkv.reshape(n_ctx * rows, -1), "ctx", scatter_dimension=0, tiled=True
        )
        attended.append((dq, dkv, d_query_gain))

    grads_in, d_attn_gain, kv_low, d_key_gain = [], [], [], []
    for b in both:
        to_slot, to_sorted, cosine, sine, marks = orders[b]
        gkv, dk_gain = key_back(attended[b][1], projected[b][2], cosine, sine, k_gain, kv_heads)
        kv_low.append(gkv)
        d_key_gain.append(dk_gain)
        grad_in, da_gain = input_back(
            attended[b][0], gkv, to_slot, qkv_w, hidden_in[b], fed[b][4], a_gain, n_tp, 4
        )
        grads_in.append(grad_in)
        d_attn_gain.append(da_gain)

    tile = min(512, 2 * kv_heads * head, queries)
    attn_grads = weight_grads(
        [sorted_normed[b] for b in both] + [fed[b][4] for b in both],
        [
            (tuple(both), [attended[b][0] for b in both]),
            (tuple(both), [kv_low[b] for b in both]),
            (tuple(micro_count + b for b in both), [state[b][2] for b in both]),
        ],
        tile,
    )
    attn_grads = lax.psum_scatter(attn_grads, "ctx", scatter_dimension=0, tiled=True).astype(F32)

    share = width // n_ctx // 128
    own = lambda gain: sum(gain).reshape(n_ctx, share, 128)
    spread = lambda gain: jnp.broadcast_to(sum(gain)[None], (n_ctx, 1, 128))
    blank = jnp.zeros((n_ctx, 4 - 2 * share, 128), F32)
    low_blank = jnp.zeros((n_ctx, 2, 128), F32)
    gains = sum_gains(
        jnp.concatenate(
            [
                own(d_attn_gain),
                own([fed[b][6] for b in both]),
                blank,
                spread([attended[b][2] for b in both]),
                spread(d_key_gain),
                low_blank,
            ],
            axis=1,
        ),
        n_ctx,
        n_tp,
        5,
    )

    mlp_grads = mlp_grads.astype(F32)
    at = queries
    keys, values = [], []
    for n in range(kv_heads):
        keys.append(attn_grads[:, at : at + head])
        values.append(attn_grads[:, at + head : at + 2 * head])
        at += 2 * head
    return (
        layer_out,
        jnp.stack(grads_in).astype(F32),
        gains[:share].reshape(-1),
        attn_grads[:, :queries],
        jnp.concatenate(keys, axis=1),
        jnp.concatenate(values, axis=1),
        gains[4],
        gains[5],
        attn_grads[:, at:].T,
        gains[share : 2 * share].reshape(-1),
        mlp_grads[:, :units],
        mlp_grads[:, units : 2 * units],
        mlp_grads[:, 2 * units :].T,
    )


def solution(mesh):
    rows = P("ctx", "tp")
    columns = P("tp", "ctx")
    tokens = P(None, "ctx", None)
    in_specs = (
        tokens,
        P(),
        P(),
        P(),
        rows,
        rows,
        rows,
        P(),
        P(),
        columns,
        P(),
        rows,
        rows,
        columns,
        tokens,
    )
    out_specs = (
        tokens,
        tokens,
        P("ctx"),
        rows,
        rows,
        rows,
        P(),
        P(),
        columns,
        P("ctx"),
        rows,
        rows,
        columns,
    )
    return jax.shard_map(
        functools.partial(on_device, mesh.shape["ctx"], mesh.shape["tp"]),
        mesh=mesh,
        in_specs=in_specs,
        out_specs=out_specs,
        check_vma=False,
    )
```

time: 1880 us -> 1050 us (0.56)
  waiting for transfers between devices: 1150 us -> 208 us
  Pallas kernels: 0 us -> 720 us
  matrix products: 412 us -> 8.03 us
  other arithmetic: 124 us -> 31.5 us
  local copies, waits for them, and re-layouts: 114 us -> 56.7 us
  blocking collectives: 53.3 us -> 0 us
    pallas_call x0 -> x22, Pallas kernels: none -> 720 us  [the longest x2 131 us: input_back(): pl.pallas_call(functools.partial(input_back_kernel, n_tp), out_shape=[jax...]
    psum x3 -> x1, waiting for transfers between devices: 602 us -> 149 us  [on_device(): layer_out = lax.psum(downs, 'tp')]
    dot_general x98 -> x4, matrix products: 412 us -> 8.03 us  [nn(): return jnp.dot(left_side, right_side, preferred_element_type=F32)]
    reduce_scatter x11 -> x4, waiting for transfers between devices: 336 us -> 59.3 us  [the longest x2 48.4 us: on_device(): lax.psum_scatter(dkv.reshape(n_ctx * rows, -1), 'ctx', scatter_dimension=...]
    all_gather x11 -> x1, waiting for transfers between devices: 207 us -> 0.01 us  [on_device(): mlp_w = lax.all_gather(mlp_own, 'ctx', axis=0, tiled=True)]
    reduce_sum x19 -> x6, other arithmetic: 55.1 us -> 6.05 us  [the longest x2 2.92 us: sort_runs(): jnp.sum(jnp.where(place[:, :, None] == slots[None, None, :], packed_runs[...]
    psum x1 -> x0, blocking collectives: 39.2 us -> none  [on_device(): lax.psum((acc_query_gain, acc_key_gain), ('ctx', 'tp'))]
    dynamic_slice x44 -> x3, local copies, waits for them, and re-layouts: 35.8 us -> 0.03 us  [the longest x2 0.02 us: layout(): packed = lax.dynamic_index_in_dim(in_order, rank, 0, keepdims=False)]
  transfers between devices with their start and end apart: 25 -> 6, of which waited for: 19 -> 3; matrix products, arithmetic and copies ran while one was open for 24% -> 5% of each run, Pallas kernels for 0% -> 52%
where the time goes in v1:
time: 1050 us; the launch traced here: 1040 us
  Pallas kernels  720 us (69%)
  waiting for transfers between devices  208 us (20%)
  local copies, waits for them, and re-layouts  56.7 us (5%)
  other arithmetic  31.5 us (3%)
  between operations  15.6 us (1%)
    psum x1, waiting for transfers between devices, on_device(): layer_out = lax.psum(downs, 'tp')  149 us
    pallas_call x2, Pallas kernels, input_back(): pl.pallas_call(functools.partial(input_back_kernel, n_tp), out_shape=[jax...  131 us
    pallas_call x2, Pallas kernels, attn_out(): pl.pallas_call(functools.partial(attn_out_kernel, n_tp), out_shape=[jax.S...  130 us
    pallas_call x2, Pallas kernels, middle_back(): pl.pallas_call(functools.partial(middle_back_kernel, n_tp), out_shape=[ja...  127 us
    pallas_call x3, Pallas kernels, gather_ctx(): pl.pallas_call(functools.partial(gather_kernel, count, n_ctx), out_shape=...  120 us
    pallas_call x2, Pallas kernels, mlp(): pl.pallas_call(functools.partial(mlp_kernel, 1.0 / n_tp), grid=(tiles,),...  66.2 us
    pallas_call x2, Pallas kernels, attend_backward(): pl.pallas_call(functools.partial(backward_kernel, head), grid_spec=pltpu....  56.9 us
    reduce_scatter x2, waiting for transfers between devices, on_device(): lax.psum_scatter(dkv.reshape(n_ctx * rows, -1), 'ctx', scatter_dimension=...  48.4 us
  transfers between devices with their start and end apart: 6, of which 3 were waited for; matrix products, arithmetic and copies ran while one was open for 5% of the time, Pallas kernels for 52%

profile of v1, /device:TPU:0, one launch (start us, length us, event | category | flops | bytes accessed | tf_op | source)
XLA Modules:
  0.0 1040.6 jit_solution(17359625796010432049)
XLA Ops:
  12.9 1.4 copy.54
  14.3 40.5 %gather_ctx.3 = (bf16[2048,1024]{1,0:T(8,128)(2,1)S(1)}, bf16[2048,512]{1,0:T(8,128)(2,1)S(1)}) custom-call(bf16[256,1024]{1,0:T(8,128)(2,1)S(1)} %slice_dynamic-update-slice_fusion.refs_0_, bf16[256,512]{1,0:T(8,128)(2,1)S(1)} %bitcast.78), custom_call_target="tpu_custom_call" | custom-call | tf_op jit(solution)/shard_map/gather_ctx/pallas_call | solution.py:121
  54.9 2.0 copy-done
  58.2 1.6 pad_maximum_fusion.1
  61.3 1.5 select_reduce_fusion.1
  64.8 1.5 select_reduce_fusion
  66.6 1.9 fusion.9
  68.7 3.9 fusion
  75.8 2.3 copy-done.1
  78.1 2.9 project_qkv.2
  81.0 42.1 %gather_ctx.4 = bf16[4096,512]{1,0:T(8,128)(2,1)S(1)} custom-call(bf16[512,512]{1,0:T(8,128)(2,1)S(1)} %get-tuple-element.68.refs_0_), custom_call_target="tpu_custom_call" | custom-call | tf_op jit(solution)/shard_map/gather_ctx/pallas_call | solution.py:121
  123.2 2.1 copy-done.3
  126.4 3.4 copy-done.4
  129.8 15.9 %attend_forward.2 = (f32[512,512]{1,0:T(8,128)S(1)}, f32[8,1,256]{2,1,0:T(1,128)S(1)}) custom-call(s32[4]{0:T(128)S(1)} %get-tuple-element.211.lo_ref, s32[4]{0:T(128)S(1)} %get-tuple-element.210.hi_ref, bf16[512,512]{1,0:T(8,128)(2,1)S(1)} %get-tuple-element.67.q_ref, bf16[8,512,512]{2,1,0:T(8,128)(2,1)S(1)} %bitcast.75, ...), custom_call_target="tpu_custom_call" | custom-call | tf_op jit(solution)/shard_map/attend_forward/pallas_call | solution.py:228
  146.9 2.3 slice_bitcast_fusion.7
  149.3 65.4 %attn_out.2 = (bf16[512,512]{1,0:T(8,128)(2,1)}, bf16[512,2048]{1,0:T(8,128)(2,1)}, bf16[512,2048]{1,0:T(8,128)(2,1)}) custom-call(f32[512,512]{1,0:T(8,128)} %copy-done.14, bf16[512,512]{1,0:T(8,128)(2,1)} %fusion.3.place_ref, bf16[2048,512]{1,0:T(8,128)(2,1)} %copy-done.7, bf16[512,2048]{1,0:T(8,128)(2,1)} %get-tuple-element.177.x_ref, f32[1,2048]{1,0:T(1,128)} %bitcast.98), custom_call_target="tpu_custom_call" | custom-call | tf_op jit(solution)/shard_map/attn_out/pallas_call | solution.py:555
  214.7 2.5 slice_bitcast_fusion.6
  217.2 33.1 %mlp.2 = (bf16[512,1536]{1,0:T(8,128)(2,1)}, bf16[512,1536]{1,0:T(8,128)(2,1)}, bf16[512,1536]{1,0:T(8,128)(2,1)}, bf16[512,2048]{1,0:T(8,128)(2,1)}, bf16[512,2048]{1,0:T(8,128)(2,1)}) custom-call(bf16[512,2048]{1,0:T(8,128)(2,1)} %get-tuple-element.71.middle_ref, bf16[512,2048]{1,0:T(8,128)(2,1)} %get-tuple-element.72.x_ref.refs_0_, ...), custom_call_target="tpu_custom_call" | custom-call | tf_op jit(solution)/shard_map/mlp/pallas_call | solution.py:684
  250.3 62.9 %middle_back.3 = (bf16[512,2048]{1,0:T(8,128)(2,1)}, bf16[512,512]{1,0:T(8,128)(2,1)}, f32[1,2048]{1,0:T(1,128)}) custom-call(bf16[512,2048]{1,0:T(8,128)(2,1)} %get-tuple-element.84.part_ref, bf16[512,2048]{1,0:T(8,128)(2,1)} %get-tuple-element.175.g_ref.refs_2_, bf16[512,2048]{1,0:T(8,128)(2,1)} %get-tuple-element.71.middle_ref, f32[1,2048]{1,0:T(1,128)} %bitcast.99, ...), custom_call_target="tpu_custom_call" | custom-call | tf_op jit(solution)/shard_map/middle_back/pallas_call | solution.py:592
  313.2 2.3 convolution_convert_fusion.3.g_ref
  315.5 1.7 broadcast_in_dim.64.pk_ref
  317.2 29.0 %attend_backward.2 = (bf16[512,512]{1,0:T(8,128)(2,1)}, bf16[8,512,512]{2,1,0:T(8,128)(2,1)}, f32[1,128]{1,0:T(1,128)}) custom-call(s32[4]{0:T(128)} %copy-done.36, s32[4]{0:T(128)} %copy-done.35, bf16[512,512]{1,0:T(8,128)(2,1)} %copy-done.26, bf16[8,512,512]{2,1,0:T(8,128)(2,1)} %bitcast.74, s32[8,512,8]{2,1,0:T(8,128)} %broadcast_in_dim.64.pk_ref, ...), custom_call_target="tpu_custom_call" | custom-call | tf_op jit(solution)/shard_map/attend_backward/pallas_call | solution.py:346
  347.2 3.2 convolution_convert_fusion.x_ref.refs_1_
  350.5 2.8 project_qkv.3
  353.4 37.7 %gather_ctx.5 = bf16[4096,512]{1,0:T(8,128)(2,1)S(1)} custom-call(bf16[512,512]{1,0:T(8,128)(2,1)S(1)} %get-tuple-element.76.refs_0_), custom_call_target="tpu_custom_call" | custom-call | tf_op jit(solution)/shard_map/gather_ctx/pallas_call | solution.py:121
  391.1 2.0 copy-done.5
  394.2 2.2 copy-done.6
  396.4 15.1 %attend_forward.3 = (f32[512,512]{1,0:T(8,128)S(1)}, f32[8,1,256]{2,1,0:T(1,128)S(1)}) custom-call(s32[4]{0:T(128)S(1)} %get-tuple-element.203.lo_ref, s32[4]{0:T(128)S(1)} %get-tuple-element.202.hi_ref, bf16[512,512]{1,0:T(8,128)(2,1)S(1)} %get-tuple-element.75.q_ref, bf16[8,512,512]{2,1,0:T(8,128)(2,1)S(1)} %bitcast.77, ...), custom_call_target="tpu_custom_call" | custom-call | tf_op jit(solution)/shard_map/attend_forward/pallas_call | solution.py:228
  413.4 64.9 %attn_out.3 = (bf16[512,512]{1,0:T(8,128)(2,1)}, bf16[512,2048]{1,0:T(8,128)(2,1)}, bf16[512,2048]{1,0:T(8,128)(2,1)}) custom-call(f32[512,512]{1,0:T(8,128)} %copy-done.15, bf16[512,512]{1,0:T(8,128)(2,1)} %fusion.4.place_ref, bf16[2048,512]{1,0:T(8,128)(2,1)} %copy-done.7, bf16[512,2048]{1,0:T(8,128)(2,1)} %get-tuple-element.178.x_ref, f32[1,2048]{1,0:T(1,128)} %bitcast.100), custom_call_target="tpu_custom_call" | custom-call | tf_op jit(solution)/shard_map/attn_out/pallas_call | solution.py:555
  478.3 33.1 %mlp.3 = (bf16[512,1536]{1,0:T(8,128)(2,1)}, bf16[512,1536]{1,0:T(8,128)(2,1)}, bf16[512,1536]{1,0:T(8,128)(2,1)}, bf16[512,2048]{1,0:T(8,128)(2,1)}, bf16[512,2048]{1,0:T(8,128)(2,1)}) custom-call(bf16[512,2048]{1,0:T(8,128)(2,1)} %get-tuple-element.78.middle_ref, bf16[512,2048]{1,0:T(8,128)(2,1)} %get-tuple-element.79.x_ref.refs_1_, ...), custom_call_target="tpu_custom_call" | custom-call | tf_op jit(solution)/shard_map/mlp/pallas_call | solution.py:684
  511.5 63.8 %middle_back.2 = (bf16[512,2048]{1,0:T(8,128)(2,1)}, bf16[512,512]{1,0:T(8,128)(2,1)}, f32[1,2048]{1,0:T(1,128)}) custom-call(bf16[512,2048]{1,0:T(8,128)(2,1)} %get-tuple-element.81.part_ref, bf16[512,2048]{1,0:T(8,128)(2,1)} %get-tuple-element.176.g_ref.refs_3_, bf16[512,2048]{1,0:T(8,128)(2,1)} %get-tuple-element.78.middle_ref, f32[1,2048]{1,0:T(1,128)} %bitcast.101, ...), custom_call_target="tpu_custom_call" | custom-call | tf_op jit(solution)/shard_map/middle_back/pallas_call | solution.py:592
  575.4 2.4 pad_maximum_fusion
  579.0 1.7 broadcast_in_dim.68.pk_ref
  580.7 27.9 %attend_backward.3 = (bf16[512,512]{1,0:T(8,128)(2,1)}, bf16[8,512,512]{2,1,0:T(8,128)(2,1)}, f32[1,128]{1,0:T(1,128)}) custom-call(s32[4]{0:T(128)} %copy-done.38, s32[4]{0:T(128)} %copy-done.37, bf16[512,512]{1,0:T(8,128)(2,1)} %copy-done.27, bf16[8,512,512]{2,1,0:T(8,128)(2,1)} %bitcast.76, s32[8,512,8]{2,1,0:T(8,128)} %broadcast_in_dim.68.pk_ref, ...), custom_call_target="tpu_custom_call" | custom-call | tf_op jit(solution)/shard_map/attend_backward/pallas_call | solution.py:346
  613.4 48.4 %reduce-scatter.7.cloned.1.call-done.grad_ref = bf16[512,512]{1,0:T(8,128)(2,1)} async-done(((bf16[4096,512]{1,0:T(8,128)(2,1)}), bf16[512,512]{1,0:T(8,128)(2,1)}) %reduce-scatter.7.cloned.1.call-update) | async-done | bytes 524304 | tf_op jit(solution)/shard_map/reduce_scatter | solution.py:951
  666.1 13.1 %weight_grads.2 = bf16[2048,1536]{1,0:T(8,128)(2,1)} custom-call(bf16[512,2048]{1,0:T(8,128)(2,1)} %copy-done.8, bf16[512,2048]{1,0:T(8,128)(2,1)} %copy-done.9, bf16[512,2048]{1,0:T(8,128)(2,1)} %get-tuple-element.91.mid_ref.refs_2_, bf16[512,2048]{1,0:T(8,128)(2,1)} %get-tuple-element.99.mid_ref.refs_3_, ...), custom_call_target="tpu_custom_call" | custom-call | tf_op jit(solution)/shard_map/weight_grads/pallas_call | solution.py:728
  679.5 28.3 %weight_grads.3 = bf16[2048,4608]{1,0:T(8,128)(2,1)} custom-call(bf16[512,2048]{1,0:T(8,128)(2,1)} %get-tuple-element.72.x_ref.refs_0_, bf16[512,2048]{1,0:T(8,128)(2,1)} %get-tuple-element.79.x_ref.refs_1_, bf16[512,2048]{1,0:T(8,128)(2,1)} %get-tuple-element.175.g_ref.refs_2_, bf16[512,2048]{1,0:T(8,128)(2,1)} %get-tuple-element.176.g_ref.refs_3_, ...), custom_call_target="tpu_custom_call" | custom-call | tf_op jit(solution)/shard_map/weight_grads/pallas_call | solution.py:728
  708.6 66.7 %input_back.2 = (bf16[512,2048]{1,0:T(8,128)(2,1)}, f32[1,2048]{1,0:T(1,128)}) custom-call(bf16[512,512]{1,0:T(8,128)(2,1)} %get-tuple-element.88.gq_ref.refs_4_, bf16[512,512]{1,0:T(8,128)(2,1)} %copy-done.24, bf16[512,512]{1,0:T(8,128)(2,1)} %fusion.3.place_ref, bf16[2048,1024]{1,0:T(8,128)(2,1)} %copy-done, bf16[512,2048]{1,0:T(8,128)(2,1)} %get-tuple-element.177.x_ref, ...), custom_call_target="tpu_custom_call" | custom-call | tf_op jit(solution)/shard_map/input_back/pallas_call | solution.py:631
  775.4 63.9 %input_back.3 = (bf16[512,2048]{1,0:T(8,128)(2,1)}, f32[1,2048]{1,0:T(1,128)}) custom-call(bf16[512,512]{1,0:T(8,128)(2,1)} %get-tuple-element.96.gq_ref.refs_5_, bf16[512,512]{1,0:T(8,128)(2,1)} %copy-done.25, bf16[512,512]{1,0:T(8,128)(2,1)} %fusion.4.place_ref, bf16[2048,1024]{1,0:T(8,128)(2,1)} %copy-done, bf16[512,2048]{1,0:T(8,128)(2,1)} %get-tuple-element.178.x_ref, ...), custom_call_target="tpu_custom_call" | custom-call | tf_op jit(solution)/shard_map/input_back/pallas_call | solution.py:631
  840.1 9.2 sum_gains.1
  850.3 5.5 maximum_convert_fusion
  855.9 1.4 convert_element_type.84
  860.6 10.8 %reduce-scatter.11.cloned.1.call-done = bf16[256,4608]{1,0:T(8,128)(2,1)} async-done(((bf16[2048,4608]{1,0:T(8,128)(2,1)}), bf16[256,4608]{1,0:T(8,128)(2,1)}) %reduce-scatter.11.cloned.1.call-update) | async-done | bytes 2359312 | tf_op jit(solution)/shard_map/reduce_scatter | solution.py:936
  871.5 2.2 convert_element_type.85
  874.9 3.1 copy.63
  878.0 2.1 fusion.11
  880.1 148.5 %all-reduce.2.cloned.1.call-done = bf16[2,512,2048]{2,1,0:T(8,128)(2,1)} async-done(((bf16[2,512,2048]{2,1,0:T(8,128)(2,1)}), bf16[2,512,2048]{2,1,0:T(8,128)(2,1)}) %all-reduce.2.cloned.1.call-update) | async-done | bytes 4194320 | tf_op jit(solution)/shard_map/psum | solution.py:941
  1028.6 4.8 copy.73
  (207 shorter events, 38.0 us)
Async XLA Ops:
  7.2 51.0 %copy-start.49 = (bf16[256,1536]{1,0:T(8,128)(2,1)S(1)}, bf16[256,1536]{1,0:T(8,128)(2,1)}, u32[]{:S(2)}) copy-start(bf16[256,1536]{1,0:T(8,128)(2,1)} %param.26) | copy-start | bytes 2359300
  7.2 51.0 %copy-start.48 = (bf16[256,1536]{1,0:T(8,128)(2,1)S(1)}, bf16[256,1536]{1,0:T(8,128)(2,1)}, u32[]{:S(2)}) copy-start(bf16[256,1536]{1,0:T(8,128)(2,1)} %param.27) | copy-start | bytes 2359300
  7.2 210.0 %all-gather.2.cloned.1.call-start = ((), (), s32[]{:S(2)}) async-start(), calls=%async_computation.4 | async-start | bytes 21233664 | tf_op jit(solution)/shard_map/all_gather | solution.py:891
  14.3 45.6 %copy-start.55 = (s32[2,4096]{1,0:T(2,128)S(1)}, s32[2,4096]{1,0:T(2,128)}, u32[]{:S(2)}) copy-start(s32[2,4096]{1,0:T(2,128)} %param.17) | copy-start | bytes 98308
  14.3 48.8 %copy-start.59 = (s32[2,3]{1,0:T(2,128)S(1)}, s32[2,3]{1,0:T(2,128)}, u32[]{:S(2)}) copy-start(s32[2,3]{1,0:T(2,128)} %param.16) | copy-start | bytes 76
  59.8 12.8 %copy-start.50 = (f32[2048]{0:T(1024)S(1)}, f32[2048]{0:T(1024)}, u32[]{:S(2)}) copy-start(f32[2048]{0:T(1024)} %param.18) | copy-start | bytes 24580
  59.8 548.9 %reduce-scatter.5.cloned.1.call-start = ((), (), s32[]{:S(2)}) async-start(), calls=%async_computation.6 | async-start | bytes 4718592 | tf_op jit(solution)/shard_map/reduce_scatter | solution.py:951
  63.4 9.2 copy-start.39
  63.5 62.3 %copy-start.54 = (s32[1,512]{1,0:T(1,128)}, s32[1,512]{1,0:T(1,128)S(1)}, u32[]{:S(2)}) copy-start(s32[1,512]{1,0:T(1,128)S(1)} %constant_dynamic-slice_fusion.3.pq_ref) | copy-start | bytes 6148
  66.3 327.2 %copy-start.53 = (s32[1,512]{1,0:T(1,128)}, s32[1,512]{1,0:T(1,128)S(1)}, u32[]{:S(2)}) copy-start(s32[1,512]{1,0:T(1,128)S(1)} %constant_dynamic-slice_fusion.1.pq_ref) | copy-start | bytes 6148
  66.5 59.2 %copy-start.52 = (s32[512]{0:T(512)}, s32[512]{0:T(512)S(1)}, u32[]{:S(2)}) copy-start(s32[512]{0:T(512)S(1)} %select_reduce_fusion.3) | copy-start | bytes 6148
  66.5 326.9 %copy-start.51 = (s32[512]{0:T(512)}, s32[512]{0:T(512)S(1)}, u32[]{:S(2)}) copy-start(s32[512]{0:T(512)S(1)} %select_reduce_fusion.2) | copy-start | bytes 6148
  68.7 7.1 copy-start.16
  68.7 7.1 copy-start.18
  73.7 4.5 copy-start.1
  73.7 4.5 copy-start.30
  73.7 4.4 copy-start.34
  75.8 47.4 %copy-start.8 = (bf16[512,2048]{1,0:T(8,128)(2,1)}, bf16[512,2048]{1,0:T(8,128)(2,1)S(1)}, u32[]{:S(2)}) copy-start(bf16[512,2048]{1,0:T(8,128)(2,1)S(1)} %convolution_convert_fusion.1.x_ref.refs_0_) | copy-start | bytes 6291460
  81.0 42.2 %copy-start.10 = (f32[512,768]{1,0:T(8,128)}, f32[512,768]{1,0:T(8,128)S(1)}, u32[]{:S(2)}) copy-start(f32[512,768]{1,0:T(8,128)S(1)} %get-tuple-element.87.raw_ref) | copy-start | bytes 4718596
  81.0 64.7 %copy-start.26 = (bf16[512,512]{1,0:T(8,128)(2,1)}, bf16[512,512]{1,0:T(8,128)(2,1)S(1)}, u32[]{:S(2)}) copy-start(bf16[512,512]{1,0:T(8,128)(2,1)S(1)} %get-tuple-element.67.q_ref) | copy-start | bytes 1572868
  126.3 22.9 %copy-start.35 = (s32[4]{0:T(128)}, s32[4]{0:T(128)S(1)}, u32[]{:S(2)}) copy-start(s32[4]{0:T(128)S(1)} %get-tuple-element.210.hi_ref) | copy-start | bytes 52
  126.3 22.9 %copy-start.36 = (s32[4]{0:T(128)}, s32[4]{0:T(128)S(1)}, u32[]{:S(2)}) copy-start(s32[4]{0:T(128)S(1)} %get-tuple-element.211.lo_ref) | copy-start | bytes 52
  126.3 3.5 copy-start.4
  129.8 17.1 %copy-start.40 = (bf16[2,512,2048]{2,1,0:T(8,128)(2,1)S(1)}, bf16[2,512,2048]{2,1,0:T(8,128)(2,1)}, u32[]{:S(2)}) copy-start(bf16[2,512,2048]{2,1,0:T(8,128)(2,1)} %param.15) | copy-start | bytes 12582916
  145.7 3.5 copy-start.14
  145.7 3.5 copy-start.32
  149.2 65.4 %copy-start.43 = (bf16[2,512,2048]{2,1,0:T(8,128)(2,1)S(1)}, bf16[2,512,2048]{2,1,0:T(8,128)(2,1)}, u32[]{:S(2)}) copy-start(bf16[2,512,2048]{2,1,0:T(8,128)(2,1)} %param.29) | copy-start | bytes 12582916
  346.2 315.6 %reduce-scatter.7.cloned.1.call-start = ((), (), s32[]{:S(2)}) async-start(), calls=%async_computation.7 | async-start | bytes 4718592 | tf_op jit(solution)/shard_map/reduce_scatter | solution.py:951
  347.1 3.3 copy-start.20
  347.2 3.3 copy-start.22
  347.2 3.4 copy-start.2
  347.2 3.3 copy-start.31
  350.4 40.6 %copy-start.9 = (bf16[512,2048]{1,0:T(8,128)(2,1)}, bf16[512,2048]{1,0:T(8,128)(2,1)S(1)}, u32[]{:S(2)}) copy-start(bf16[512,2048]{1,0:T(8,128)(2,1)S(1)} %convolution_convert_fusion.x_ref.refs_1_) | copy-start | bytes 6291460
  353.4 37.7 %copy-start.12 = (f32[512,768]{1,0:T(8,128)}, f32[512,768]{1,0:T(8,128)S(1)}, u32[]{:S(2)}) copy-start(f32[512,768]{1,0:T(8,128)S(1)} %get-tuple-element.95.raw_ref) | copy-start | bytes 4718596
  353.4 58.1 %copy-start.27 = (bf16[512,512]{1,0:T(8,128)(2,1)}, bf16[512,512]{1,0:T(8,128)(2,1)S(1)}, u32[]{:S(2)}) copy-start(bf16[512,512]{1,0:T(8,128)(2,1)S(1)} %get-tuple-element.75.q_ref) | copy-start | bytes 1572868
  394.2 84.1 %copy-start.37 = (s32[4]{0:T(128)}, s32[4]{0:T(128)S(1)}, u32[]{:S(2)}) copy-start(s32[4]{0:T(128)S(1)} %get-tuple-element.202.hi_ref) | copy-start | bytes 52
  394.2 84.1 %copy-start.38 = (s32[4]{0:T(128)}, s32[4]{0:T(128)S(1)}, u32[]{:S(2)}) copy-start(s32[4]{0:T(128)S(1)} %get-tuple-element.203.lo_ref) | copy-start | bytes 52
  511.5 63.9 %copy-start.45 = (bf16[512,2048]{1,0:T(8,128)(2,1)S(1)}, bf16[512,2048]{1,0:T(8,128)(2,1)}, u32[]{:S(2)}) copy-start(bf16[512,2048]{1,0:T(8,128)(2,1)} %get-tuple-element.74) | copy-start | bytes 6291460
  511.5 63.9 %copy-start.47 = (bf16[512,2048]{1,0:T(8,128)(2,1)S(1)}, bf16[512,2048]{1,0:T(8,128)(2,1)}, u32[]{:S(2)}) copy-start(bf16[512,2048]{1,0:T(8,128)(2,1)} %get-tuple-element.80) | copy-start | bytes 6291460
  575.4 2.4 copy-start.60
  608.6 53.2 %copy-start.13 = (f32[512,768]{1,0:T(8,128)S(1)}, f32[512,768]{1,0:T(8,128)}, u32[]{:S(2)}) copy-start(f32[512,768]{1,0:T(8,128)} %copy-done.12) | copy-start | bytes 4718596
  608.6 247.2 %reduce-scatter.9.cloned.1.call-start = ((), (), s32[]{:S(2)}) async-start(), calls=%async_computation.8 | async-start | bytes 7077888 | tf_op jit(solution)/shard_map/reduce_scatter | solution.py:978
  679.2 192.2 %reduce-scatter.11.cloned.1.call-start = ((), (), s32[]{:S(2)}) async-start(), calls=%async_computation.9 | async-start | bytes 21233664 | tf_op jit(solution)/shard_map/reduce_scatter | solution.py:936
  707.9 320.7 %all-reduce.2.cloned.1.call-start = ((), (), s32[]{:S(2)}) async-start(), calls=%async_computation.5 | async-start | bytes 8388608 | tf_op jit(solution)/shard_map/psum | solution.py:941
  775.3 63.9 %copy-start.58 = (f32[1,2048]{1,0:T(1,128)S(1)}, f32[1,2048]{1,0:T(1,128)}, u32[]{:S(2)}) copy-start(f32[1,2048]{1,0:T(1,128)} %get-tuple-element.101) | copy-start | bytes 24580
  775.3 75.0 %copy-start.46 = (bf16[512,2048]{1,0:T(8,128)(2,1)S(1)}, bf16[512,2048]{1,0:T(8,128)(2,1)}, u32[]{:S(2)}) copy-start(bf16[512,2048]{1,0:T(8,128)(2,1)} %get-tuple-element.92) | copy-start | bytes 6291460
  855.9 2.4 copy-start.42
  873.7 4.3 copy-start.41
  (21 other events, 25.9 us)
Sparse Core Ops, SparseCore 0:
  59.9 122.0 all-gather.1
  346.4 56.4 reduce-scatter.4
  608.8 52.9 reduce-scatter.6
  679.4 61.7 reduce-scatter.8
  745.0 126.3 reduce-scatter.10
  873.8 154.7 all-reduce.1

commit v2 on v1

--- a/solution.py
+++ b/solution.py
@@ -50,9 +50,13 @@
     return pl.BlockSpec(shape, lambda *ids: (0,) * len(shape))
 
 
-def gather_kernel(count, n_ctx, *refs):
-    sources, results, sems = refs[:count], refs[count : 2 * count], refs[2 * count :]
+def after(value, *others):
+    return lax.optimization_barrier((value, others))[0]
+
+
+def gather_parts(sources, results, sems, n_ctx):
     own_sem, send_sem, recv_sem, pass_sem, take_sem = sems
+    count = len(sources)
     me = lax.axis_index("ctx")
     column = lax.axis_index("tp")
     chip, core = me // 2, lax.rem(me, 2)
@@ -61,12 +65,6 @@
 
     def peer(d):
         return jnp.bitwise_xor(chip, d) * 2 + core
-
-    barrier = pltpu.get_barrier_semaphore()
-    pl.semaphore_signal(barrier, inc=1, device_id=(partner, column), device_id_type=MESH)
-    for d in range(1, chips):
-        pl.semaphore_signal(barrier, inc=1, device_id=(peer(d), column), device_id_type=MESH)
-    pl.semaphore_wait(barrier, chips)
 
     def rows_of(array, owner):
         rows = sources[array].shape[0]
@@ -96,22 +94,73 @@
     def local(array):
         return pltpu.make_async_copy(sources[array], rows_of(array, me), own_sem.at[array])
 
+    def onward(array, d):
+        rows = sources[array].shape[0]
+        half = rows // 2
+        slot = 3 if d == 1 else 0
+
+        def of(owner):
+            at = pl.multiple_of(owner * rows + (0 if d == 1 else half), half)
+            return results[array].at[pl.ds(at, half)]
+
+        return pltpu.make_async_remote_copy(
+            src_ref=of(peer(d)),
+            dst_ref=of(peer(d)),
+            send_sem=send_sem.at[array, slot],
+            recv_sem=recv_sem.at[array, slot],
+            device_id=(peer(3 - d), column),
+            device_id_type=MESH,
+        )
+
+    direct = range(1, chips) if chips != 4 else (1, 2)
+
+    def start():
+        for d in direct:
+            for array in range(count):
+                across(array, d).start()
+        for array in range(count):
+            passed(array, 0).start()
+            local(array).start()
+
+    def relay(array, d):
+        if d in direct:
+            across(array, d).wait_recv()
+            if chips == 4:
+                onward(array, d).start()
+        else:
+            onward(array, 1).wait_recv()
+            onward(array, 2).wait_recv()
+        passed(array, d).start()
+
+    def finish():
+        for array in range(count):
+            local(array).wait()
+            for d in range(chips):
+                if d in direct:
+                    across(array, d).wait_send()
+                elif d > 0:
+                    onward(array, 1).wait_send()
+                    onward(array, 2).wait_send()
+                passed(array, d).wait_send()
+                passed(array, d).wait_recv()
+
+    peers = [(partner, column)] + [(peer(d), column) for d in direct]
+    return peers, start, relay, finish
+
+
+def gather_kernel(count, n_ctx, *refs):
+    peers, start, relay, finish = gather_parts(
+        refs[:count], refs[count : 2 * count], refs[2 * count :], n_ctx
+    )
+    barrier = pltpu.get_barrier_semaphore()
+    for peer in peers:
+        pl.semaphore_signal(barrier, inc=1, device_id=peer, device_id_type=MESH)
+    pl.semaphore_wait(barrier, len(peers))
+    start()
     for array in range(count):
-        for d in range(1, chips):
-            across(array, d).start()
-        passed(array, 0).start()
-        local(array).start()
-    for array in range(count):
-        for d in range(1, chips):
-            across(array, d).wait_recv()
-            passed(array, d).start()
-    for array in range(count):
-        local(array).wait()
-        for d in range(chips):
-            if d > 0:
-                across(array, d).wait_send()
-            passed(array, d).wait_send()
-            passed(array, d).wait_recv()
+        for d in range(1, n_ctx // 2):
+            relay(array, d)
+    finish()
 
 
 def gather_ctx(arrays, n_ctx, collective):
@@ -309,7 +358,7 @@
         at = pl.ds(pl.multiple_of(j * SUB, SUB), SUB)
         keys = kv_ref[:, at, :head].reshape(runs * SUB, head)
         values = kv_ref[:, at, head:].reshape(runs * SUB, head)
-        packed = pk_ref[j][:, :1]
+        packed = jnp.broadcast_to(pk_ref[j], (8, pk_ref.shape[2])).T[:, :1]
         allowed = (packed <= newest) & (packed >= oldest)
         probs = jnp.where(allowed, jnp.exp2(nt(keys, query) * (scale * LOG2E) - mass), 0.0)
         dscores = (probs * (nt(values, grad) - row_dot)).astype(BF16)
@@ -337,7 +386,7 @@
 
 
 def attend_backward(query, kv, marks, grad, out, mass, raw, cosine, sine, gain, head, kv_heads):
-    lo, hi, unused, unused_too, unused_three, pk_col, pq_row, sq_row = marks
+    lo, hi, pk_row, unused, unused_too, pq_row, sq_row = marks
     rows, width = query.shape
     runs = kv.shape[0]
     group = width // (kv_heads * head)
@@ -351,7 +400,7 @@
             in_specs=[
                 pl.BlockSpec((QROWS, group * head), own),
                 pl.BlockSpec((runs, rows, 2 * head), lambda n, i, *s: (0, 0, n)),
-                whole(pk_col.shape),
+                whole(pk_row.shape),
                 pl.BlockSpec((1, QROWS), lambda n, i, *s: (0, i)),
                 pl.BlockSpec((1, QROWS), lambda n, i, *s: (0, i)),
                 pl.BlockSpec((QROWS, group * head), own),
@@ -376,7 +425,7 @@
         ],
         compiler_params=params(56),
         name="attend_backward",
-    )(lo, hi, query, kv, pk_col, pq_row, sq_row, grad, out, mass, raw, cosine, sine, gain)
+    )(lo, hi, query, kv, pk_row, pq_row, sq_row, grad, out, mass, raw, cosine, sine, gain)
 
 
 def key_back_kernel(head, kv_heads, grad_ref, raw_ref, cos_ref, sin_ref, gain_ref, out_ref, dgain_ref):
@@ -409,19 +458,55 @@
     )(grad, raw, cosine, sine, gain)
 
 
-def line_scratch(chunks, rows, width):
+def run_jobs(n_tp, line, jobs, collective, megabytes, name, alias=None):
+    rows, width = line[2], line[3]
+    chunks = CHUNKS
     dma = pltpu.SemaphoreType.DMA
-    buffer = VMEM((chunks, rows, width), BF16)
-    return [buffer] * 5 + [dma((2, chunks)), dma((2, chunks))]
-
-
-def line_sum(n_tp, scratch, produce, consume):
+    buffer = VMEM((chunks, rows // chunks, width), BF16)
+    line_scratch = [buffer] * 5 + [dma((2, chunks)), dma((2, chunks))]
+    parts = [(line[0], line[1], line_scratch)] + [job[:3] for job in jobs]
+    space = lambda inside: pl.BlockSpec(memory_space=VMEM if inside else ANY)
+    n_ins = [len(part[0]) for part in parts]
+    n_outs = [len(part[1]) for part in parts]
+    n_scratch = [len(part[2]) for part in parts]
+
+    def kernel(*refs):
+        def split(at, counts):
+            groups = []
+            for count in counts:
+                groups.append(refs[at : at + count])
+                at += count
+            return groups
+
+        ins = split(0, n_ins)
+        outs = split(sum(n_ins), n_outs)
+        scratch = split(sum(n_ins) + sum(n_outs), n_scratch)
+        bound = [job[3](ins[i + 1], outs[i + 1], scratch[i + 1]) for i, job in enumerate(jobs)]
+        produce, consume = line[4](ins[0], outs[0])
+        line_sum(n_tp, scratch[0], produce, consume, bound)
+
+    return pl.pallas_call(
+        kernel,
+        out_shape=[out[0] for part in parts for out in part[1]],
+        in_specs=[space(inside) for part in parts for unused, inside in part[0]],
+        out_specs=[space(inside) for part in parts for unused, inside in part[1]],
+        scratch_shapes=[item for part in parts for item in part[2]],
+        input_output_aliases=alias or {},
+        compiler_params=params(megabytes, collective),
+        name=name,
+    )(*[array for part in parts for array, unused in part[0]])
+
+
+def line_sum(n_tp, scratch, produce, consume, jobs):
     part, from_left, from_right, to_right, to_left, send_sem, recv_sem = scratch
     chunks = part.shape[0]
     place = lax.axis_index("tp")
     line = lax.axis_index("ctx")
     has_left, has_right = place > 0, place < n_tp - 1
     barrier = pltpu.get_barrier_semaphore()
+    peers = [peer for job in jobs for peer in job[0]]
+    for peer in peers:
+        pl.semaphore_signal(barrier, inc=1, device_id=peer, device_id_type=MESH)
 
     @pl.when(has_left)
     def _():
@@ -431,7 +516,11 @@
     def _():
         pl.semaphore_signal(barrier, inc=1, device_id=(line, place + 1), device_id_type=MESH)
 
-    pl.semaphore_wait(barrier, has_left.astype(jnp.int32) + has_right.astype(jnp.int32))
+    pl.semaphore_wait(
+        barrier, has_left.astype(jnp.int32) + has_right.astype(jnp.int32) + len(peers)
+    )
+    for job in jobs:
+        job[1]()
 
     def right(c):
         return pltpu.make_async_remote_copy(
@@ -507,9 +596,14 @@
             def _():
                 consume(c_out, to_right[c_out].astype(F32))
 
+        for job in jobs:
+            job[2](s)
         return carry
 
     lax.fori_loop(0, chunks + LAG * (n_tp - 1), step, 0)
+
+    for job in jobs:
+        job[3]()
 
     def finish(c, carry):
         @pl.when(has_right)
@@ -533,165 +627,366 @@
     return jnp.mean(values * values, axis=-1, keepdims=True)
 
 
-def attn_out_kernel(n_tp, mixed_ref, place_ref, w_ref, x_ref, gain_ref, own_ref, middle_ref, normed_ref, *scratch):
-    rows = scratch[0].shape[1]
-
-    def produce(c):
-        own = nn(place_ref[piece(c, rows), :], mixed_ref[...].astype(BF16)).astype(BF16)
-        own_ref[piece(c, rows), :] = own
-        return nt(own, w_ref[...])
-
-    def consume(c, total):
-        middle = x_ref[piece(c, rows), :].astype(F32) + total
-        middle_ref[piece(c, rows), :] = middle.astype(BF16)
-        unit = middle * lax.rsqrt(mean_square(middle) + EPSILON)
-        normed_ref[piece(c, rows), :] = (unit * gain_ref[...]).astype(BF16)
-
-    line_sum(n_tp, scratch, produce, consume)
-
-
-def attn_out(mixed, place, weight, inputs, gain, n_tp, collective):
+def shape(rows, width, dtype=BF16):
+    return jax.ShapeDtypeStruct((rows, width), dtype)
+
+
+def attn_out_line(mixed, place, weight, inputs, gain):
     rows, width = inputs.shape
-    return pl.pallas_call(
-        functools.partial(attn_out_kernel, n_tp),
-        out_shape=[
-            jax.ShapeDtypeStruct(mixed.shape, BF16),
-            jax.ShapeDtypeStruct((rows, width), BF16),
-            jax.ShapeDtypeStruct((rows, width), BF16),
-        ],
-        in_specs=[pl.BlockSpec(memory_space=VMEM)] * 5,
-        out_specs=[pl.BlockSpec(memory_space=VMEM)] * 3,
-        scratch_shapes=line_scratch(CHUNKS, rows // CHUNKS, width),
-        compiler_params=params(56, collective),
-        name="attn_out",
-    )(mixed, place, weight, inputs, gain)
-
-
-def middle_back_kernel(n_tp, part_ref, g_ref, middle_ref, gain_ref, w_ref, low_ref, mixed_ref, dgain_ref, *scratch):
-    rows = scratch[0].shape[1]
-    dgain_ref[...] = jnp.zeros_like(dgain_ref)
-
-    def produce(c):
-        return part_ref[piece(c, rows), :]
-
-    def consume(c, total):
-        middle = middle_ref[piece(c, rows), :].astype(F32)
-        inverse = lax.rsqrt(mean_square(middle) + EPSILON)
-        unit = middle * inverse
-        dgain_ref[...] += jnp.sum(total * unit, axis=0, keepdims=True)
-        grad = g_ref[piece(c, rows), :].astype(F32) + back(total, unit, inverse, gain_ref[...])
-        low = grad.astype(BF16)
-        low_ref[piece(c, rows), :] = low
-        mixed_ref[piece(c, rows), :] = nn(low, w_ref[...]).astype(BF16)
-
-    line_sum(n_tp, scratch, produce, consume)
-
-
-def middle_back(part, grad, middle, gain, weight, n_tp, collective):
+    size = rows // CHUNKS
+
+    def bind(ins, outs):
+        mixed_ref, place_ref, w_ref, x_ref, gain_ref = ins
+        own_ref, middle_ref, normed_ref = outs
+
+        def produce(c):
+            own = nn(place_ref[piece(c, size), :], mixed_ref[...].astype(BF16)).astype(BF16)
+            own_ref[piece(c, size), :] = own
+            return nt(own, w_ref[...])
+
+        def consume(c, total):
+            middle = x_ref[piece(c, size), :].astype(F32) + total
+            middle_ref[piece(c, size), :] = middle.astype(BF16)
+            unit = middle * lax.rsqrt(mean_square(middle) + EPSILON)
+            normed_ref[piece(c, size), :] = (unit * gain_ref[...]).astype(BF16)
+
+        return produce, consume
+
+    return (
+        [(item, True) for item in (mixed, place, weight, inputs, gain)],
+        [(shape(*mixed.shape), True), (shape(rows, width), True), (shape(rows, width), True)],
+        rows,
+        width,
+        bind,
+    )
+
+
+def middle_back_line(part, grad, middle, gain, weight):
     rows, width = grad.shape
-    return pl.pallas_call(
-        functools.partial(middle_back_kernel, n_tp),
-        out_shape=[
-            jax.ShapeDtypeStruct((rows, width), BF16),
-            jax.ShapeDtypeStruct((rows, weight.shape[1]), BF16),
-            jax.ShapeDtypeStruct((1, width), F32),
-        ],
-        in_specs=[pl.BlockSpec(memory_space=VMEM)] * 5,
-        out_specs=[pl.BlockSpec(memory_space=VMEM)] * 3,
-        scratch_shapes=line_scratch(CHUNKS, rows // CHUNKS, width),
-        compiler_params=params(56, collective),
-        name="middle_back",
-    )(part, grad, middle, gain, weight)
-
-
-def input_back_kernel(n_tp, gq_ref, gkv_ref, place_ref, w_ref, x_ref, mid_ref, gain_ref, out_ref, dgain_ref, *scratch):
-    rows = scratch[0].shape[1]
-    queries = gq_ref.shape[1]
-    dgain_ref[...] = jnp.zeros_like(dgain_ref)
-
-    def produce(c):
-        place = place_ref[piece(c, rows), :]
-        own_q = nn(place, gq_ref[...]).astype(BF16)
-        own_kv = nn(place, gkv_ref[...]).astype(BF16)
-        return nt(own_q, w_ref[:, :queries]) + nt(own_kv, w_ref[:, queries:])
-
-    def consume(c, total):
-        x = x_ref[piece(c, rows), :].astype(F32)
-        inverse = lax.rsqrt(mean_square(x) + EPSILON)
-        unit = x * inverse
-        dgain_ref[...] += jnp.sum(total * unit, axis=0, keepdims=True)
-        grad = mid_ref[piece(c, rows), :].astype(F32) + back(total, unit, inverse, gain_ref[...])
-        out_ref[piece(c, rows), :] = grad.astype(BF16)
-
-    line_sum(n_tp, scratch, produce, consume)
-
-
-def input_back(gq, gkv, place, weight, inputs, mid, gain, n_tp, collective):
+    size = rows // CHUNKS
+
+    def bind(ins, outs):
+        part_ref, g_ref, middle_ref, gain_ref, w_ref = ins
+        low_ref, mixed_ref, dgain_ref = outs
+        dgain_ref[...] = jnp.zeros_like(dgain_ref)
+
+        def produce(c):
+            return part_ref[piece(c, size), :]
+
+        def consume(c, total):
+            middle = middle_ref[piece(c, size), :].astype(F32)
+            inverse = lax.rsqrt(mean_square(middle) + EPSILON)
+            unit = middle * inverse
+            dgain_ref[...] += jnp.sum(total * unit, axis=0, keepdims=True)
+            grad = g_ref[piece(c, size), :].astype(F32) + back(total, unit, inverse, gain_ref[...])
+            low = grad.astype(BF16)
+            low_ref[piece(c, size), :] = low
+            mixed_ref[piece(c, size), :] = nn(low, w_ref[...]).astype(BF16)
+
+        return produce, consume
+
+    return (
+        [(item, True) for item in (part, grad, middle, gain, weight)],
+        [(shape(rows, width), True), (shape(rows, weight.shape[1]), True), (shape(1, width, F32), True)],
+        rows,
+        width,
+        bind,
+    )
+
+
+def input_back_line(gq, gkv, place, weight, inputs, mid, gain):
     rows, width = inputs.shape
-    return pl.pallas_call(
-        functools.partial(input_back_kernel, n_tp),
-        out_shape=[
-            jax.ShapeDtypeStruct((rows, width), BF16),
-            jax.ShapeDtypeStruct((1, width), F32),
-        ],
-        in_specs=[pl.BlockSpec(memory_space=VMEM)] * 7,
-        out_specs=[pl.BlockSpec(memory_space=VMEM)] * 2,
-        scratch_shapes=line_scratch(CHUNKS, rows // CHUNKS, width),
-        compiler_params=params(56, collective),
-        name="input_back",
-    )(gq, gkv, place, weight, inputs, mid, gain)
-
-
-def mlp_kernel(share, middle_ref, x_ref, g_ref, wg_ref, wu_ref, wd_ref, hid_ref, gg_ref, gu_ref, down_ref, gn_ref, down_acc, gn_acc):
-    step = pl.program_id(0)
-    gate = nn(x_ref[...], wg_ref[...])
-    up = nn(x_ref[...], wu_ref[...])
-    grad = nn(g_ref[...], wd_ref[...])
-    sigmoid = jax.nn.sigmoid(gate)
-    silu = gate * sigmoid
-    hidden = (silu * up).astype(BF16)
-    g_up = (grad * silu).astype(BF16)
-    g_gate = (grad * up * sigmoid * (1.0 + gate * (1.0 - sigmoid))).astype(BF16)
-    hid_ref[...] = hidden
-    gu_ref[...] = g_up
-    gg_ref[...] = g_gate
-    down = nt(hidden, wd_ref[...])
-    gn = nt(g_gate, wg_ref[...]) + nt(g_up, wu_ref[...])
-
-    @pl.when(step == 0)
-    def _():
-        down_acc[...] = down + middle_ref[...].astype(F32) * share
-        gn_acc[...] = gn
-
-    @pl.when(step > 0)
-    def _():
-        down_acc[...] += down
-        gn_acc[...] += gn
-
-    @pl.when(step == pl.num_programs(0) - 1)
-    def _():
-        down_ref[...] = down_acc[...].astype(BF16)
-        gn_ref[...] = gn_acc[...].astype(BF16)
-
-
-def mlp(middle, normed, grad, weight, n_tp):
+    size = rows // CHUNKS
+
+    def bind(ins, outs):
+        gq_ref, gkv_ref, place_ref, w_ref, x_ref, mid_ref, gain_ref = ins
+        out_ref, dgain_ref = outs
+        queries = gq_ref.shape[1]
+        dgain_ref[...] = jnp.zeros_like(dgain_ref)
+
+        def produce(c):
+            slots = place_ref[piece(c, size), :]
+            own_q = nn(slots, gq_ref[...]).astype(BF16)
+            own_kv = nn(slots, gkv_ref[...]).astype(BF16)
+            return nt(own_q, w_ref[:, :queries]) + nt(own_kv, w_ref[:, queries:])
+
+        def consume(c, total):
+            x = x_ref[piece(c, size), :].astype(F32)
+            inverse = lax.rsqrt(mean_square(x) + EPSILON)
+            unit = x * inverse
+            dgain_ref[...] += jnp.sum(total * unit, axis=0, keepdims=True)
+            grad = mid_ref[piece(c, size), :].astype(F32) + back(total, unit, inverse, gain_ref[...])
+            out_ref[piece(c, size), :] = grad.astype(BF16)
+
+        return produce, consume
+
+    return (
+        [(item, True) for item in (gq, gkv, place, weight, inputs, mid, gain)],
+        [(shape(rows, width), True), (shape(1, width, F32), True)],
+        rows,
+        width,
+        bind,
+    )
+
+
+def gather_job(own, n_ctx):
+    chips = n_ctx // 2
+    dma = pltpu.SemaphoreType.DMA
+
+    def bind(ins, outs, scratch):
+        peers, start, relay, finish = gather_parts(ins, outs, scratch, n_ctx)
+
+        def hook(s):
+            for d in range(1, chips):
+
+                @pl.when(s == CHUNKS - 2 * chips + 2 * d)
+                def _(d=d):
+                    relay(0, d)
+
+        return peers, start, hook, finish
+
+    return (
+        [(own, False)],
+        [(shape(n_ctx * own.shape[0], own.shape[1]), False)],
+        [dma((1,))] + [dma((1, chips))] * 4,
+        bind,
+    )
+
+
+def mlp_job(middle, normed, grad, weight, n_tp):
     rows, width = normed.shape
     units = weight.shape[1] // 3
     tile = 256
-    tiles = units // tile
-    column = lambda at: pl.BlockSpec((width, tile), lambda j: (0, at * tiles + j))
-    out = pl.BlockSpec((rows, tile), lambda j: (0, j))
-    return pl.pallas_call(
-        functools.partial(mlp_kernel, 1.0 / n_tp),
-        grid=(tiles,),
-        out_shape=[jax.ShapeDtypeStruct((rows, units), BF16)] * 3
-        + [jax.ShapeDtypeStruct((rows, width), BF16)] * 2,
-        in_specs=[whole((rows, width))] * 3 + [column(0), column(1), column(2)],
-        out_specs=[out, out, out, whole((rows, width)), whole((rows, width))],
-        scratch_shapes=[VMEM((rows, width), F32)] * 2,
-        compiler_params=params(60),
-        name="mlp",
-    )(middle, normed, grad, weight, weight, weight)
+    tiles, down_tiles = units // tile, width // tile
+    share = 1.0 / n_tp
+    dma = pltpu.SemaphoreType.DMA
+
+    def bind(ins, outs, scratch):
+        middle_ref, x_ref, g_ref, w_hbm = ins
+        hid_ref, gg_ref, gu_ref, down_ref, gn_ref = outs
+        w_ref, sem = scratch
+
+        def load(t, part):
+            at = pl.ds(pl.multiple_of(part * units + t * tile, tile), tile)
+            return pltpu.make_async_copy(w_hbm.at[:, at], w_ref.at[:, at], sem.at[part, t])
+
+        def start():
+            for t in range(tiles):
+                for part in range(3):
+                    load(t, part).start()
+
+        def first(t):
+            for part in range(3):
+                load(t, part).wait()
+            cols = [
+                pl.ds(pl.multiple_of(part * units + t * tile, tile), tile) for part in range(3)
+            ]
+            gate = nn(x_ref[...], w_ref[:, cols[0]])
+            up = nn(x_ref[...], w_ref[:, cols[1]])
+            grad = nn(g_ref[...], w_ref[:, cols[2]])
+            sigmoid = jax.nn.sigmoid(gate)
+            silu = gate * sigmoid
+            hid_ref[:, cols[0]] = (silu * up).astype(BF16)
+            gu_ref[:, cols[0]] = (grad * silu).astype(BF16)
+            gg_ref[:, cols[0]] = (grad * up * sigmoid * (1.0 + gate * (1.0 - sigmoid))).astype(BF16)
+
+        def second(t):
+            at = pl.ds(pl.multiple_of(t * tile, tile), tile)
+            down = nt(hid_ref[...], w_ref[at, 2 * units :])
+            down_ref[:, at] = (down + middle_ref[:, at].astype(F32) * share).astype(BF16)
+            gn_ref[:, at] = (
+                nt(gg_ref[...], w_ref[at, :units]) + nt(gu_ref[...], w_ref[at, units : 2 * units])
+            ).astype(BF16)
+
+        def hook(s):
+            h = s - 1
+
+            @pl.when((h >= 0) & (h < tiles))
+            def _():
+                first(h)
+
+            @pl.when((h >= tiles) & (h < tiles + down_tiles))
+            def _():
+                second(h - tiles)
+
+        return [], start, hook, lambda: None
+
+    return (
+        [(middle, True), (normed, True), (grad, True), (weight, False)],
+        [(shape(rows, units), True)] * 3 + [(shape(rows, width), True)] * 2,
+        [VMEM(weight.shape, BF16), dma((3, tiles))],
+        bind,
+    )
+
+
+def weight_job(lefts, groups, tile, every, room):
+    rows, width = lefts[0].shape
+    rights = [side for unused, sides in groups for side in sides]
+    counts = [sides[0].shape[1] // tile for unused, sides in groups]
+    total = sum(counts)
+    dma = pltpu.SemaphoreType.DMA
+    sources = list(lefts) + rights
+
+    def bind(ins, outs, scratch):
+        (out_hbm,) = outs
+        held, sems, out_buf, out_sem = scratch[: len(sources)], scratch[-3], scratch[-2], scratch[-1]
+
+        def load(i):
+            return pltpu.make_async_copy(ins[i], held[i], sems.at[i])
+
+        def save(h):
+            slot = lax.rem(h, 2)
+            return pltpu.make_async_copy(
+                out_buf.at[slot],
+                out_hbm.at[:, pl.ds(pl.multiple_of(h * tile, tile), tile)],
+                out_sem.at[slot],
+            )
+
+        def start():
+            for i in range(len(sources)):
+                load(i).start()
+
+        def hook(s):
+            @pl.when(s == 1)
+            def _():
+                for i in range(len(sources)):
+                    load(i).wait()
+
+            h = (s - 1) // every
+            now = (s >= 1) & (lax.rem(s - 1, every) == 0) & (h < total)
+
+            @pl.when(now & (h >= 2))
+            def _():
+                save(h - 2).wait()
+
+            first, at = 0, len(lefts)
+            for (indices, sides), count in zip(groups, counts):
+                left_refs = [held[i] for i in indices]
+                right_refs = held[at : at + len(sides)]
+                at += len(sides)
+
+                @pl.when(now & (h >= first) & (h < first + count))
+                def _(left_refs=left_refs, right_refs=right_refs, first=first):
+                    cols = pl.ds(pl.multiple_of((h - first) * tile, tile), tile)
+                    grads = tn(left_refs[0][...], right_refs[0][:, cols])
+                    for left_ref, right_ref in zip(left_refs[1:], right_refs[1:]):
+                        grads = grads + tn(left_ref[...], right_ref[:, cols])
+                    out_buf[lax.rem(h, 2)] = grads.astype(BF16)
+
+                first += count
+
+            @pl.when(now)
+            def _():
+                save(h).start()
+
+        def finish():
+            save(total - 2).wait()
+            save(total - 1).wait()
+
+        return [], start, hook, finish
+
+    return (
+        [(item, False) for item in sources] + [(room, False)],
+        [(shape(width, total * tile), False)],
+        [VMEM(item.shape, BF16) for item in sources]
+        + [dma((len(sources),)), VMEM((2, width, tile), BF16), dma((2,))],
+        bind,
+    )
+
+
+def scatter_job(whole_rows, n_ctx, dtype, first, second):
+    total, width = whole_rows.shape
+    rows = total // n_ctx
+    chips = n_ctx // 2
+    dma = pltpu.SemaphoreType.DMA
+
+    def bind(ins, outs, scratch):
+        (source,), (out_ref,) = ins, outs
+        mine, near, far, load_sem, near_send, near_recv, far_send, far_recv = scratch
+        me, column = lax.axis_index("ctx"), lax.axis_index("tp")
+        chip, core = me // 2, lax.rem(me, 2)
+
+        def block(d, which):
+            at = (jnp.bitwise_xor(chip, d) * 2 + which) * rows
+            return source.at[pl.ds(pl.multiple_of(at, rows), rows)]
+
+        def load(d):
+            return pltpu.make_async_copy(block(d, core), mine.at[d], load_sem.at[d])
+
+        def beside(d):
+            return pltpu.make_async_remote_copy(
+                src_ref=block(d, 1 - core),
+                dst_ref=near.at[d],
+                send_sem=near_send.at[d],
+                recv_sem=near_recv.at[d],
+                device_id=(chip * 2 + 1 - core, column),
+                device_id_type=MESH,
+            )
+
+        def across(d):
+            return pltpu.make_async_remote_copy(
+                src_ref=mine.at[d],
+                dst_ref=far.at[d - 1],
+                send_sem=far_send.at[d],
+                recv_sem=far_recv.at[d],
+                device_id=(jnp.bitwise_xor(chip, d) * 2 + core, column),
+                device_id_type=MESH,
+            )
+
+        peers = [(chip * 2 + 1 - core, column)] + [
+            (jnp.bitwise_xor(chip, d) * 2 + core, column) for d in range(1, chips)
+        ]
+        order = list(range(chips - 1, -1, -1))
+
+        def start():
+            for d in order:
+                load(d).start()
+                beside(d).start()
+
+        def near_sum():
+            for d in order:
+                load(d).wait()
+                beside(d).wait_recv()
+                mine[d] = (mine[d].astype(F32) + near[d].astype(F32)).astype(BF16)
+                if d > 0:
+                    across(d).start()
+
+        def far_sum():
+            for d in range(1, chips):
+                across(d).wait_recv()
+            result = mine[0].astype(F32)
+            for d in range(1, chips):
+                result = result + far[d - 1].astype(F32)
+            out_ref[...] = result.astype(dtype)
+
+        def hook(s):
+            @pl.when(s == first)
+            def _():
+                near_sum()
+
+            @pl.when(s == second)
+            def _():
+                far_sum()
+
+        def finish():
+            for d in range(chips):
+                beside(d).wait_send()
+                if d > 0:
+                    across(d).wait_send()
+
+        return peers, start, hook, finish
+
+    return (
+        [(whole_rows, False)],
+        [(shape(rows, width, dtype), True)],
+        [
+            VMEM((chips, rows, width), BF16),
+            VMEM((chips, rows, width), BF16),
+            VMEM((chips - 1, rows, width), BF16),
+        ]
+        + [dma((chips,))] * 5,
+        bind,
+    )
 
 
 def weight_kernel(starts, parts, *refs):
@@ -839,14 +1134,12 @@
     lo = jnp.sum((largest[None, :] < oldest[:, None]).astype(jnp.int32), axis=1)
     hi = jnp.sum((smallest[None, :] <= newest[:, None]).astype(jnp.int32), axis=1)
     keys = grouped.transpose(1, 0, 2).reshape(blocks, n_ctx * SUB)
-    pk_col = jnp.broadcast_to(keys[:, :, None], (blocks, n_ctx * SUB, 8))
     marks = (
         lo,
         hi,
         keys[:, None, :],
         packed[:, None],
         first[:, None],
-        pk_col,
         packed[None, :],
         first[None, :],
     )
@@ -887,95 +1180,133 @@
         pieces += [w_key[:, at], w_value[:, at]]
     qkv_w, out_w = gather_ctx([jnp.concatenate(pieces, axis=1), w_out.T], n_ctx, 0)
     mlp_own = jnp.concatenate([w_gate, w_up, w_down.T], axis=1)
-    mlp_own, qkv_w = lax.optimization_barrier((mlp_own, qkv_w))
-    mlp_w = lax.all_gather(mlp_own, "ctx", axis=0, tiled=True)
-
     orders = [layout(seq_lengths[b], token_order[b], rank, n_ctx, head) for b in range(micro_count)]
     inputs = hidden_in.astype(F32)
     inverse = lax.rsqrt(jnp.mean(inputs * inputs, axis=-1, keepdims=True) + EPSILON)
     normed = (inputs * inverse * attn_gain).astype(BF16)
-    sorted_normed = [nn(orders[b][1], normed[b]).astype(BF16) for b in range(micro_count)]
-
-    projected = []
-    for b in range(micro_count):
-        q, kv, raw = project_qkv(
+    both = range(micro_count)
+    last = micro_count - 1
+    sorted_normed = [nn(orders[b][1], normed[b]).astype(BF16) for b in both]
+    projected = [
+        project_qkv(
             sorted_normed[b], qkv_w, orders[b][2], orders[b][3], q_gain, k_gain, heads, kv_heads
         )
-        (kv_all,) = gather_ctx([kv], n_ctx, 1)
-        projected.append((q, kv_all.reshape(n_ctx, rows, -1), raw))
-
-    state = []
-    for b in range(micro_count):
-        q, kv_all, raw = projected[b]
-        mixed_full, mass = attend_forward(q, kv_all, orders[b][4], head, kv_heads)
-        mixed, middle, normed_two = attn_out(
-            mixed_full, orders[b][0], out_w, hidden_in[b], m_gain, n_tp, 2
+        for b in both
+    ]
+    kv_own = after([p[1] for p in projected], projected[last][0])
+    (kv_first,) = gather_ctx([kv_own[0]], n_ctx, 1)
+    kv_all = [kv_first.reshape(n_ctx, rows, -1)]
+    mlp_w = lax.all_gather(after(mlp_own, kv_first), "ctx", axis=0, tiled=True)
+
+    def forward(b):
+        return attend_forward(projected[b][0], kv_all[b], orders[b][4], head, kv_heads)
+
+    def out_line(b):
+        return attn_out_line(attended[b][0], orders[b][0], out_w, hidden_in[b], m_gain)
+
+    def middle_line(b):
+        return middle_back_line(fed[b][4], cotangent[b], middles[b][1], m_gain, out_w)
+
+    def feed(b):
+        return mlp_job(middles[b][1], middles[b][2], cotangent[b], mlp_w, n_tp)
+
+    attended, middles, fed, mids, backs = [], [], [], [], []
+    attended.append(forward(0))
+    results = run_jobs(n_tp, out_line(0), [gather_job(kv_own[1], n_ctx)], 2, 40, "attn_out_gather")
+    middles.append(results[:3])
+    kv_all.append(results[3].reshape(n_ctx, rows, -1))
+    attended.append(forward(1))
+    results = run_jobs(n_tp, out_line(1), [feed(0)], 3, 60, "attn_out_mlp")
+    middles.append(results[:3])
+    fed.append(results[3:])
+    results = run_jobs(n_tp, middle_line(0), [feed(1)], 4, 60, "middle_back_mlp")
+    mids.append(results[:3])
+    fed.append(results[3:])
+
+    layer_out = jnp.stack(lax.psum([fed[b][3] for b in both], "tp"))
+
+    def backward(b, grad):
+        q, unused, raw = projected[b]
+        to_slot, to_sorted, cosine, sine, marks = orders[b]
+        g_mixed = nn(to_sorted, grad).astype(BF16)
+        mixed_full, mass = attended[b]
+        return attend_backward(
+            q, kv_all[b], marks, g_mixed, mixed_full, mass, raw, cosine, sine, q_gain, head, kv_heads
         )
-        state.append((mixed_full, mass, mixed, middle, normed_two))
-
-    fed = []
-    for b in range(micro_count):
-        mixed_full, mass, mixed, middle, normed_two = state[b]
-        hidden, g_gate, g_up, down, g_n2 = mlp(middle, normed_two, cotangent[b], mlp_w, n_tp)
-        g_mid, g_mixed, d_mlp_gain = middle_back(
-            g_n2, cotangent[b], middle, m_gain, out_w, n_tp, 3
+
+    backs.append(backward(0, mids[0][1]))
+    tile = 512 if units % 512 == 0 else 256
+    line = middle_line(1)
+    line[0][0] = (after(line[0][0][0], backs[0][0]), True)
+    results = run_jobs(
+        n_tp,
+        line,
+        [
+            weight_job(
+                [middles[b][2] for b in both] + [cotangent[b] for b in both],
+                [
+                    (tuple(both), [fed[b][1] for b in both]),
+                    (tuple(both), [fed[b][2] for b in both]),
+                    (tuple(micro_count + b for b in both), [fed[b][0] for b in both]),
+                ],
+                tile,
+                2,
+                mlp_w,
+            ),
+            scatter_job(backs[0][1].reshape(n_ctx * rows, -1), n_ctx, BF16, 4, 16),
+        ],
+        5,
+        60,
+        "middle_back_weights",
+        {5 + 5 * micro_count: 3},
+    )
+    mids.append(results[:3])
+    mlp_grads = lax.psum_scatter(results[3], "ctx", scatter_dimension=0, tiled=True)
+    dkv_first = results[4]
+    backs.append(backward(1, mids[1][1]))
+
+    def key_part(b, dkv):
+        return key_back(dkv, projected[b][2], orders[b][2], orders[b][3], k_gain, kv_heads)
+
+    def in_line(b, gkv):
+        return input_back_line(
+            backs[b][0], gkv, orders[b][0], qkv_w, hidden_in[b], mids[b][0], a_gain
         )
-        fed.append((hidden, g_gate, g_up, down, g_mid, g_mixed, d_mlp_gain))
-
-    both = range(micro_count)
-    tile = 512 if units % 512 == 0 else 256
-    mlp_grads = weight_grads(
-        [state[b][4] for b in both] + [cotangent[b] for b in both],
+
+    gkv_first, dk_gain_first = key_part(0, after(dkv_first, backs[1][0]))
+    results = run_jobs(
+        n_tp,
+        in_line(0, gkv_first),
+        [scatter_job(backs[1][1].reshape(n_ctx * rows, -1), n_ctx, BF16, 4, 16)],
+        6,
+        60,
+        "input_back_keys",
+    )
+    grad_in_first, da_gain_first, dkv_last = results
+    gkv_last, dk_gain_last = key_part(1, dkv_last)
+    tile = min(512, 2 * kv_heads * head, queries)
+    gkvs = [gkv_first, gkv_last]
+    attn_grads = weight_grads(
+        [sorted_normed[b] for b in both] + [mids[b][0] for b in both],
         [
-            (tuple(both), [fed[b][1] for b in both]),
-            (tuple(both), [fed[b][2] for b in both]),
-            (tuple(micro_count + b for b in both), [fed[b][0] for b in both]),
+            (tuple(both), [backs[b][0] for b in both]),
+            (tuple(both), [gkvs[b] for b in both]),
+            (tuple(micro_count + b for b in both), [middles[b][0] for b in both]),
         ],
         tile,
     )
-    mlp_grads = lax.psum_scatter(mlp_grads, "ctx", scatter_dimension=0, tiled=True)
-
-    downs = jnp.stack([fed[b][3] for b in both])
-    downs, last = lax.optimization_barrier((downs, fed[-1][5]))
-    fed[-1] = fed[-1][:5] + (last,) + fed[-1][6:]
-    layer_out = lax.psum(downs, "tp")
-
-    attended = []
-    for b in both:
-        q, kv_all, raw = projected[b]
-        to_slot, to_sorted, cosine, sine, marks = orders[b]
-        g_mixed = nn(to_sorted, fed[b][5]).astype(BF16)
-        dq, dkv, d_query_gain = attend_backward(
-            q, kv_all, marks, g_mixed, state[b][0], state[b][1], raw, cosine, sine, q_gain, head, kv_heads
-        )
-        dkv = lax.psum_scatter(
-            dkv.reshape(n_ctx * rows, -1), "ctx", scatter_dimension=0, tiled=True
-        )
-        attended.append((dq, dkv, d_query_gain))
-
-    grads_in, d_attn_gain, kv_low, d_key_gain = [], [], [], []
-    for b in both:
-        to_slot, to_sorted, cosine, sine, marks = orders[b]
-        gkv, dk_gain = key_back(attended[b][1], projected[b][2], cosine, sine, k_gain, kv_heads)
-        kv_low.append(gkv)
-        d_key_gain.append(dk_gain)
-        grad_in, da_gain = input_back(
-            attended[b][0], gkv, to_slot, qkv_w, hidden_in[b], fed[b][4], a_gain, n_tp, 4
-        )
-        grads_in.append(grad_in)
-        d_attn_gain.append(da_gain)
-
-    tile = min(512, 2 * kv_heads * head, queries)
-    attn_grads = weight_grads(
-        [sorted_normed[b] for b in both] + [fed[b][4] for b in both],
-        [
-            (tuple(both), [attended[b][0] for b in both]),
-            (tuple(both), [kv_low[b] for b in both]),
-            (tuple(micro_count + b for b in both), [state[b][2] for b in both]),
-        ],
-        tile,
-    )
-    attn_grads = lax.psum_scatter(attn_grads, "ctx", scatter_dimension=0, tiled=True).astype(F32)
+    results = run_jobs(
+        n_tp,
+        in_line(1, gkv_last),
+        [scatter_job(attn_grads, n_ctx, F32, 5, 20)],
+        7,
+        60,
+        "input_back_weights",
+    )
+    grad_in_last, da_gain_last, attn_grads = results
+    grads_in = [grad_in_first, grad_in_last]
+    d_attn_gain = [da_gain_first, da_gain_last]
+    d_key_gain = [dk_gain_first, dk_gain_last]
 
     share = width // n_ctx // 128
     own = lambda gain: sum(gain).reshape(n_ctx, share, 128)
@@ -986,9 +1317,9 @@
         jnp.concatenate(
             [
                 own(d_attn_gain),
-                own([fed[b][6] for b in both]),
+                own([mids[b][2] for b in both]),
                 blank,
-                spread([attended[b][2] for b in both]),
+                spread([backs[b][2] for b in both]),
                 spread(d_key_gain),
                 low_blank,
             ],
@@ -996,7 +1327,7 @@
         ),
         n_ctx,
         n_tp,
-        5,
+        8,
     )
 
     mlp_grads = mlp_grads.astype(F32)

time: 1050 us -> 768 us (0.73)
  waiting for transfers between devices: 208 us -> 0.05 us
  Pallas kernels: 720 us -> 663 us
  local copies, waits for them, and re-layouts: 56.7 us -> 42.8 us
    psum x1, waiting for transfers between devices: 149 us -> 0.01 us  [on_device(): layer_out = jnp.stack(lax.psum([fed[b][3] for b in both], 'tp'))]
    pallas_call x3 -> x2, Pallas kernels: 120 us -> 55.8 us  [gather_ctx(): pl.pallas_call(functools.partial(gather_kernel, count, n_ctx), out_shape=...]
    reduce_scatter x4 -> x1, waiting for transfers between devices: 59.3 us -> 0.01 us  [on_device(): lax.psum_scatter(results[3], 'ctx', scatter_dimension=0, tiled=True)]
    pallas_call x2 -> x1, Pallas kernels: 41.5 us -> 13.3 us  [weight_grads(): pl.pallas_call(functools.partial(weight_kernel, starts, len(lefts)), grid...]
    pallas_call x8 -> x6, Pallas kernels: 454 us -> 478 us  [run_jobs(): pl.pallas_call(kernel, out_shape=[out[0] for part in parts for out in par...]
    unnamed x135 -> x156, local copies, waits for them, and re-layouts: 40.4 us -> 25.4 us
    pallas_call x2, Pallas kernels: 56.9 us -> 68.8 us  [attend_backward(): pl.pallas_call(functools.partial(backward_kernel, head), grid_spec=pltpu....]
  transfers between devices with their start and end apart: 6 -> 3, of which waited for: 3 -> 0; matrix products, arithmetic and copies ran while one was open for 5% -> 4% of each run, Pallas kernels for 52% -> 61%
where the time goes in v2:
time: 768 us; the launch traced here: 762 us
  Pallas kernels  663 us (86%)
  local copies, waits for them, and re-layouts  42.8 us (6%)
  other arithmetic  34.7 us (5%)
  between operations  15.4 us (2%)
    pallas_call x6, Pallas kernels, run_jobs(): pl.pallas_call(kernel, out_shape=[out[0] for part in parts for out in par...  478 us
    pallas_call x2, Pallas kernels, attend_backward(): pl.pallas_call(functools.partial(backward_kernel, head), grid_spec=pltpu....  68.8 us
    pallas_call x2, Pallas kernels, gather_ctx(): pl.pallas_call(functools.partial(gather_kernel, count, n_ctx), out_shape=...  55.8 us
    pallas_call x2, Pallas kernels, attend_forward(): pl.pallas_call(functools.partial(forward_kernel, head), grid_spec=pltpu.P...  32 us
    unnamed x156, local copies, waits for them, and re-layouts  25.4 us
  transfers between devices with their start and end apart: 3, of which 0 were waited for; matrix products, arithmetic and copies ran while one was open for 4% of the time, Pallas kernels for 61%

profile of v2, /device:TPU:0, one launch (start us, length us, event | category | flops | bytes accessed | tf_op | source)
XLA Modules:
  0.0 762.1 jit_solution(18036050448674305643)
XLA Ops:
  8.2 1.4 convert_reduce_fusion
  9.5 1.5 select_reduce_fusion
  11.0 1.4 convert_reduce_fusion.1
  12.4 1.5 select_reduce_fusion.1
  16.0 2.7 fusion.10
  18.9 3.2 fusion
  22.7 3.3 fusion.2
  26.0 1.3 convolution_convert_fusion.x_ref.refs_0_
  27.3 1.3 convolution_convert_fusion.1.x_ref.refs_1_
  28.8 32.9 %gather_ctx.2 = (bf16[2048,1024]{1,0:T(8,128)(2,1)S(1)}, bf16[2048,512]{1,0:T(8,128)(2,1)S(1)}) custom-call(bf16[256,1024]{1,0:T(8,128)(2,1)S(1)} %slice_dynamic-update-slice_fusion.refs_0_, bf16[256,512]{1,0:T(8,128)(2,1)S(1)} %bitcast.77), custom_call_target="tpu_custom_call" | custom-call | tf_op jit(solution)/shard_map/gather_ctx/pallas_call | solution.py:170
  61.9 3.0 project_qkv.3
  65.0 1.1 copy-done.12
  66.1 3.0 project_qkv.2
  69.1 1.1 copy-done.10
  71.8 22.9 %gather_ctx.3 = bf16[4096,512]{1,0:T(8,128)(2,1)S(1)} custom-call(bf16[512,512]{1,0:T(8,128)(2,1)S(1)} %get-tuple-element.76.refs_0_), custom_call_target="tpu_custom_call" | custom-call | tf_op jit(solution)/shard_map/gather_ctx/pallas_call | solution.py:170
  94.7 2.0 copy-done.1
  96.7 1.4 copy.62
  98.1 2.9 pad_maximum_fusion.1
  104.9 2.2 copy-done.2
  107.1 16.0 %attend_forward.2 = (f32[512,512]{1,0:T(8,128)S(1)}, f32[8,1,256]{2,1,0:T(1,128)S(1)}) custom-call(s32[4]{0:T(128)S(1)} %convert_reduce_fusion.3.lo_ref, s32[4]{0:T(128)S(1)} %convert_reduce_fusion.2.hi_ref, bf16[512,512]{1,0:T(8,128)(2,1)S(1)} %get-tuple-element.73.q_ref, bf16[8,512,512]{2,1,0:T(8,128)(2,1)S(1)} %bitcast.74, ...), custom_call_target="tpu_custom_call" | custom-call | tf_op jit(solution)/shard_map/attend_forward/pallas_call | solution.py:277
  123.9 4.8 slice_bitcast_fusion.4
  128.8 66.5 %attn_out_gather.1 = (bf16[512,512]{1,0:T(8,128)(2,1)S(1)}, bf16[512,2048]{1,0:T(8,128)(2,1)S(1)}, bf16[512,2048]{1,0:T(8,128)(2,1)S(1)}, bf16[4096,512]{1,0:T(8,128)(2,1)}) custom-call(f32[512,512]{1,0:T(8,128)S(1)} %get-tuple-element.77.refs_0_.out_ref, bf16[512,512]{1,0:T(8,128)(2,1)S(1)} %fusion.3.refs_1_.refs_2_, ...), custom_call_target="tpu_custom_call" | custom-call | tf_op jit(solution)/shard_map/attn_out_gather/pallas_call | solution.py:488
  195.3 1.3 copy-done.6
  198.2 2.5 copy-done.5
  200.7 16.0 %attend_forward.3 = (f32[512,512]{1,0:T(8,128)S(1)}, f32[8,1,256]{2,1,0:T(1,128)S(1)}) custom-call(s32[4]{0:T(128)S(1)} %get-tuple-element.219.lo_ref, s32[4]{0:T(128)S(1)} %get-tuple-element.218.hi_ref, bf16[512,512]{1,0:T(8,128)(2,1)S(1)} %copy-done.26, bf16[8,512,512]{2,1,0:T(8,128)(2,1)S(1)} %bitcast.76, ...), custom_call_target="tpu_custom_call" | custom-call | tf_op jit(solution)/shard_map/attend_forward/pallas_call | solution.py:277
  216.7 1.0 copy-done.15
  219.2 69.1 %attn_out_mlp.1 = (bf16[512,512]{1,0:T(8,128)(2,1)}, bf16[512,2048]{1,0:T(8,128)(2,1)}, bf16[512,2048]{1,0:T(8,128)(2,1)}, bf16[512,1536]{1,0:T(8,128)(2,1)}, bf...) custom-call(f32[512,512]{1,0:T(8,128)} %copy-done.15, ...), custom_call_target="tpu_custom_call" | custom-call | tf_op jit(solution)/shard_map/attn_out_mlp/pallas_call | solution.py:488
  288.3 68.3 %middle_back_mlp.1 = (bf16[512,2048]{1,0:T(8,128)(2,1)}, bf16[512,512]{1,0:T(8,128)(2,1)}, f32[1,2048]{1,0:T(1,128)}, bf16[512,1536]{1,0:T(8,128)(2,1)}, bf16[51...) custom-call(bf16[512,2048]{1,0:T(8,128)(2,1)} %get-tuple-element.86.refs_, ...), custom_call_target="tpu_custom_call" | custom-call | tf_op jit(solution)/shard_map/middle_back_mlp/pallas_call | solution.py:488
  357.7 1.3 convolution_convert_fusion.3.g_ref
  359.0 34.5 %attend_backward.2 = (bf16[512,512]{1,0:T(8,128)(2,1)}, bf16[8,512,512]{2,1,0:T(8,128)(2,1)}, f32[1,128]{1,0:T(1,128)}) custom-call(s32[4]{0:T(128)} %copy-done.45, s32[4]{0:T(128)} %copy-done.46, bf16[512,512]{1,0:T(8,128)(2,1)} %copy-done.27, bf16[8,512,512]{2,1,0:T(8,128)(2,1)} %bitcast.73, s32[8,1,512]{2,1,0:T(1,128)} %copy-done.37, ...), custom_call_target="tpu_custom_call" | custom-call | tf_op jit(solution)/shard_map/attend_backward/pallas_call | solution.py:395
  393.5 124.1 %middle_back_weights.1 = (bf16[512,2048]{1,0:T(8,128)(2,1)}, bf16[512,512]{1,0:T(8,128)(2,1)}, f32[1,2048]{1,0:T(1,128)}, bf16[2048,4608]{1,0:T(8,128)(2,1)}, bf16[512,512]{1,0:T(8,128)(2,1)}) custom-call(bf16[512,2048]{1,0:T(8,128)(2,1)} %get-tuple-element.95.refs_0_, ...), custom_call_target="tpu_custom_call", output_to_operand_aliasing={{3}: (15, {})} | custom-call | tf_op jit(solution)/shard_map/middle_back_weights/pallas_call | solution.py:488
  517.6 1.0 copy-done.70
  518.6 1.2 convolution_convert_fusion.2.g_ref
  519.9 34.3 %attend_backward.3 = (bf16[512,512]{1,0:T(8,128)(2,1)}, bf16[8,512,512]{2,1,0:T(8,128)(2,1)}, f32[1,128]{1,0:T(1,128)}) custom-call(s32[4]{0:T(128)} %copy-done.44, s32[4]{0:T(128)} %copy-done.43, bf16[512,512]{1,0:T(8,128)(2,1)} %copy-done.25, bf16[8,512,512]{2,1,0:T(8,128)(2,1)} %bitcast.75, s32[8,1,512]{2,1,0:T(1,128)} %copy-done.36, ...), custom_call_target="tpu_custom_call" | custom-call | tf_op jit(solution)/shard_map/attend_backward/pallas_call | solution.py:395
  555.6 68.6 %input_back_keys.1 = (bf16[512,2048]{1,0:T(8,128)(2,1)}, f32[1,2048]{1,0:T(1,128)}, bf16[512,512]{1,0:T(8,128)(2,1)}) custom-call(bf16[512,512]{1,0:T(8,128)(2,1)} %get-tuple-element.93.refs_0_.refs_4_, bf16[512,512]{1,0:T(8,128)(2,1)} %copy-done.28, bf16[512,512]{1,0:T(8,128)(2,1)} %copy-done.14, bf16[2048,1024]{1,0:T(8,128)(2,1)} %copy-done, ...), custom_call_target="tpu_custom_call" | custom-call | tf_op jit(solution)/shard_map/input_back_keys/pallas_call | solution.py:488
  624.3 1.0 copy-done.35
  626.7 13.3 %weight_grads.1.refs_7_ = bf16[2048,1536]{1,0:T(8,128)(2,1)} custom-call(bf16[512,2048]{1,0:T(8,128)(2,1)} %copy-done.8, bf16[512,2048]{1,0:T(8,128)(2,1)} %copy-done.9, bf16[512,2048]{1,0:T(8,128)(2,1)} %get-tuple-element.110.refs_5_.refs_2_, bf16[512,2048]{1,0:T(8,128)(2,1)} %get-tuple-element.115.refs_3_.refs_5_, ...), custom_call_target="tpu_custom_call" | custom-call | tf_op jit(solution)/shard_map/weight_grads/pallas_call | solution.py:1023
  640.0 81.1 %input_back_weights.1 = (bf16[512,2048]{1,0:T(8,128)(2,1)}, f32[1,2048]{1,0:T(1,128)}, f32[256,1536]{1,0:T(8,128)}) custom-call(bf16[512,512]{1,0:T(8,128)(2,1)} %get-tuple-element.107.refs_5_.refs_0_, bf16[512,512]{1,0:T(8,128)(2,1)} %copy-done.29, bf16[512,512]{1,0:T(8,128)(2,1)} %fusion.4.refs_1_.refs_2_, bf16[2048,1024]{1,0:T(8,128)(2,1)} %copy-done, ...), custom_call_target="tpu_custom_call" | custom-call | tf_op jit(solution)/shard_map/input_back_weights/pallas_call | solution.py:488
  722.1 8.7 %sum_gains.1 = f32[8,128]{1,0:T(8,128)S(1)} custom-call(f32[8,8,128]{2,1,0:T(8,128)S(1)} %concatenate.33.x_ref), custom_call_target="tpu_custom_call" | custom-call | tf_op jit(solution)/shard_map/sum_gains/pallas_call | solution.py:1084
  730.8 2.2 slice_bitcast_fusion.9
  733.0 1.0 copy.63
  734.0 1.3 fusion.12
  737.8 3.9 maximum_convert_fusion
  741.8 4.6 pad_maximum_fusion
  746.4 2.2 convert_element_type.81
  748.6 1.3 slice_bitcast_fusion.8
  749.9 3.2 copy.64
  753.0 2.1 fusion.11
  (210 shorter events, 20.2 us)
Async XLA Ops:
  7.2 212.0 %all-gather.2.cloned.1.call-start = ((), (), s32[]{:S(2)}) async-start(), calls=%async_computation.1 | async-start | bytes 21233664 | tf_op jit(solution)/shard_map/all_gather | solution.py:1199
  13.9 13.4 %copy-start.65 = (s32[1,512]{1,0:T(1,128)}, s32[1,512]{1,0:T(1,128)S(1)}, u32[]{:S(2)}) copy-start(s32[1,512]{1,0:T(1,128)S(1)} %constant_dynamic-slice_fusion.2) | copy-start | bytes 6148
  13.9 12.1 %copy-start.63 = (s32[1,512]{1,0:T(1,128)}, s32[1,512]{1,0:T(1,128)S(1)}, u32[]{:S(2)}) copy-start(s32[1,512]{1,0:T(1,128)S(1)} %get-tuple-element.220) | copy-start | bytes 6148
  13.9 90.2 %copy-start.57 = (s32[1,512]{1,0:T(1,128)}, s32[1,512]{1,0:T(1,128)S(1)}, u32[]{:S(2)}) copy-start(s32[1,512]{1,0:T(1,128)S(1)} %get-tuple-element.221.pq_ref) | copy-start | bytes 6148
  15.9 85.9 %copy-start.60 = (s32[512]{0:T(512)}, s32[512]{0:T(512)S(1)}, u32[]{:S(2)}) copy-start(s32[512]{0:T(512)S(1)} %select_reduce_fusion.2) | copy-start | bytes 6148
  15.9 6.3 copy-start.61
  16.0 86.2 %copy-start.58 = (s32[512]{0:T(512)}, s32[512]{0:T(512)S(1)}, u32[]{:S(2)}) copy-start(s32[512]{0:T(512)S(1)} %select_reduce_fusion.3) | copy-start | bytes 6148
  18.9 43.0 %copy-start.21 = (f32[512,128]{1,0:T(8,128)}, f32[512,128]{1,0:T(8,128)S(1)}, u32[]{:S(2)}) copy-start(f32[512,128]{1,0:T(8,128)S(1)} %pad_maximum_fusion.4.cos_ref) | copy-start | bytes 786436
  22.7 42.2 %copy-start.23 = (f32[512,128]{1,0:T(8,128)}, f32[512,128]{1,0:T(8,128)S(1)}, u32[]{:S(2)}) copy-start(f32[512,128]{1,0:T(8,128)S(1)} %pad_maximum_fusion.2.cos_ref) | copy-start | bytes 786436
  27.3 34.6 %copy-start.8 = (bf16[512,2048]{1,0:T(8,128)(2,1)}, bf16[512,2048]{1,0:T(8,128)(2,1)S(1)}, u32[]{:S(2)}) copy-start(bf16[512,2048]{1,0:T(8,128)(2,1)S(1)} %convolution_convert_fusion.x_ref.refs_0_) | copy-start | bytes 6291460
  27.3 34.4 %copy-start.51 = (f32[512,64]{1,0:T(8,128)S(1)}, f32[512,64]{1,0:T(8,128)}, u32[]{:S(2)}) copy-start(f32[512,64]{1,0:T(8,128)} %get-tuple-element.217) | copy-start | bytes 393220
  28.6 36.3 %copy-start.9 = (bf16[512,2048]{1,0:T(8,128)(2,1)}, bf16[512,2048]{1,0:T(8,128)(2,1)S(1)}, u32[]{:S(2)}) copy-start(bf16[512,2048]{1,0:T(8,128)(2,1)S(1)} %convolution_convert_fusion.1.x_ref.refs_1_) | copy-start | bytes 6291460
  28.6 33.3 %copy-start.41 = (f32[128]{0:T(128)S(1)}, f32[128]{0:T(128)}, u32[]{:S(2)}) copy-start(f32[128]{0:T(128)} %param.22) | copy-start | bytes 1540
  28.6 33.3 %copy-start.42 = (f32[128]{0:T(128)S(1)}, f32[128]{0:T(128)}, u32[]{:S(2)}) copy-start(f32[128]{0:T(128)} %param.23) | copy-start | bytes 1540
  28.8 36.2 %copy-start.19 = (f32[512,128]{1,0:T(8,128)}, f32[512,128]{1,0:T(8,128)S(1)}, u32[]{:S(2)}) copy-start(f32[512,128]{1,0:T(8,128)S(1)} %pad_maximum_fusion.5.sin_ref) | copy-start | bytes 786436
  61.7 67.0 %copy-start.3 = (bf16[2048,512]{1,0:T(8,128)(2,1)}, bf16[2048,512]{1,0:T(8,128)(2,1)S(1)}, u32[]{:S(2)}) copy-start(bf16[2048,512]{1,0:T(8,128)(2,1)S(1)} %get-tuple-element.78.refs_2_.refs_4_) | copy-start | bytes 6291460
  66.1 38.8 %copy-start.27 = (bf16[512,512]{1,0:T(8,128)(2,1)}, bf16[512,512]{1,0:T(8,128)(2,1)S(1)}, u32[]{:S(2)}) copy-start(bf16[512,512]{1,0:T(8,128)(2,1)S(1)} %get-tuple-element.73.q_ref) | copy-start | bytes 1572868
  101.1 640.7 %all-reduce.3.cloned.1.call-start = ((), (), s32[]{:S(2)}) async-start(), calls=%async_computation.3 | async-start | bytes 8388608 | tf_op jit(solution)/shard_map/psum | solution.py:1226
  102.2 20.9 %copy-start.37 = (s32[8,1,512]{2,1,0:T(1,128)}, s32[8,1,512]{2,1,0:T(1,128)S(1)}, u32[]{:S(2)}) copy-start(s32[8,1,512]{2,1,0:T(1,128)S(1)} %broadcast_in_dim_reshape.6.pk_ref) | copy-start | bytes 49156
  103.3 94.8 %copy-start.36 = (s32[8,1,512]{2,1,0:T(1,128)}, s32[8,1,512]{2,1,0:T(1,128)S(1)}, u32[]{:S(2)}) copy-start(s32[8,1,512]{2,1,0:T(1,128)S(1)} %broadcast_in_dim_reshape.7.pk_ref) | copy-start | bytes 49156
  104.7 18.4 %copy-start.45 = (s32[4]{0:T(128)}, s32[4]{0:T(128)S(1)}, u32[]{:S(2)}) copy-start(s32[4]{0:T(128)S(1)} %convert_reduce_fusion.3.lo_ref) | copy-start | bytes 52
  104.8 18.2 %copy-start.46 = (s32[4]{0:T(128)}, s32[4]{0:T(128)S(1)}, u32[]{:S(2)}) copy-start(s32[4]{0:T(128)S(1)} %convert_reduce_fusion.2.hi_ref) | copy-start | bytes 52
  107.0 16.6 %copy-start.64 = (s32[1,512]{1,0:T(1,128)S(1)}, s32[1,512]{1,0:T(1,128)}, u32[]{:S(2)}) copy-start(s32[1,512]{1,0:T(1,128)} %copy-done.63) | copy-start | bytes 6148
  107.1 16.8 %copy-start.47 = (bf16[2,512,2048]{2,1,0:T(8,128)(2,1)S(1)}, bf16[2,512,2048]{2,1,0:T(8,128)(2,1)}, u32[]{:S(2)}) copy-start(bf16[2,512,2048]{2,1,0:T(8,128)(2,1)} %param.15) | copy-start | bytes 12582916
  123.7 5.0 copy-start.16
  128.7 66.6 %copy-start.4 = (bf16[512,2048]{1,0:T(8,128)(2,1)}, bf16[512,2048]{1,0:T(8,128)(2,1)S(1)}, u32[]{:S(2)}) copy-start(bf16[512,2048]{1,0:T(8,128)(2,1)S(1)} %get-tuple-element.222.refs_3_.refs_4_) | copy-start | bytes 6291460
  128.7 68.7 %copy-start.59 = (s32[512]{0:T(512)S(1)}, s32[512]{0:T(512)}, u32[]{:S(2)}) copy-start(s32[512]{0:T(512)} %copy-done.58) | copy-start | bytes 6148
  128.7 68.8 %copy-start.62 = (s32[1,512]{1,0:T(1,128)S(1)}, s32[1,512]{1,0:T(1,128)}, u32[]{:S(2)}) copy-start(s32[1,512]{1,0:T(1,128)} %copy-done.61) | copy-start | bytes 6148
  128.8 69.4 %copy-start.26 = (bf16[512,512]{1,0:T(8,128)(2,1)S(1)}, bf16[512,512]{1,0:T(8,128)(2,1)}, u32[]{:S(2)}) copy-start(bf16[512,512]{1,0:T(8,128)(2,1)} %copy-done.25) | copy-start | bytes 1572868
  128.8 69.4 %copy-start.30 = (s32[512,1]{1,0:T(8,128)S(1)}, s32[512,1]{1,0:T(8,128)}, u32[]{:S(2)}) copy-start(s32[512,1]{1,0:T(8,128)} %copy.60.pq_ref) | copy-start | bytes 6148
  197.4 19.2 %copy-start.7 = (bf16[512,2048]{1,0:T(8,128)(2,1)}, bf16[512,2048]{1,0:T(8,128)(2,1)S(1)}, u32[]{:S(2)}) copy-start(bf16[512,2048]{1,0:T(8,128)(2,1)S(1)} %get-tuple-element.82.refs_5_.refs_2_) | copy-start | bytes 6291460
  198.1 18.5 %copy-start.43 = (s32[4]{0:T(128)}, s32[4]{0:T(128)S(1)}, u32[]{:S(2)}) copy-start(s32[4]{0:T(128)S(1)} %get-tuple-element.218.hi_ref) | copy-start | bytes 52
  198.1 18.5 %copy-start.44 = (s32[4]{0:T(128)}, s32[4]{0:T(128)S(1)}, u32[]{:S(2)}) copy-start(s32[4]{0:T(128)S(1)} %get-tuple-element.219.lo_ref) | copy-start | bytes 52
  200.7 17.6 %copy-start.66 = (s32[1,512]{1,0:T(1,128)S(1)}, s32[1,512]{1,0:T(1,128)}, u32[]{:S(2)}) copy-start(s32[1,512]{1,0:T(1,128)} %copy-done.65) | copy-start | bytes 6148
  356.7 389.7 %reduce-scatter.2.cloned.1.call-start = ((), (), s32[]{:S(2)}) async-start(), calls=%async_computation.2 | async-start | bytes 21233664 | tf_op jit(solution)/shard_map/reduce_scatter | solution.py:1264
  519.9 34.4 %copy-start.13 = (f32[512,768]{1,0:T(8,128)S(1)}, f32[512,768]{1,0:T(8,128)}, u32[]{:S(2)}) copy-start(f32[512,768]{1,0:T(8,128)} %copy-done.12) | copy-start | bytes 4718596
  519.9 34.4 %copy-start.20 = (f32[512,128]{1,0:T(8,128)S(1)}, f32[512,128]{1,0:T(8,128)}, u32[]{:S(2)}) copy-start(f32[512,128]{1,0:T(8,128)} %copy-done.19) | copy-start | bytes 786436
  519.9 34.4 %copy-start.22 = (f32[512,128]{1,0:T(8,128)S(1)}, f32[512,128]{1,0:T(8,128)}, u32[]{:S(2)}) copy-start(f32[512,128]{1,0:T(8,128)} %copy-done.21) | copy-start | bytes 786436
  519.9 34.4 %copy-start.34 = (bf16[512,512]{1,0:T(8,128)(2,1)S(1)}, bf16[512,512]{1,0:T(8,128)(2,1)}, u32[]{:S(2)}) copy-start(bf16[512,512]{1,0:T(8,128)(2,1)} %get-tuple-element.108.grad_ref) | copy-start | bytes 1572868
  555.6 68.6 %copy-start.11 = (f32[512,768]{1,0:T(8,128)S(1)}, f32[512,768]{1,0:T(8,128)}, u32[]{:S(2)}) copy-start(f32[512,768]{1,0:T(8,128)} %copy-done.10) | copy-start | bytes 4718596
  555.6 68.6 %copy-start.18 = (f32[512,128]{1,0:T(8,128)S(1)}, f32[512,128]{1,0:T(8,128)}, u32[]{:S(2)}) copy-start(f32[512,128]{1,0:T(8,128)} %copy-done.17) | copy-start | bytes 786436
  555.6 68.6 %copy-start.24 = (f32[512,128]{1,0:T(8,128)S(1)}, f32[512,128]{1,0:T(8,128)}, u32[]{:S(2)}) copy-start(f32[512,128]{1,0:T(8,128)} %copy-done.23) | copy-start | bytes 786436
  640.0 81.2 %copy-start.67 = (f32[1,2048]{1,0:T(1,128)S(1)}, f32[1,2048]{1,0:T(1,128)}, u32[]{:S(2)}) copy-start(f32[1,2048]{1,0:T(1,128)} %get-tuple-element.121) | copy-start | bytes 24580
  640.0 81.2 %copy-start.68 = (f32[1,2048]{1,0:T(1,128)S(1)}, f32[1,2048]{1,0:T(1,128)}, u32[]{:S(2)}) copy-start(f32[1,2048]{1,0:T(1,128)} %get-tuple-element.122) | copy-start | bytes 24580
  640.0 81.2 %copy-start.69 = (f32[1,2048]{1,0:T(1,128)S(1)}, f32[1,2048]{1,0:T(1,128)}, u32[]{:S(2)}) copy-start(f32[1,2048]{1,0:T(1,128)} %get-tuple-element.119) | copy-start | bytes 24580
  640.0 81.9 %copy-start.72 = (f32[1,128]{1,0:T(1,128)S(1)}, f32[1,128]{1,0:T(1,128)}, u32[]{:S(2)}) copy-start(f32[1,128]{1,0:T(1,128)} %get-tuple-element.123) | copy-start | bytes 1540
  640.0 81.9 %copy-start.73 = (f32[1,128]{1,0:T(1,128)S(1)}, f32[1,128]{1,0:T(1,128)}, u32[]{:S(2)}) copy-start(f32[1,128]{1,0:T(1,128)} %get-tuple-element.124) | copy-start | bytes 1540
  730.8 7.0 copy-start.49
  (29 other events, 64.9 us)
Sparse Core Ops, SparseCore 0:
  101.2 112.3 all-gather.1
  356.8 197.3 all-reduce.2
  558.3 160.8 reduce-scatter.1

commit v3 on v2

--- a/solution.py
+++ b/solution.py
@@ -17,9 +17,10 @@
 ANY = pl.ANY
 LOG2E = math.log2(math.e)
 SUB = 64
-QROWS = 128
+QROWS = 256
 CHUNKS = 16
 LAG = 2
+GROUP = 128
 
 
 def params(megabytes, collective=None):
@@ -241,59 +242,74 @@
     )
 
 
-def forward_kernel(head, lo_ref, hi_ref, q_ref, kv_ref, pk_ref, pq_ref, sq_ref, out_ref, mass_ref):
-    block = pl.program_id(1)
+def head_parts(block, head, kv_heads):
+    wide = block.shape[1] // kv_heads
+    return [heads_to_rows(block[:, n * wide : (n + 1) * wide], head) for n in range(kv_heads)]
+
+
+def keys_and_values(kv_ref, at, n, head):
     runs = kv_ref.shape[0]
+    take = lambda i: kv_ref[:, at, i * head : (i + 1) * head].reshape(runs * SUB, head)
+    return take(2 * n), take(2 * n + 1)
+
+
+def forward_kernel(head, kv_heads, lo_ref, hi_ref, q_ref, kv_ref, pk_ref, pq_ref, sq_ref, out_ref, mass_ref):
+    block = pl.program_id(0)
     rows = q_ref.shape[0]
-    group = q_ref.shape[1] // head
+    wide = q_ref.shape[1] // kv_heads
+    group = wide // head
     scale = head ** (-0.5) * LOG2E
-    query = heads_to_rows(q_ref[...], head)
-    newest = jnp.concatenate([pq_ref[...]] * group, axis=0)
-    oldest = jnp.concatenate([sq_ref[...]] * group, axis=0)
+    queries = head_parts(q_ref[...], head, kv_heads)
+    newest, oldest = pq_ref[...], sq_ref[...]
 
     def step(j, carry):
-        total, mass = carry
         at = pl.ds(pl.multiple_of(j * SUB, SUB), SUB)
-        keys = kv_ref[:, at, :head].reshape(runs * SUB, head)
-        values = kv_ref[:, at, head:].reshape(runs * SUB, head)
         packed = pk_ref[j]
         allowed = (packed <= newest) & (packed >= oldest)
-        probs = jnp.where(allowed, jnp.exp2(nt(query, keys) * scale), 0.0)
-        mass = mass + jnp.sum(probs, axis=1, keepdims=True)
-        return total + nn(probs.astype(BF16), values), mass
-
-    start = (jnp.zeros((group * rows, head), F32), jnp.zeros((group * rows, 1), F32))
-    total, mass = lax.fori_loop(lo_ref[block], hi_ref[block], step, start)
-    out_ref[...] = rows_to_heads(total / mass, rows)
-    mass_ref[0] = jnp.broadcast_to(jnp.log2(mass), (group * rows, 128)).T[0:1]
+        allowed = jnp.concatenate([allowed] * group, axis=0)
+        result = []
+        for n, (total, mass) in enumerate(carry):
+            keys, values = keys_and_values(kv_ref, at, n, head)
+            probs = jnp.where(allowed, jnp.exp2(nt(queries[n], keys) * scale), 0.0)
+            for i in range(probs.shape[1] // 128):
+                mass = mass + probs[:, i * 128 : (i + 1) * 128]
+            result.append((total + nn(probs.astype(BF16), values), mass))
+        return tuple(result)
+
+    zero = (jnp.zeros((group * rows, head), F32), jnp.zeros((group * rows, 128), F32))
+    results = lax.fori_loop(lo_ref[block], hi_ref[block], step, (zero,) * kv_heads)
+    for n, (total, mass) in enumerate(results):
+        mass = jnp.sum(mass, axis=1, keepdims=True)
+        out_ref[:, n * wide : (n + 1) * wide] = rows_to_heads(total / mass, rows)
+        mass_ref[0, n : n + 1] = jnp.broadcast_to(jnp.log2(mass), (group * rows, 128)).T[0:1]
 
 
 def attend_forward(query, kv, marks, head, kv_heads):
     lo, hi, pk_row, pq_col, sq_col = marks[:5]
     rows, width = query.shape
-    runs = kv.shape[0]
     group = width // (kv_heads * head)
     blocks = rows // QROWS
+    own = lambda i, *s: (i, 0)
     return pl.pallas_call(
-        functools.partial(forward_kernel, head),
+        functools.partial(forward_kernel, head, kv_heads),
         grid_spec=pltpu.PrefetchScalarGridSpec(
             num_scalar_prefetch=2,
-            grid=(kv_heads, blocks),
+            grid=(blocks,),
             in_specs=[
-                pl.BlockSpec((QROWS, group * head), lambda n, i, *s: (i, n)),
-                pl.BlockSpec((runs, rows, 2 * head), lambda n, i, *s: (0, 0, n)),
+                pl.BlockSpec((QROWS, width), own),
+                whole(kv.shape),
                 whole(pk_row.shape),
-                pl.BlockSpec((QROWS, 1), lambda n, i, *s: (i, 0)),
-                pl.BlockSpec((QROWS, 1), lambda n, i, *s: (i, 0)),
+                pl.BlockSpec((QROWS, 1), own),
+                pl.BlockSpec((QROWS, 1), own),
             ],
             out_specs=[
-                pl.BlockSpec((QROWS, group * head), lambda n, i, *s: (i, n)),
-                pl.BlockSpec((1, 1, group * QROWS), lambda n, i, *s: (n * blocks + i, 0, 0)),
+                pl.BlockSpec((QROWS, width), own),
+                pl.BlockSpec((1, kv_heads, group * QROWS), lambda i, *s: (i, 0, 0)),
             ],
         ),
         out_shape=[
             jax.ShapeDtypeStruct((rows, width), F32),
-            jax.ShapeDtypeStruct((kv_heads * blocks, 1, group * QROWS), F32),
+            jax.ShapeDtypeStruct((blocks, kv_heads, group * QROWS), F32),
         ],
         compiler_params=params(40),
         name="attend_forward",
@@ -311,6 +327,7 @@
 
 def backward_kernel(
     head,
+    kv_heads,
     lo_ref,
     hi_ref,
     q_ref,
@@ -328,95 +345,94 @@
     dq_ref,
     dkv_ref,
     dgain_ref,
-    dk_acc,
-    dv_acc,
+    acc,
 ):
-    n, block = pl.program_id(0), pl.program_id(1)
+    block = pl.program_id(0)
     runs = kv_ref.shape[0]
     rows = q_ref.shape[0]
-    group = q_ref.shape[1] // head
+    group = q_ref.shape[1] // (kv_heads * head)
     scale = head ** (-0.5)
-    query = heads_to_rows(q_ref[...], head)
-    grad = heads_to_rows(g_ref[...], head)
-    mixed = heads_to_rows(out_ref[...], head)
-    row_dot = jnp.sum(grad.astype(F32) * mixed, axis=1, keepdims=True)
-    row_dot = jnp.broadcast_to(row_dot, (group * rows, 128)).T[0:1]
-    mass = mass_ref[0]
-    newest = jnp.concatenate([pq_ref[...]] * group, axis=1)
-    oldest = jnp.concatenate([sq_ref[...]] * group, axis=1)
+    queries = head_parts(q_ref[...], head, kv_heads)
+    grads = head_parts(g_ref[...], head, kv_heads)
+    mixed = head_parts(out_ref[...], head, kv_heads)
+    dots = []
+    for grad, own in zip(grads, mixed):
+        dot = jnp.sum(grad.astype(F32) * own, axis=1, keepdims=True)
+        dots.append(jnp.broadcast_to(dot, (group * rows, 128)).T[0:1])
+    newest, oldest = pq_ref[0], sq_ref[0]
 
     @pl.when(block == 0)
     def _():
-        dk_acc[...] = jnp.zeros_like(dk_acc)
-        dv_acc[...] = jnp.zeros_like(dv_acc)
-
-    @pl.when((block == 0) & (n == 0))
-    def _():
+        acc[...] = jnp.zeros_like(acc)
         dgain_ref[...] = jnp.zeros_like(dgain_ref)
 
-    def step(j, dq):
+    def step(j, dqs):
         at = pl.ds(pl.multiple_of(j * SUB, SUB), SUB)
-        keys = kv_ref[:, at, :head].reshape(runs * SUB, head)
-        values = kv_ref[:, at, head:].reshape(runs * SUB, head)
         packed = jnp.broadcast_to(pk_ref[j], (8, pk_ref.shape[2])).T[:, :1]
         allowed = (packed <= newest) & (packed >= oldest)
-        probs = jnp.where(allowed, jnp.exp2(nt(keys, query) * (scale * LOG2E) - mass), 0.0)
-        dscores = (probs * (nt(values, grad) - row_dot)).astype(BF16)
-        dk_acc[:, at, :] += nn(dscores, query).reshape(runs, SUB, head)
-        dv_acc[:, at, :] += nn(probs.astype(BF16), grad).reshape(runs, SUB, head)
-        return dq + tn(dscores, keys)
-
-    dq = lax.fori_loop(
-        lo_ref[block], hi_ref[block], step, jnp.zeros((group * rows, head), F32)
-    )
-    dq = dq * scale
+        result = []
+        for n, dq in enumerate(dqs):
+            keys, values = keys_and_values(kv_ref, at, n, head)
+            scores = nt(keys, queries[n]) * (scale * LOG2E) - mass_ref[0, n : n + 1]
+            probs = jnp.where(allowed, jnp.exp2(scores), 0.0)
+            dscores = (probs * (nt(values, grads[n]) - dots[n])).astype(BF16)
+            key_cols = slice(2 * n * head, (2 * n + 1) * head)
+            value_cols = slice((2 * n + 1) * head, (2 * n + 2) * head)
+            acc[:, at, key_cols] += nn(dscores, queries[n]).reshape(runs, SUB, head)
+            acc[:, at, value_cols] += nn(probs.astype(BF16), grads[n]).reshape(runs, SUB, head)
+            result.append(dq + tn(dscores, keys))
+        return tuple(result)
+
+    zero = jnp.zeros((group * rows, head), F32)
+    dqs = lax.fori_loop(lo_ref[block], hi_ref[block], step, (zero,) * kv_heads)
     cosine, sine = cos_ref[...], sin_ref[...]
-    for g in range(group):
-        own = unturn(dq[g * rows : (g + 1) * rows], cosine, sine)
-        raw = raw_ref[:, g * head : (g + 1) * head]
-        inverse = lax.rsqrt(jnp.mean(raw * raw, axis=-1, keepdims=True) + EPSILON)
-        unit = raw * inverse
-        dgain_ref[...] += jnp.sum(own * unit, axis=0, keepdims=True)
-        dq_ref[:, g * head : (g + 1) * head] = back(own, unit, inverse, gain_ref[...]).astype(BF16)
-
-    @pl.when(block == pl.num_programs(1) - 1)
+    for n in range(kv_heads):
+        for g in range(group):
+            own = unturn(dqs[n][g * rows : (g + 1) * rows] * scale, cosine, sine)
+            cols = slice((n * group + g) * head, (n * group + g + 1) * head)
+            raw = raw_ref[:, cols]
+            inverse = lax.rsqrt(jnp.mean(raw * raw, axis=-1, keepdims=True) + EPSILON)
+            unit = raw * inverse
+            dgain_ref[...] += jnp.sum(own * unit, axis=0, keepdims=True)
+            dq_ref[:, cols] = back(own, unit, inverse, gain_ref[...]).astype(BF16)
+
+    @pl.when(block == pl.num_programs(0) - 1)
     def _():
-        dkv_ref[:, :, :head] = (dk_acc[...] * scale).astype(BF16)
-        dkv_ref[:, :, head:] = dv_acc[...].astype(BF16)
+        for n in range(kv_heads):
+            key_cols = slice(2 * n * head, (2 * n + 1) * head)
+            value_cols = slice((2 * n + 1) * head, (2 * n + 2) * head)
+            dkv_ref[:, :, key_cols] = (acc[:, :, key_cols] * scale).astype(BF16)
+            dkv_ref[:, :, value_cols] = acc[:, :, value_cols].astype(BF16)
 
 
 def attend_backward(query, kv, marks, grad, out, mass, raw, cosine, sine, gain, head, kv_heads):
     lo, hi, pk_row, unused, unused_too, pq_row, sq_row = marks
     rows, width = query.shape
-    runs = kv.shape[0]
     group = width // (kv_heads * head)
     blocks = rows // QROWS
-    own = lambda n, i, *s: (i, n)
+    own = lambda i, *s: (i, 0)
+    line = lambda i, *s: (i, 0, 0)
     return pl.pallas_call(
-        functools.partial(backward_kernel, head),
+        functools.partial(backward_kernel, head, kv_heads),
         grid_spec=pltpu.PrefetchScalarGridSpec(
             num_scalar_prefetch=2,
-            grid=(kv_heads, blocks),
+            grid=(blocks,),
             in_specs=[
-                pl.BlockSpec((QROWS, group * head), own),
-                pl.BlockSpec((runs, rows, 2 * head), lambda n, i, *s: (0, 0, n)),
+                pl.BlockSpec((QROWS, width), own),
+                whole(kv.shape),
                 whole(pk_row.shape),
-                pl.BlockSpec((1, QROWS), lambda n, i, *s: (0, i)),
-                pl.BlockSpec((1, QROWS), lambda n, i, *s: (0, i)),
-                pl.BlockSpec((QROWS, group * head), own),
-                pl.BlockSpec((QROWS, group * head), own),
-                pl.BlockSpec((1, 1, group * QROWS), lambda n, i, *s: (n * blocks + i, 0, 0)),
-                pl.BlockSpec((QROWS, group * head), own),
-                pl.BlockSpec((QROWS, head), lambda n, i, *s: (i, 0)),
-                pl.BlockSpec((QROWS, head), lambda n, i, *s: (i, 0)),
+                pl.BlockSpec((1, 1, group * QROWS), line),
+                pl.BlockSpec((1, 1, group * QROWS), line),
+                pl.BlockSpec((QROWS, width), own),
+                pl.BlockSpec((QROWS, width), own),
+                pl.BlockSpec((1, kv_heads, group * QROWS), line),
+                pl.BlockSpec((QROWS, width), own),
+                pl.BlockSpec((QROWS, head), own),
+                pl.BlockSpec((QROWS, head), own),
                 whole((1, head)),
             ],
-            out_specs=[
-                pl.BlockSpec((QROWS, group * head), own),
-                pl.BlockSpec((runs, rows, 2 * head), lambda n, i, *s: (0, 0, n)),
-                whole((1, head)),
-            ],
-            scratch_shapes=[VMEM((runs, rows, head), F32)] * 2,
+            out_specs=[pl.BlockSpec((QROWS, width), own), whole(kv.shape), whole((1, head))],
+            scratch_shapes=[VMEM(kv.shape, F32)],
         ),
         out_shape=[
             jax.ShapeDtypeStruct((rows, width), BF16),
@@ -458,48 +474,126 @@
     )(grad, raw, cosine, sine, gain)
 
 
+LOAD, SAVE = "load", "save"
+
+
+class One:
+    def __init__(self, array, index):
+        self.array, self.index = array, index
+        self.shape, self.dtype = array.shape[1:], array.dtype
+
+
+def source(item):
+    return item.array if isinstance(item, One) else item
+
+
+class Loaded:
+    def __init__(self, source, held, sem):
+        self.ref = held
+        self.copy = lambda: pltpu.make_async_copy(source, held, sem)
+
+    def start(self):
+        self.copy().start()
+
+    def wait(self):
+        self.copy().wait()
+
+
+class Saved:
+    def __init__(self, held, result, sems, axis):
+        self.ref, self.result, self.sems, self.axis = held, result, sems, axis
+        self.count = sems.shape[0]
+
+    def part(self, i):
+        size = self.ref.shape[self.axis] // self.count
+        at = pl.ds(pl.multiple_of(i * size, size), size)
+        return (at, slice(None)) if self.axis == 0 else (slice(None), at)
+
+    def copy(self, i):
+        at = self.part(i)
+        return pltpu.make_async_copy(self.ref.at[at], self.result.at[at], self.sems.at[i])
+
+    def save(self, i):
+        self.copy(i).start()
+
+    def finish(self):
+        def one(i, carry):
+            self.copy(i).wait()
+            return carry
+
+        lax.fori_loop(0, self.count, one, 0)
+
+
 def run_jobs(n_tp, line, jobs, collective, megabytes, name, alias=None):
     rows, width = line[2], line[3]
-    chunks = CHUNKS
     dma = pltpu.SemaphoreType.DMA
-    buffer = VMEM((chunks, rows // chunks, width), BF16)
-    line_scratch = [buffer] * 5 + [dma((2, chunks)), dma((2, chunks))]
+    line_scratch = [VMEM((rows, width), BF16)] * 5 + [dma((2, CHUNKS)), dma((2, CHUNKS))]
     parts = [(line[0], line[1], line_scratch)] + [job[:3] for job in jobs]
-    space = lambda inside: pl.BlockSpec(memory_space=VMEM if inside else ANY)
-    n_ins = [len(part[0]) for part in parts]
-    n_outs = [len(part[1]) for part in parts]
-    n_scratch = [len(part[2]) for part in parts]
+    arrays = [source(array) for part in parts for array, unused in part[0]]
+    spec = lambda how: pl.BlockSpec(memory_space=VMEM if how is VMEM else ANY)
+    scratch_shapes, plan = [], []
+    for ins, outs, scratch in parts:
+        at = len(scratch_shapes)
+        scratch_shapes += scratch
+        plan.append([range(at, len(scratch_shapes)), {}, {}])
+        for i, (array, how) in enumerate(ins):
+            if how is LOAD:
+                plan[-1][1][i] = len(scratch_shapes)
+                scratch_shapes += [VMEM(array.shape[-2:], array.dtype), dma]
+        for i, (out, how) in enumerate(outs):
+            if isinstance(how, tuple):
+                plan[-1][2][i] = len(scratch_shapes)
+                scratch_shapes += [VMEM(out.shape, out.dtype), dma((how[1],))]
+    n_ins = sum(len(part[0]) for part in parts)
+    n_outs = sum(len(part[1]) for part in parts)
 
     def kernel(*refs):
-        def split(at, counts):
-            groups = []
-            for count in counts:
-                groups.append(refs[at : at + count])
-                at += count
-            return groups
-
-        ins = split(0, n_ins)
-        outs = split(sum(n_ins), n_outs)
-        scratch = split(sum(n_ins) + sum(n_outs), n_scratch)
-        bound = [job[3](ins[i + 1], outs[i + 1], scratch[i + 1]) for i, job in enumerate(jobs)]
-        produce, consume = line[4](ins[0], outs[0])
-        line_sum(n_tp, scratch[0], produce, consume, bound)
+        ins, outs, scratch = refs[:n_ins], refs[n_ins : n_ins + n_outs], refs[n_ins + n_outs :]
+        groups, loads, saves = [], [], []
+        in_at = out_at = 0
+        for (own_ins, own_outs, unused), (own_scratch, loaded, saved) in zip(parts, plan):
+            in_refs = list(ins[in_at : in_at + len(own_ins)])
+            out_refs = list(outs[out_at : out_at + len(own_outs)])
+            in_at += len(own_ins)
+            out_at += len(own_outs)
+            for i, k in loaded.items():
+                which = own_ins[i][0]
+                at = in_refs[i].at[which.index] if isinstance(which, One) else in_refs[i]
+                in_refs[i] = Loaded(at, scratch[k], scratch[k + 1])
+                loads.append(in_refs[i])
+            for i, k in saved.items():
+                out_refs[i] = Saved(scratch[k], out_refs[i], scratch[k + 1], own_outs[i][1][2])
+                saves.append(out_refs[i])
+            groups.append((in_refs, out_refs, [scratch[k] for k in own_scratch]))
+        for item in loads:
+            item.start()
+        bound = [job[3](*groups[i + 1]) for i, job in enumerate(jobs)]
+        line_sum(n_tp, groups[0][2], line[4](*groups[0][:2]), bound)
+        for item in saves:
+            item.finish()
 
     return pl.pallas_call(
         kernel,
         out_shape=[out[0] for part in parts for out in part[1]],
-        in_specs=[space(inside) for part in parts for unused, inside in part[0]],
-        out_specs=[space(inside) for part in parts for unused, inside in part[1]],
-        scratch_shapes=[item for part in parts for item in part[2]],
+        in_specs=[spec(how) for part in parts for unused, how in part[0]],
+        out_specs=[spec(how) for part in parts for unused, how in part[1]],
+        scratch_shapes=scratch_shapes,
         input_output_aliases=alias or {},
         compiler_params=params(megabytes, collective),
         name=name,
-    )(*[array for part in parts for array, unused in part[0]])
-
-
-def line_sum(n_tp, scratch, produce, consume, jobs):
+    )(*arrays)
+
+
+def piece(c, rows):
+    return pl.ds(pl.multiple_of(c * rows, rows), rows)
+
+
+def line_sum(n_tp, scratch, main, jobs):
     part, from_left, from_right, to_right, to_left, send_sem, recv_sem = scratch
-    chunks = part.shape[0]
+    produce_ready, consume_ready, produce, consume = main
+    chunks = CHUNKS
+    size = part.shape[0] // chunks
+    groups = part.shape[0] // GROUP
     place = lax.axis_index("tp")
     line = lax.axis_index("ctx")
     has_left, has_right = place > 0, place < n_tp - 1
@@ -516,6 +610,12 @@
     def _():
         pl.semaphore_signal(barrier, inc=1, device_id=(line, place + 1), device_id_type=MESH)
 
+    def fill(g):
+        part[piece(g, GROUP), :] = produce(g).astype(BF16)
+
+    for item in produce_ready:
+        item.wait()
+    fill(0)
     pl.semaphore_wait(
         barrier, has_left.astype(jnp.int32) + has_right.astype(jnp.int32) + len(peers)
     )
@@ -524,8 +624,8 @@
 
     def right(c):
         return pltpu.make_async_remote_copy(
-            src_ref=to_right.at[c],
-            dst_ref=from_left.at[c],
+            src_ref=to_right.at[piece(c, size)],
+            dst_ref=from_left.at[piece(c, size)],
             send_sem=send_sem.at[0, c],
             recv_sem=recv_sem.at[0, c],
             device_id=(line, place + 1),
@@ -534,8 +634,8 @@
 
     def left(c):
         return pltpu.make_async_remote_copy(
-            src_ref=to_left.at[c],
-            dst_ref=from_right.at[c],
+            src_ref=to_left.at[piece(c, size)],
+            dst_ref=from_right.at[piece(c, size)],
             send_sem=send_sem.at[1, c],
             recv_sem=recv_sem.at[1, c],
             device_id=(line, place - 1),
@@ -552,20 +652,18 @@
         c_left = s - LAG * (n_tp - 1 - place)
         c_out = s - late
 
-        @pl.when(s < chunks)
-        def _():
-            part[s] = produce(s).astype(BF16)
-
         @pl.when((c_right >= 0) & (c_right < chunks))
         def _():
+            at = piece(c_right, size)
+
             @pl.when(jnp.logical_not(has_left))
             def _():
-                to_right[c_right] = part[c_right]
+                to_right[at, :] = part[at, :]
 
             @pl.when(has_left)
             def _():
                 right(c_right).wait_recv()
-                to_right[c_right] = plus(part[c_right], from_left[c_right])
+                to_right[at, :] = plus(part[at, :], from_left[at, :])
 
             @pl.when(has_right)
             def _():
@@ -573,28 +671,41 @@
 
         @pl.when((c_left >= 0) & (c_left < chunks))
         def _():
+            at = piece(c_left, size)
+
             @pl.when(jnp.logical_not(has_right))
             def _():
-                to_left[c_left] = part[c_left]
+                to_left[at, :] = part[at, :]
 
             @pl.when(has_right)
             def _():
                 left(c_left).wait_recv()
-                to_left[c_left] = plus(part[c_left], from_right[c_left])
+                to_left[at, :] = plus(part[at, :], from_right[at, :])
 
             @pl.when(has_left)
             def _():
                 left(c_left).start()
+
+        @pl.when((s + 1 < groups))
+        def _():
+            fill(s + 1)
+
+        @pl.when(s == 1)
+        def _():
+            for item in consume_ready:
+                item.wait()
 
         @pl.when((c_out >= 0) & (c_out < chunks))
         def _():
+            at = piece(c_out, size)
+
             @pl.when(has_right)
             def _():
-                consume(c_out, to_right[c_out].astype(F32) + from_right[c_out].astype(F32))
+                consume(c_out, to_right[at, :].astype(F32) + from_right[at, :].astype(F32))
 
             @pl.when(jnp.logical_not(has_right))
             def _():
-                consume(c_out, to_right[c_out].astype(F32))
+                consume(c_out, to_right[at, :].astype(F32))
 
         for job in jobs:
             job[2](s)
@@ -619,10 +730,6 @@
     lax.fori_loop(0, chunks, finish, 0)
 
 
-def piece(c, rows):
-    return pl.ds(pl.multiple_of(c * rows, rows), rows)
-
-
 def mean_square(values):
     return jnp.mean(values * values, axis=-1, keepdims=True)
 
@@ -634,27 +741,36 @@
 def attn_out_line(mixed, place, weight, inputs, gain):
     rows, width = inputs.shape
     size = rows // CHUNKS
+    groups = rows // GROUP
 
     def bind(ins, outs):
-        mixed_ref, place_ref, w_ref, x_ref, gain_ref = ins
-        own_ref, middle_ref, normed_ref = outs
-
-        def produce(c):
-            own = nn(place_ref[piece(c, size), :], mixed_ref[...].astype(BF16)).astype(BF16)
-            own_ref[piece(c, size), :] = own
-            return nt(own, w_ref[...])
+        mixed_in, place_in, w_in, x_in, gain_ref = ins
+        own_out, middle_out, normed_out = outs
+
+        def produce(g):
+            own = nn(place_in.ref[piece(g, GROUP), :], mixed_in.ref[...].astype(BF16)).astype(BF16)
+            own_out.ref[piece(g, GROUP), :] = own
+            own_out.save(g)
+            return nt(own, w_in.ref[...])
 
         def consume(c, total):
-            middle = x_ref[piece(c, size), :].astype(F32) + total
-            middle_ref[piece(c, size), :] = middle.astype(BF16)
+            at = piece(c, size)
+            middle = x_in.ref[at, :].astype(F32) + total
+            middle_out.ref[at, :] = middle.astype(BF16)
+            middle_out.save(c)
             unit = middle * lax.rsqrt(mean_square(middle) + EPSILON)
-            normed_ref[piece(c, size), :] = (unit * gain_ref[...]).astype(BF16)
-
-        return produce, consume
+            normed_out.ref[at, :] = (unit * gain_ref[...]).astype(BF16)
+            normed_out.save(c)
+
+        return [mixed_in, place_in, w_in], [x_in], produce, consume
 
     return (
-        [(item, True) for item in (mixed, place, weight, inputs, gain)],
-        [(shape(*mixed.shape), True), (shape(rows, width), True), (shape(rows, width), True)],
+        [(mixed, LOAD), (place, LOAD), (weight, LOAD), (inputs, LOAD), (gain, VMEM)],
+        [
+            (shape(*mixed.shape), (SAVE, groups, 0)),
+            (shape(rows, width), (SAVE, CHUNKS, 0)),
+            (shape(rows, width), (SAVE, CHUNKS, 0)),
+        ],
         rows,
         width,
         bind,
@@ -664,30 +780,43 @@
 def middle_back_line(part, grad, middle, gain, weight):
     rows, width = grad.shape
     size = rows // CHUNKS
+    groups = rows // GROUP
+    each = GROUP // size
 
     def bind(ins, outs):
-        part_ref, g_ref, middle_ref, gain_ref, w_ref = ins
-        low_ref, mixed_ref, dgain_ref = outs
+        part_in, g_in, middle_in, gain_ref, w_in = ins
+        low_out, mixed_out, dgain_ref = outs
         dgain_ref[...] = jnp.zeros_like(dgain_ref)
 
-        def produce(c):
-            return part_ref[piece(c, size), :]
+        def produce(g):
+            return part_in.ref[piece(g, GROUP), :]
 
         def consume(c, total):
-            middle = middle_ref[piece(c, size), :].astype(F32)
+            at = piece(c, size)
+            middle = middle_in.ref[at, :].astype(F32)
             inverse = lax.rsqrt(mean_square(middle) + EPSILON)
             unit = middle * inverse
             dgain_ref[...] += jnp.sum(total * unit, axis=0, keepdims=True)
-            grad = g_ref[piece(c, size), :].astype(F32) + back(total, unit, inverse, gain_ref[...])
-            low = grad.astype(BF16)
-            low_ref[piece(c, size), :] = low
-            mixed_ref[piece(c, size), :] = nn(low, w_ref[...]).astype(BF16)
-
-        return produce, consume
+            grad = g_in.ref[at, :].astype(F32) + back(total, unit, inverse, gain_ref[...])
+            low_out.ref[at, :] = grad.astype(BF16)
+            low_out.save(c)
+
+            @pl.when(lax.rem(c, each) == each - 1)
+            def _():
+                g = c // each
+                at = piece(g, GROUP)
+                mixed_out.ref[at, :] = nn(low_out.ref[at, :], w_in.ref[...]).astype(BF16)
+                mixed_out.save(g)
+
+        return [part_in], [g_in, middle_in, w_in], produce, consume
 
     return (
-        [(item, True) for item in (part, grad, middle, gain, weight)],
-        [(shape(rows, width), True), (shape(rows, weight.shape[1]), True), (shape(1, width, F32), True)],
+        [(part, LOAD), (grad, LOAD), (middle, LOAD), (gain, VMEM), (weight, LOAD)],
+        [
+            (shape(rows, width), (SAVE, CHUNKS, 0)),
+            (shape(rows, weight.shape[1]), (SAVE, groups, 0)),
+            (shape(1, width, F32), VMEM),
+        ],
         rows,
         width,
         bind,
@@ -699,30 +828,32 @@
     size = rows // CHUNKS
 
     def bind(ins, outs):
-        gq_ref, gkv_ref, place_ref, w_ref, x_ref, mid_ref, gain_ref = ins
-        out_ref, dgain_ref = outs
-        queries = gq_ref.shape[1]
+        gq_in, gkv_in, place_in, w_in, x_in, mid_in, gain_ref = ins
+        out, dgain_ref = outs
+        queries = gq.shape[1]
         dgain_ref[...] = jnp.zeros_like(dgain_ref)
 
-        def produce(c):
-            slots = place_ref[piece(c, size), :]
-            own_q = nn(slots, gq_ref[...]).astype(BF16)
-            own_kv = nn(slots, gkv_ref[...]).astype(BF16)
-            return nt(own_q, w_ref[:, :queries]) + nt(own_kv, w_ref[:, queries:])
+        def produce(g):
+            slots = place_in.ref[piece(g, GROUP), :]
+            own_q = nn(slots, gq_in.ref[...]).astype(BF16)
+            own_kv = nn(slots, gkv_in.ref[...]).astype(BF16)
+            return nt(own_q, w_in.ref[:, :queries]) + nt(own_kv, w_in.ref[:, queries:])
 
         def consume(c, total):
-            x = x_ref[piece(c, size), :].astype(F32)
+            at = piece(c, size)
+            x = x_in.ref[at, :].astype(F32)
             inverse = lax.rsqrt(mean_square(x) + EPSILON)
             unit = x * inverse
             dgain_ref[...] += jnp.sum(total * unit, axis=0, keepdims=True)
-            grad = mid_ref[piece(c, size), :].astype(F32) + back(total, unit, inverse, gain_ref[...])
-            out_ref[piece(c, size), :] = grad.astype(BF16)
-
-        return produce, consume
+            grad = mid_in.ref[at, :].astype(F32) + back(total, unit, inverse, gain_ref[...])
+            out.ref[at, :] = grad.astype(BF16)
+            out.save(c)
+
+        return [gq_in, gkv_in, place_in, w_in], [x_in, mid_in], produce, consume
 
     return (
-        [(item, True) for item in (gq, gkv, place, weight, inputs, mid, gain)],
-        [(shape(rows, width), True), (shape(1, width, F32), True)],
+        [(item, LOAD) for item in (gq, gkv, place, weight, inputs, mid)] + [(gain, VMEM)],
+        [(shape(rows, width), (SAVE, CHUNKS, 0)), (shape(1, width, F32), VMEM)],
         rows,
         width,
         bind,
@@ -746,8 +877,8 @@
         return peers, start, hook, finish
 
     return (
-        [(own, False)],
-        [(shape(n_ctx * own.shape[0], own.shape[1]), False)],
+        [(own, ANY)],
+        [(shape(n_ctx * own.shape[0], own.shape[1]), ANY)],
         [dma((1,))] + [dma((1, chips))] * 4,
         bind,
     )
@@ -759,11 +890,12 @@
     tile = 256
     tiles, down_tiles = units // tile, width // tile
     share = 1.0 / n_tp
+    every = max(1, CHUNKS // 16)
     dma = pltpu.SemaphoreType.DMA
 
     def bind(ins, outs, scratch):
-        middle_ref, x_ref, g_ref, w_hbm = ins
-        hid_ref, gg_ref, gu_ref, down_ref, gn_ref = outs
+        middle_in, x_in, g_in, w_hbm = ins
+        hid, gg, gu, down_out, gn_out = outs
         w_ref, sem = scratch
 
         def load(t, part):
@@ -781,39 +913,50 @@
             cols = [
                 pl.ds(pl.multiple_of(part * units + t * tile, tile), tile) for part in range(3)
             ]
-            gate = nn(x_ref[...], w_ref[:, cols[0]])
-            up = nn(x_ref[...], w_ref[:, cols[1]])
-            grad = nn(g_ref[...], w_ref[:, cols[2]])
+            gate = nn(x_in.ref[...], w_ref[:, cols[0]])
+            up = nn(x_in.ref[...], w_ref[:, cols[1]])
+            grad = nn(g_in.ref[...], w_ref[:, cols[2]])
             sigmoid = jax.nn.sigmoid(gate)
             silu = gate * sigmoid
-            hid_ref[:, cols[0]] = (silu * up).astype(BF16)
-            gu_ref[:, cols[0]] = (grad * silu).astype(BF16)
-            gg_ref[:, cols[0]] = (grad * up * sigmoid * (1.0 + gate * (1.0 - sigmoid))).astype(BF16)
+            hid.ref[:, cols[0]] = (silu * up).astype(BF16)
+            gu.ref[:, cols[0]] = (grad * silu).astype(BF16)
+            gg.ref[:, cols[0]] = (grad * up * sigmoid * (1.0 + gate * (1.0 - sigmoid))).astype(BF16)
+            for out in (hid, gu, gg):
+                out.save(t)
 
         def second(t):
             at = pl.ds(pl.multiple_of(t * tile, tile), tile)
-            down = nt(hid_ref[...], w_ref[at, 2 * units :])
-            down_ref[:, at] = (down + middle_ref[:, at].astype(F32) * share).astype(BF16)
-            gn_ref[:, at] = (
-                nt(gg_ref[...], w_ref[at, :units]) + nt(gu_ref[...], w_ref[at, units : 2 * units])
+            down = nt(hid.ref[...], w_ref[at, 2 * units :])
+            down_out.ref[:, at] = (down + middle_in.ref[:, at].astype(F32) * share).astype(BF16)
+            gn_out.ref[:, at] = (
+                nt(gg.ref[...], w_ref[at, :units]) + nt(gu.ref[...], w_ref[at, units : 2 * units])
             ).astype(BF16)
+            down_out.save(t)
+            gn_out.save(t)
 
         def hook(s):
-            h = s - 1
-
-            @pl.when((h >= 0) & (h < tiles))
+            h = (s - 1) // every
+            now = lax.rem(s - 1, every) == 0
+
+            @pl.when(s == 1)
+            def _():
+                for item in (middle_in, x_in, g_in):
+                    item.wait()
+
+            @pl.when(now & (s >= 1) & (h < tiles))
             def _():
                 first(h)
 
-            @pl.when((h >= tiles) & (h < tiles + down_tiles))
+            @pl.when(now & (h >= tiles) & (h < tiles + down_tiles))
             def _():
                 second(h - tiles)
 
         return [], start, hook, lambda: None
 
     return (
-        [(middle, True), (normed, True), (grad, True), (weight, False)],
-        [(shape(rows, units), True)] * 3 + [(shape(rows, width), True)] * 2,
+        [(middle, LOAD), (normed, LOAD), (grad, LOAD), (weight, ANY)],
+        [(shape(rows, units), (SAVE, tiles, 1))] * 3
+        + [(shape(rows, width), (SAVE, down_tiles, 1))] * 2,
         [VMEM(weight.shape, BF16), dma((3, tiles))],
         bind,
     )
@@ -829,10 +972,8 @@
 
     def bind(ins, outs, scratch):
         (out_hbm,) = outs
-        held, sems, out_buf, out_sem = scratch[: len(sources)], scratch[-3], scratch[-2], scratch[-1]
-
-        def load(i):
-            return pltpu.make_async_copy(ins[i], held[i], sems.at[i])
+        held = [item.ref for item in ins[: len(sources)]]
+        out_buf, out_sem = scratch
 
         def save(h):
             slot = lax.rem(h, 2)
@@ -842,15 +983,11 @@
                 out_sem.at[slot],
             )
 
-        def start():
-            for i in range(len(sources)):
-                load(i).start()
-
         def hook(s):
             @pl.when(s == 1)
             def _():
-                for i in range(len(sources)):
-                    load(i).wait()
+                for item in ins[: len(sources)]:
+                    item.wait()
 
             h = (s - 1) // every
             now = (s >= 1) & (lax.rem(s - 1, every) == 0) & (h < total)
@@ -883,13 +1020,12 @@
             save(total - 2).wait()
             save(total - 1).wait()
 
-        return [], start, hook, finish
+        return [], lambda: None, hook, finish
 
     return (
-        [(item, False) for item in sources] + [(room, False)],
-        [(shape(width, total * tile), False)],
-        [VMEM(item.shape, BF16) for item in sources]
-        + [dma((len(sources),)), VMEM((2, width, tile), BF16), dma((2,))],
+        [(item, LOAD) for item in sources] + [(room, ANY)],
+        [(shape(width, total * tile), ANY)],
+        [VMEM((2, width, tile), BF16), dma((2,))],
         bind,
     )
 
@@ -977,8 +1113,8 @@
         return peers, start, hook, finish
 
     return (
-        [(whole_rows, False)],
-        [(shape(rows, width, dtype), True)],
+        [(whole_rows, ANY)],
+        [(shape(rows, width, dtype), VMEM)],
         [
             VMEM((chips, rows, width), BF16),
             VMEM((chips, rows, width), BF16),
@@ -1108,7 +1244,7 @@
     return place, in_order
 
 
-def layout(lengths_row, order_row, rank, n_ctx, head):
+def layout(lengths_row, order_row, rank, n_ctx, head, group):
     runs = order_row.reshape(n_ctx, -1)
     rows = runs.shape[1]
     place, in_order = sort_runs(runs)
@@ -1134,14 +1270,15 @@
     lo = jnp.sum((largest[None, :] < oldest[:, None]).astype(jnp.int32), axis=1)
     hi = jnp.sum((smallest[None, :] <= newest[:, None]).astype(jnp.int32), axis=1)
     keys = grouped.transpose(1, 0, 2).reshape(blocks, n_ctx * SUB)
+    of_group = lambda row: jnp.tile(row.reshape(-1, 1, QROWS), (1, 1, group))
     marks = (
         lo,
         hi,
         keys[:, None, :],
         packed[:, None],
         first[:, None],
-        packed[None, :],
-        first[None, :],
+        of_group(packed),
+        of_group(first),
     )
     return to_slot, to_sorted, cosine, sine, marks
 
@@ -1180,7 +1317,7 @@
         pieces += [w_key[:, at], w_value[:, at]]
     qkv_w, out_w = gather_ctx([jnp.concatenate(pieces, axis=1), w_out.T], n_ctx, 0)
     mlp_own = jnp.concatenate([w_gate, w_up, w_down.T], axis=1)
-    orders = [layout(seq_lengths[b], token_order[b], rank, n_ctx, head) for b in range(micro_count)]
+    orders = [layout(seq_lengths[b], token_order[b], rank, n_ctx, head, heads // kv_heads) for b in range(micro_count)]
     inputs = hidden_in.astype(F32)
     inverse = lax.rsqrt(jnp.mean(inputs * inputs, axis=-1, keepdims=True) + EPSILON)
     normed = (inputs * inverse * attn_gain).astype(BF16)
@@ -1202,13 +1339,13 @@
         return attend_forward(projected[b][0], kv_all[b], orders[b][4], head, kv_heads)
 
     def out_line(b):
-        return attn_out_line(attended[b][0], orders[b][0], out_w, hidden_in[b], m_gain)
+        return attn_out_line(attended[b][0], orders[b][0], out_w, One(hidden_in, b), m_gain)
 
     def middle_line(b):
-        return middle_back_line(fed[b][4], cotangent[b], middles[b][1], m_gain, out_w)
+        return middle_back_line(fed[b][4], One(cotangent, b), middles[b][1], m_gain, out_w)
 
     def feed(b):
-        return mlp_job(middles[b][1], middles[b][2], cotangent[b], mlp_w, n_tp)
+        return mlp_job(middles[b][1], middles[b][2], One(cotangent, b), mlp_w, n_tp)
 
     attended, middles, fed, mids, backs = [], [], [], [], []
     attended.append(forward(0))
@@ -1237,23 +1374,23 @@
     backs.append(backward(0, mids[0][1]))
     tile = 512 if units % 512 == 0 else 256
     line = middle_line(1)
-    line[0][0] = (after(line[0][0][0], backs[0][0]), True)
+    line[0][0] = (after(line[0][0][0], backs[0][0]), LOAD)
     results = run_jobs(
         n_tp,
         line,
         [
             weight_job(
-                [middles[b][2] for b in both] + [cotangent[b] for b in both],
+                [middles[b][2] for b in both] + [One(cotangent, b) for b in both],
                 [
                     (tuple(both), [fed[b][1] for b in both]),
                     (tuple(both), [fed[b][2] for b in both]),
                     (tuple(micro_count + b for b in both), [fed[b][0] for b in both]),
                 ],
                 tile,
-                2,
+                2 * max(1, CHUNKS // 16),
                 mlp_w,
             ),
-            scatter_job(backs[0][1].reshape(n_ctx * rows, -1), n_ctx, BF16, 4, 16),
+            scatter_job(backs[0][1].reshape(n_ctx * rows, -1), n_ctx, BF16, CHUNKS // 4, CHUNKS),
         ],
         5,
         60,
@@ -1270,14 +1407,14 @@
 
     def in_line(b, gkv):
         return input_back_line(
-            backs[b][0], gkv, orders[b][0], qkv_w, hidden_in[b], mids[b][0], a_gain
+            backs[b][0], gkv, orders[b][0], qkv_w, One(hidden_in, b), mids[b][0], a_gain
         )
 
     gkv_first, dk_gain_first = key_part(0, after(dkv_first, backs[1][0]))
     results = run_jobs(
         n_tp,
         in_line(0, gkv_first),
-        [scatter_job(backs[1][1].reshape(n_ctx * rows, -1), n_ctx, BF16, 4, 16)],
+        [scatter_job(backs[1][1].reshape(n_ctx * rows, -1), n_ctx, BF16, CHUNKS // 4, CHUNKS)],
         6,
         60,
         "input_back_keys",
@@ -1298,7 +1435,7 @@
     results = run_jobs(
         n_tp,
         in_line(1, gkv_last),
-        [scatter_job(attn_grads, n_ctx, F32, 5, 20)],
+        [scatter_job(attn_grads, n_ctx, F32, CHUNKS // 4, CHUNKS + 2)],
         7,
         60,
         "input_back_weights",

time: 768 us -> 731 us (0.952)
  Pallas kernels: 663 us -> 615 us
    pallas_call x6, Pallas kernels: 478 us -> 442 us  [run_jobs(): pl.pallas_call(kernel, out_shape=[out[0] for part in parts for out in par...]
    pallas_call x4, Pallas kernels: 101 us -> 87.6 us  [the longest x2 61.4 us: attend_backward(): pl.pallas_call(functools.partial(backward_kernel, head, kv_heads), grid_s...]
    unnamed x156 -> x140, local copies, waits for them, and re-layouts: 25.4 us -> 25.6 us
  transfers between devices with their start and end apart: 3 -> 3, of which waited for: 0 -> 2; matrix products, arithmetic and copies ran while one was open for 4% -> 4% of each run, Pallas kernels for 61% -> 59%
where the time goes in v3:
time: 731 us; the launch traced here: 721 us
  Pallas kernels  615 us (84%)
  local copies, waits for them, and re-layouts  45.3 us (6%)
  other arithmetic  35.7 us (5%)
  between operations  15.4 us (2%)
    pallas_call x6, Pallas kernels, run_jobs(): pl.pallas_call(kernel, out_shape=[out[0] for part in parts for out in par...  442 us
    pallas_call x2, Pallas kernels, attend_backward(): pl.pallas_call(functools.partial(backward_kernel, head, kv_heads), grid_s...  61.4 us
    pallas_call x2, Pallas kernels, gather_ctx(): pl.pallas_call(functools.partial(gather_kernel, count, n_ctx), out_shape=...  55.8 us
    pallas_call x2, Pallas kernels, attend_forward(): pl.pallas_call(functools.partial(forward_kernel, head, kv_heads), grid_sp...  26.2 us
    unnamed x140, local copies, waits for them, and re-layouts  25.6 us
  transfers between devices with their start and end apart: 3, of which 2 were waited for; matrix products, arithmetic and copies ran while one was open for 4% of the time, Pallas kernels for 59%

profile of v3, /device:TPU:0, one launch (start us, length us, event | category | flops | bytes accessed | tf_op | source)
XLA Modules:
  0.0 721.3 jit_solution(18075321571199144762)
XLA Ops:
  8.3 1.4 convert_reduce_fusion
  9.6 1.5 select_reduce_fusion
  12.2 1.3 convert_reduce_fusion.1
  13.6 1.5 select_reduce_fusion.1
  17.9 3.1 fusion
  21.3 3.2 fusion.2
  24.5 1.3 convolution_convert_fusion.x_ref.refs_0_
  25.8 1.3 convolution_convert_fusion.1.x_ref.refs_1_
  27.1 32.9 %gather_ctx.2 = (bf16[2048,1024]{1,0:T(8,128)(2,1)S(1)}, bf16[2048,512]{1,0:T(8,128)(2,1)S(1)}) custom-call(bf16[256,1024]{1,0:T(8,128)(2,1)S(1)} %slice_dynamic-update-slice_fusion.refs_0_, bf16[256,512]{1,0:T(8,128)(2,1)S(1)} %bitcast.58), custom_call_target="tpu_custom_call" | custom-call | tf_op jit(solution)/shard_map/gather_ctx/pallas_call | solution.py:171
  60.1 1.9 fusion.10
  62.5 3.0 project_qkv.3
  65.5 1.1 copy-done.11
  66.6 3.0 project_qkv.2
  69.7 1.1 copy-done.9
  72.4 22.9 %gather_ctx.3 = bf16[4096,512]{1,0:T(8,128)(2,1)S(1)} custom-call(bf16[512,512]{1,0:T(8,128)(2,1)S(1)} %get-tuple-element.76.refs_0_), custom_call_target="tpu_custom_call" | custom-call | tf_op jit(solution)/shard_map/gather_ctx/pallas_call | solution.py:171
  95.3 2.0 copy-done.1
  97.3 1.4 copy.64
  98.7 2.9 pad_maximum_fusion.1
  107.9 3.0 copy-done.2
  110.9 12.1 %attend_forward.2 = (f32[512,512]{1,0:T(8,128)S(1)}, f32[2,2,512]{2,1,0:T(2,128)S(1)}) custom-call(s32[2]{0:T(128)S(1)} %get-tuple-element.226.lo_ref, s32[2]{0:T(128)S(1)} %get-tuple-element.227.hi_ref, bf16[512,512]{1,0:T(8,128)(2,1)S(1)} %get-tuple-element.73.q_ref, bf16[8,512,512]{2,1,0:T(8,128)(2,1)S(1)} %bitcast.55, ...), custom_call_target="tpu_custom_call" | custom-call | tf_op jit(solution)/shard_map/attend_forward/pallas_call | solution.py:293
  124.5 65.5 %attn_out_gather.1 = (bf16[512,512]{1,0:T(8,128)(2,1)S(1)}, bf16[512,2048]{1,0:T(8,128)(2,1)S(1)}, bf16[512,2048]{1,0:T(8,128)(2,1)S(1)}, bf16[4096,512]{1,0:T(8,128)(2,1)S(1)}) custom-call(f32[512,512]{1,0:T(8,128)S(1)} %get-tuple-element.77.refs_0_.out_ref, bf16[512,512]{1,0:T(8,128)(2,1)S(1)} %fusion.3.refs_1_.refs_2_, ...), custom_call_target="tpu_custom_call" | custom-call | tf_op jit(solution)/shard_map/attn_out_gather/pallas_call | solution.py:575
  190.0 1.3 copy-done.5
  191.4 1.3 copy-done.6
  194.3 14.1 %attend_forward.3 = (f32[512,512]{1,0:T(8,128)S(1)}, f32[2,2,512]{2,1,0:T(2,128)S(1)}) custom-call(s32[2]{0:T(128)S(1)} %get-tuple-element.218.lo_ref, s32[2]{0:T(128)S(1)} %get-tuple-element.219.hi_ref, bf16[512,512]{1,0:T(8,128)(2,1)S(1)} %copy-done.25, bf16[8,512,512]{2,1,0:T(8,128)(2,1)S(1)} %bitcast.56, ...), custom_call_target="tpu_custom_call" | custom-call | tf_op jit(solution)/shard_map/attend_forward/pallas_call | solution.py:293
  208.4 2.0 copy-done.4
  210.4 1.0 copy-done.14
  212.9 4.0 all-gather.2.cloned.1.call-done.refs_8_.refs_15_
  217.0 63.4 %attn_out_mlp.1 = (bf16[512,512]{1,0:T(8,128)(2,1)}, bf16[512,2048]{1,0:T(8,128)(2,1)}, bf16[512,2048]{1,0:T(8,128)(2,1)}, bf16[512,1536]{1,0:T(8,128)(2,1)}, bf...) custom-call(f32[512,512]{1,0:T(8,128)} %copy-done.14, ...), custom_call_target="tpu_custom_call" | custom-call | tf_op jit(solution)/shard_map/attn_out_mlp/pallas_call | solution.py:575
  280.4 63.6 %middle_back_mlp.1 = (bf16[512,2048]{1,0:T(8,128)(2,1)}, bf16[512,512]{1,0:T(8,128)(2,1)}, f32[1,2048]{1,0:T(1,128)}, bf16[512,1536]{1,0:T(8,128)(2,1)}, bf16[51...) custom-call(bf16[512,2048]{1,0:T(8,128)(2,1)} %get-tuple-element.86.refs_, ...), custom_call_target="tpu_custom_call" | custom-call | tf_op jit(solution)/shard_map/middle_back_mlp/pallas_call | solution.py:575
  346.0 1.3 convolution_convert_fusion.3.g_ref
  347.2 28.8 %attend_backward.2 = (bf16[512,512]{1,0:T(8,128)(2,1)}, bf16[8,512,512]{2,1,0:T(8,128)(2,1)}, f32[1,128]{1,0:T(1,128)}) custom-call(s32[2]{0:T(128)} %copy-done.44, s32[2]{0:T(128)} %copy-done.45, bf16[512,512]{1,0:T(8,128)(2,1)} %copy-done.26, bf16[8,512,512]{2,1,0:T(8,128)(2,1)} %bitcast.54, s32[8,1,512]{2,1,0:T(1,128)} %copy-done.36, ...), custom_call_target="tpu_custom_call" | custom-call | tf_op jit(solution)/shard_map/attend_backward/pallas_call | solution.py:415
  376.1 118.9 %middle_back_weights.1 = (bf16[512,2048]{1,0:T(8,128)(2,1)}, bf16[512,512]{1,0:T(8,128)(2,1)}, f32[1,2048]{1,0:T(1,128)}, bf16[2048,4608]{1,0:T(8,128)(2,1)}, bf16[512,512]{1,0:T(8,128)(2,1)}) custom-call(bf16[512,2048]{1,0:T(8,128)(2,1)} %get-tuple-element.95.refs_0_, bf16[2,512,2048]{2,1,0:T(8,128)(2,1)} %refs_8_.1, ...), custom_call_target="tpu_custom_call", output_to_operand_aliasing={{3}: (15, {})} | custom-call | tf_op jit(solution)/shard_map/middle_back_weights/pallas_call | solution.py:575
  496.3 1.3 convolution_convert_fusion.2.g_ref
  497.5 32.5 %attend_backward.3 = (bf16[512,512]{1,0:T(8,128)(2,1)}, bf16[8,512,512]{2,1,0:T(8,128)(2,1)}, f32[1,128]{1,0:T(1,128)}) custom-call(s32[2]{0:T(128)} %copy-done.42, s32[2]{0:T(128)} %copy-done.43, bf16[512,512]{1,0:T(8,128)(2,1)} %copy-done.24, bf16[8,512,512]{2,1,0:T(8,128)(2,1)} %bitcast.57, s32[8,1,512]{2,1,0:T(1,128)} %copy-done.35, ...), custom_call_target="tpu_custom_call" | custom-call | tf_op jit(solution)/shard_map/attend_backward/pallas_call | solution.py:415
  531.5 66.6 %input_back_keys.1 = (bf16[512,2048]{1,0:T(8,128)(2,1)}, f32[1,2048]{1,0:T(1,128)}, bf16[512,512]{1,0:T(8,128)(2,1)}) custom-call(bf16[512,512]{1,0:T(8,128)(2,1)} %get-tuple-element.93.refs_0_.refs_4_, bf16[512,512]{1,0:T(8,128)(2,1)} %copy-done.27, bf16[512,512]{1,0:T(8,128)(2,1)} %copy-done.13, bf16[2048,1024]{1,0:T(8,128)(2,1)} %copy-done, ...), custom_call_target="tpu_custom_call" | custom-call | tf_op jit(solution)/shard_map/input_back_keys/pallas_call | solution.py:575
  598.1 1.0 copy-done.34
  600.5 13.3 %weight_grads.1.refs_7_ = bf16[2048,1536]{1,0:T(8,128)(2,1)} custom-call(bf16[512,2048]{1,0:T(8,128)(2,1)} %copy-done.7, bf16[512,2048]{1,0:T(8,128)(2,1)} %copy-done.8, bf16[512,2048]{1,0:T(8,128)(2,1)} %get-tuple-element.110.refs_5_.refs_2_, bf16[512,2048]{1,0:T(8,128)(2,1)} %get-tuple-element.115.refs_3_.refs_5_, ...), custom_call_target="tpu_custom_call" | custom-call | tf_op jit(solution)/shard_map/weight_grads/pallas_call | solution.py:1159
  613.9 64.0 %input_back_weights.1 = (bf16[512,2048]{1,0:T(8,128)(2,1)}, f32[1,2048]{1,0:T(1,128)}, f32[256,1536]{1,0:T(8,128)}) custom-call(bf16[512,512]{1,0:T(8,128)(2,1)} %get-tuple-element.107.refs_5_.refs_0_, bf16[512,512]{1,0:T(8,128)(2,1)} %copy-done.28, bf16[512,512]{1,0:T(8,128)(2,1)} %fusion.4.refs_1_.refs_2_, bf16[2048,1024]{1,0:T(8,128)(2,1)} %copy-done, ...), custom_call_target="tpu_custom_call" | custom-call | tf_op jit(solution)/shard_map/input_back_weights/pallas_call | solution.py:575
  678.9 9.1 %sum_gains.1 = f32[8,128]{1,0:T(8,128)S(1)} custom-call(f32[8,8,128]{2,1,0:T(8,128)S(1)} %concatenate.33.x_ref), custom_call_target="tpu_custom_call" | custom-call | tf_op jit(solution)/shard_map/sum_gains/pallas_call | solution.py:1220
  688.0 2.1 slice_bitcast_fusion.5
  690.1 1.0 copy.65
  691.1 1.1 fusion.18
  694.8 5.5 maximum_convert_fusion
  700.3 4.6 pad_maximum_fusion
  705.7 2.2 convert_element_type.81
  707.9 1.3 slice_bitcast_fusion.4
  709.2 3.1 copy.66
  712.2 2.1 fusion.17
  (202 shorter events, 28.2 us)
Async XLA Ops:
  7.2 13.8 %copy-start.48 = (bf16[256,512]{1,0:T(8,128)(2,1)S(1)}, bf16[256,512]{1,0:T(8,128)(2,1)}, u32[]{:S(2)}) copy-start(bf16[256,512]{1,0:T(8,128)(2,1)} %param.19) | copy-start | bytes 786436
  7.2 13.8 %copy-start.50 = (bf16[256,256]{1,0:T(8,128)(2,1)S(1)}, bf16[256,256]{1,0:T(8,128)(2,1)}, u32[]{:S(2)}) copy-start(bf16[256,256]{1,0:T(8,128)(2,1)} %param.20) | copy-start | bytes 393220
  7.2 13.8 %copy-start.51 = (bf16[256,256]{1,0:T(8,128)(2,1)S(1)}, bf16[256,256]{1,0:T(8,128)(2,1)}, u32[]{:S(2)}) copy-start(bf16[256,256]{1,0:T(8,128)(2,1)} %param.21) | copy-start | bytes 393220
  7.2 13.9 %copy-start.49 = (bf16[512,256]{1,0:T(8,128)(2,1)S(1)}, bf16[512,256]{1,0:T(8,128)(2,1)}, u32[]{:S(2)}) copy-start(bf16[512,256]{1,0:T(8,128)(2,1)} %param.24) | copy-start | bytes 786436
  7.2 14.1 %copy-start.52 = (f32[2048]{0:T(1024)S(1)}, f32[2048]{0:T(1024)}, u32[]{:S(2)}) copy-start(f32[2048]{0:T(1024)} %param.18) | copy-start | bytes 24580
  7.2 209.8 %all-gather.2.cloned.1.call-start = ((), (), s32[]{:S(2)}) async-start(), calls=%async_computation.1 | async-start | bytes 21233664 | tf_op jit(solution)/shard_map/all_gather | solution.py:1336
  15.1 9.5 %copy-start.53 = (s32[1,512]{1,0:T(1,128)}, s32[1,512]{1,0:T(1,128)S(1)}, u32[]{:S(2)}) copy-start(s32[1,512]{1,0:T(1,128)S(1)} %get-tuple-element.220) | copy-start | bytes 6148
  25.8 36.6 %copy-start.7 = (bf16[512,2048]{1,0:T(8,128)(2,1)}, bf16[512,2048]{1,0:T(8,128)(2,1)S(1)}, u32[]{:S(2)}) copy-start(bf16[512,2048]{1,0:T(8,128)(2,1)S(1)} %convolution_convert_fusion.x_ref.refs_0_) | copy-start | bytes 6291460
  27.1 39.5 %copy-start.8 = (bf16[512,2048]{1,0:T(8,128)(2,1)}, bf16[512,2048]{1,0:T(8,128)(2,1)S(1)}, u32[]{:S(2)}) copy-start(bf16[512,2048]{1,0:T(8,128)(2,1)S(1)} %convolution_convert_fusion.1.x_ref.refs_1_) | copy-start | bytes 6291460
  27.1 35.3 %copy-start.40 = (f32[128]{0:T(128)S(1)}, f32[128]{0:T(128)}, u32[]{:S(2)}) copy-start(f32[128]{0:T(128)} %param.22) | copy-start | bytes 1540
  27.1 35.3 %copy-start.41 = (f32[128]{0:T(128)S(1)}, f32[128]{0:T(128)}, u32[]{:S(2)}) copy-start(f32[128]{0:T(128)} %param.23) | copy-start | bytes 1540
  60.0 6.6 copy-start
  60.0 64.4 %copy-start.3 = (bf16[2048,512]{1,0:T(8,128)(2,1)}, bf16[2048,512]{1,0:T(8,128)(2,1)S(1)}, u32[]{:S(2)}) copy-start(bf16[2048,512]{1,0:T(8,128)(2,1)S(1)} %get-tuple-element.78.refs_2_.refs_4_) | copy-start | bytes 6291460
  62.2 7.5 %copy-start.20 = (f32[512,128]{1,0:T(8,128)}, f32[512,128]{1,0:T(8,128)S(1)}, u32[]{:S(2)}) copy-start(f32[512,128]{1,0:T(8,128)S(1)} %get-tuple-element.224.cos_ref) | copy-start | bytes 786436
  62.2 7.5 %copy-start.22 = (f32[512,128]{1,0:T(8,128)}, f32[512,128]{1,0:T(8,128)S(1)}, u32[]{:S(2)}) copy-start(f32[512,128]{1,0:T(8,128)S(1)} %get-tuple-element.225.sin_ref) | copy-start | bytes 786436
  62.4 7.2 %copy-start.16 = (f32[512,128]{1,0:T(8,128)}, f32[512,128]{1,0:T(8,128)S(1)}, u32[]{:S(2)}) copy-start(f32[512,128]{1,0:T(8,128)S(1)} %get-tuple-element.222.cos_ref) | copy-start | bytes 786436
  62.4 7.2 %copy-start.18 = (f32[512,128]{1,0:T(8,128)}, f32[512,128]{1,0:T(8,128)S(1)}, u32[]{:S(2)}) copy-start(f32[512,128]{1,0:T(8,128)S(1)} %get-tuple-element.223.sin_ref) | copy-start | bytes 786436
  66.6 41.3 %copy-start.26 = (bf16[512,512]{1,0:T(8,128)(2,1)}, bf16[512,512]{1,0:T(8,128)(2,1)S(1)}, u32[]{:S(2)}) copy-start(bf16[512,512]{1,0:T(8,128)(2,1)S(1)} %get-tuple-element.73.q_ref) | copy-start | bytes 1572868
  101.6 22.8 %copy-start.37 = (f32[2048]{0:T(1024)S(1)}, f32[2048]{0:T(1024)}, u32[]{:S(2)}) copy-start(f32[2048]{0:T(1024)} %param.25) | copy-start | bytes 24580
  101.7 598.6 %all-reduce.3.cloned.1.call-start = ((), (), s32[]{:S(2)}) async-start(), calls=%async_computation.3 | async-start | bytes 8388608 | tf_op jit(solution)/shard_map/psum | solution.py:1363
  104.1 85.9 %copy-start.36 = (s32[8,1,512]{2,1,0:T(1,128)}, s32[8,1,512]{2,1,0:T(1,128)S(1)}, u32[]{:S(2)}) copy-start(s32[8,1,512]{2,1,0:T(1,128)S(1)} %broadcast_in_dim_reshape.6.pk_ref) | copy-start | bytes 49156
  105.8 88.4 %copy-start.35 = (s32[8,1,512]{2,1,0:T(1,128)}, s32[8,1,512]{2,1,0:T(1,128)S(1)}, u32[]{:S(2)}) copy-start(s32[8,1,512]{2,1,0:T(1,128)S(1)} %broadcast_in_dim_reshape.7.pk_ref) | copy-start | bytes 49156
  107.9 82.1 %copy-start.44 = (s32[2]{0:T(128)}, s32[2]{0:T(128)S(1)}, u32[]{:S(2)}) copy-start(s32[2]{0:T(128)S(1)} %get-tuple-element.226.lo_ref) | copy-start | bytes 28
  107.9 82.1 %copy-start.45 = (s32[2]{0:T(128)}, s32[2]{0:T(128)S(1)}, u32[]{:S(2)}) copy-start(s32[2]{0:T(128)S(1)} %get-tuple-element.227.hi_ref) | copy-start | bytes 28
  110.9 13.5 %copy-start.32 = (bf16[512,512]{1,0:T(8,128)(2,1)S(1)}, bf16[512,512]{1,0:T(8,128)(2,1)}, u32[]{:S(2)}) copy-start(bf16[512,512]{1,0:T(8,128)(2,1)} %copy-done.31) | copy-start | bytes 1572868
  123.6 66.4 %copy-start.15 = (f32[512,512]{1,0:T(8,128)}, f32[512,512]{1,0:T(8,128)S(1)}, u32[]{:S(2)}) copy-start(f32[512,512]{1,0:T(8,128)S(1)} %get-tuple-element.77.refs_0_.out_ref) | copy-start | bytes 3145732
  124.4 65.6 %copy-start.13 = (bf16[512,512]{1,0:T(8,128)(2,1)}, bf16[512,512]{1,0:T(8,128)(2,1)S(1)}, u32[]{:S(2)}) copy-start(bf16[512,512]{1,0:T(8,128)(2,1)S(1)} %fusion.3.refs_1_.refs_2_) | copy-start | bytes 1572868
  124.4 69.1 %copy-start.58 = (s32[2,256]{1,0:T(2,128)S(1)}, s32[2,256]{1,0:T(2,128)}, u32[]{:S(2)}) copy-start(s32[2,256]{1,0:T(2,128)} %reshape.163) | copy-start | bytes 6148
  124.5 69.2 %copy-start.59 = (s32[2,256]{1,0:T(2,128)S(1)}, s32[2,256]{1,0:T(2,128)}, u32[]{:S(2)}) copy-start(s32[2,256]{1,0:T(2,128)} %reshape.164) | copy-start | bytes 6148
  124.5 69.8 %copy-start.25 = (bf16[512,512]{1,0:T(8,128)(2,1)S(1)}, bf16[512,512]{1,0:T(8,128)(2,1)}, u32[]{:S(2)}) copy-start(bf16[512,512]{1,0:T(8,128)(2,1)} %copy-done.24) | copy-start | bytes 1572868
  124.5 69.8 %copy-start.29 = (s32[512,1]{1,0:T(8,128)S(1)}, s32[512,1]{1,0:T(8,128)}, u32[]{:S(2)}) copy-start(s32[512,1]{1,0:T(8,128)} %copy.62.pq_ref) | copy-start | bytes 6148
  194.2 86.2 %copy-start.42 = (s32[2]{0:T(128)}, s32[2]{0:T(128)S(1)}, u32[]{:S(2)}) copy-start(s32[2]{0:T(128)S(1)} %get-tuple-element.218.lo_ref) | copy-start | bytes 28
  194.2 86.2 %copy-start.43 = (s32[2]{0:T(128)}, s32[2]{0:T(128)S(1)}, u32[]{:S(2)}) copy-start(s32[2]{0:T(128)S(1)} %get-tuple-element.219.hi_ref) | copy-start | bytes 28
  344.1 361.6 %reduce-scatter.2.cloned.1.call-start = ((), (), s32[]{:S(2)}) async-start(), calls=%async_computation.2 | async-start | bytes 21233664 | tf_op jit(solution)/shard_map/reduce_scatter | solution.py:1401
  497.5 32.6 %copy-start.12 = (f32[512,768]{1,0:T(8,128)S(1)}, f32[512,768]{1,0:T(8,128)}, u32[]{:S(2)}) copy-start(f32[512,768]{1,0:T(8,128)} %copy-done.11) | copy-start | bytes 4718596
  497.5 32.6 %copy-start.21 = (f32[512,128]{1,0:T(8,128)S(1)}, f32[512,128]{1,0:T(8,128)}, u32[]{:S(2)}) copy-start(f32[512,128]{1,0:T(8,128)} %copy-done.20) | copy-start | bytes 786436
  497.5 32.6 %copy-start.23 = (f32[512,128]{1,0:T(8,128)S(1)}, f32[512,128]{1,0:T(8,128)}, u32[]{:S(2)}) copy-start(f32[512,128]{1,0:T(8,128)} %copy-done.22) | copy-start | bytes 786436
  497.5 32.6 %copy-start.33 = (bf16[512,512]{1,0:T(8,128)(2,1)S(1)}, bf16[512,512]{1,0:T(8,128)(2,1)}, u32[]{:S(2)}) copy-start(bf16[512,512]{1,0:T(8,128)(2,1)} %get-tuple-element.108.grad_ref) | copy-start | bytes 1572868
  531.5 66.6 %copy-start.10 = (f32[512,768]{1,0:T(8,128)S(1)}, f32[512,768]{1,0:T(8,128)}, u32[]{:S(2)}) copy-start(f32[512,768]{1,0:T(8,128)} %copy-done.9) | copy-start | bytes 4718596
  531.5 66.6 %copy-start.17 = (f32[512,128]{1,0:T(8,128)S(1)}, f32[512,128]{1,0:T(8,128)}, u32[]{:S(2)}) copy-start(f32[512,128]{1,0:T(8,128)} %copy-done.16) | copy-start | bytes 786436
  531.5 66.6 %copy-start.19 = (f32[512,128]{1,0:T(8,128)S(1)}, f32[512,128]{1,0:T(8,128)}, u32[]{:S(2)}) copy-start(f32[512,128]{1,0:T(8,128)} %copy-done.18) | copy-start | bytes 786436
  613.8 64.1 %copy-start.55 = (f32[1,2048]{1,0:T(1,128)S(1)}, f32[1,2048]{1,0:T(1,128)}, u32[]{:S(2)}) copy-start(f32[1,2048]{1,0:T(1,128)} %get-tuple-element.121) | copy-start | bytes 24580
  613.8 64.1 %copy-start.56 = (f32[1,2048]{1,0:T(1,128)S(1)}, f32[1,2048]{1,0:T(1,128)}, u32[]{:S(2)}) copy-start(f32[1,2048]{1,0:T(1,128)} %get-tuple-element.122) | copy-start | bytes 24580
  613.8 64.1 %copy-start.57 = (f32[1,2048]{1,0:T(1,128)S(1)}, f32[1,2048]{1,0:T(1,128)}, u32[]{:S(2)}) copy-start(f32[1,2048]{1,0:T(1,128)} %get-tuple-element.119) | copy-start | bytes 24580
  613.8 65.0 %copy-start.64 = (f32[1,128]{1,0:T(1,128)S(1)}, f32[1,128]{1,0:T(1,128)}, u32[]{:S(2)}) copy-start(f32[1,128]{1,0:T(1,128)} %get-tuple-element.123) | copy-start | bytes 1540
  613.8 65.0 %copy-start.65 = (f32[1,128]{1,0:T(1,128)S(1)}, f32[1,128]{1,0:T(1,128)}, u32[]{:S(2)}) copy-start(f32[1,128]{1,0:T(1,128)} %get-tuple-element.124) | copy-start | bytes 1540
  677.9 16.9 %copy-start.47 = (bf16[512,2048]{1,0:T(8,128)(2,1)S(1)}, bf16[512,2048]{1,0:T(8,128)(2,1)}, u32[]{:S(2)}) copy-start(bf16[512,2048]{1,0:T(8,128)(2,1)} %get-tuple-element.112) | copy-start | bytes 6291460
  707.9 4.3 copy-start.46
  (21 other events, 26.3 us)
Sparse Core Ops, SparseCore 0:
  101.8 115.1 all-gather.1
  344.2 196.8 all-reduce.2
  545.2 160.5 reduce-scatter.1

commit v4 on v3

--- a/solution.py
+++ b/solution.py
@@ -149,36 +149,202 @@
     return peers, start, relay, finish
 
 
-def gather_kernel(count, n_ctx, *refs):
-    peers, start, relay, finish = gather_parts(
-        refs[:count], refs[count : 2 * count], refs[2 * count :], n_ctx
-    )
+def gather_kernel(index, n_ctx, source_ref, result_ref, *sems):
+    peers, start, relay, finish = gather_parts([source_ref.at[index]], [result_ref], sems, n_ctx)
     barrier = pltpu.get_barrier_semaphore()
     for peer in peers:
         pl.semaphore_signal(barrier, inc=1, device_id=peer, device_id_type=MESH)
     pl.semaphore_wait(barrier, len(peers))
     start()
-    for array in range(count):
-        for d in range(1, n_ctx // 2):
-            relay(array, d)
+    for d in range(1, n_ctx // 2):
+        relay(0, d)
     finish()
 
 
-def gather_ctx(arrays, n_ctx, collective):
-    count = len(arrays)
+def gather_ctx(array, index, n_ctx, collective):
+    dma = pltpu.SemaphoreType.DMA
+    unused, rows, width = array.shape
+    return pl.pallas_call(
+        functools.partial(gather_kernel, index, n_ctx),
+        out_shape=jax.ShapeDtypeStruct((n_ctx * rows, width), array.dtype),
+        in_specs=[pl.BlockSpec(memory_space=ANY)],
+        out_specs=pl.BlockSpec(memory_space=ANY),
+        scratch_shapes=[dma((1,))] + [dma((1, n_ctx // 2))] * 4,
+        compiler_params=params(60, collective),
+        name="gather_ctx",
+    )(array)
+
+
+def begin_kernel(
+    n_ctx,
+    head,
+    kv_heads,
+    x_hbm,
+    order_ref,
+    lengths_ref,
+    gain_ref,
+    frequency_ref,
+    wq_ref,
+    wk_ref,
+    wv_ref,
+    wo_ref,
+    wg_hbm,
+    wu_hbm,
+    wd_ref,
+    qkv_hbm,
+    out_hbm,
+    mlp_hbm,
+    sorted_ref,
+    to_slot_ref,
+    to_sorted_ref,
+    cos_ref,
+    sin_ref,
+    keys_ref,
+    newest_ref,
+    oldest_ref,
+    x_ref,
+    normed_ref,
+    qkv_own,
+    wo_turned,
+    mlp_own,
+    load_sem,
+    mlp_sem,
+    *gather_sems,
+):
+    micro_count, rows, width = x_ref.shape
+    queries, units = wq_ref.shape[1], wg_hbm.shape[1]
+    me = lax.axis_index("ctx")
+
+    def load(b):
+        return pltpu.make_async_copy(x_hbm.at[b], x_ref.at[b], load_sem.at[b])
+
+    for b in range(micro_count):
+        load(b).start()
+    wo_turned[...] = wo_ref[...].T
+    qkv_own[:, :queries] = wq_ref[...]
+    for n in range(kv_heads):
+        at = queries + 2 * n * head
+        own = slice(n * head, (n + 1) * head)
+        qkv_own[:, at : at + head] = wk_ref[:, own]
+        qkv_own[:, at + head : at + 2 * head] = wv_ref[:, own]
+    sources = [qkv_own, wo_turned]
+    peers, start, relay, finish = gather_parts(sources, [qkv_hbm, out_hbm], gather_sems, n_ctx)
+    barrier = pltpu.get_barrier_semaphore()
+    for peer in peers:
+        pl.semaphore_signal(barrier, inc=1, device_id=peer, device_id_type=MESH)
+    pl.semaphore_wait(barrier, len(peers))
+    start()
+    mlp_loads = [
+        pltpu.make_async_copy(item, mlp_own.at[:, slice(i * units, (i + 1) * units)], mlp_sem.at[i])
+        for i, item in enumerate((wg_hbm, wu_hbm))
+    ]
+    for copy in mlp_loads:
+        copy.start()
+    mlp_own[:, 2 * units :] = wd_ref[...].T
+
+    def relays(low, high):
+        for d in range(low, high):
+            for item in range(len(sources)):
+                relay(item, d)
+
+    across = lax.broadcasted_iota(jnp.int32, (rows, rows), 1)
+    down = lax.broadcasted_iota(jnp.int32, (rows, rows), 0)
+    column_of = lambda row: jnp.broadcast_to(row, (8, rows)).T[:, :1]
+
+    def in_order(row):
+        column = column_of(row)
+        place = jnp.sum((row < column).astype(jnp.int32), axis=1, keepdims=True)
+        return place, jnp.sum(jnp.where(place == across, column, 0), axis=0, keepdims=True)
+
+    for b in range(micro_count):
+
+        def run(r, carry):
+            row = order_ref[pl.ds(b * n_ctx + r, 1), :]
+            keys_ref[pl.ds(b * n_ctx + r, 1), :] = in_order(row)[1]
+            return carry
+
+        lax.fori_loop(0, n_ctx, run, 0)
+        row = order_ref[pl.ds(b * n_ctx + me, 1), :]
+        place, packed = in_order(row)
+        packed = column_of(packed)
+        place_row = jnp.sum((column_of(row) < row).astype(jnp.int32), axis=0, keepdims=True)
+        to_slot_ref[b] = (place == across).astype(F32).astype(BF16)
+        to_sorted = (place_row == down).astype(F32).astype(BF16)
+        to_sorted_ref[b] = to_sorted
+        first = jnp.zeros_like(packed)
+        begin = lengths_ref[b, 0] * 0
+        for i in range(lengths_ref.shape[1]):
+            first = jnp.maximum(first, jnp.where(packed >= begin, begin, 0))
+            begin = begin + lengths_ref[b, i]
+        newest_ref[b] = packed
+        oldest_ref[b] = first
+        angles = (packed - first).astype(F32) * frequency_ref[0:1, :]
+        cos_ref[b] = jnp.cos(angles)
+        sin_ref[b] = jnp.sin(angles) * frequency_ref[1:2, :]
+        load(b).wait()
+        for g in range(rows // GROUP):
+            at = slice(g * GROUP, (g + 1) * GROUP)
+            x = x_ref[b, at, :].astype(F32)
+            inverse = lax.rsqrt(jnp.mean(x * x, axis=-1, keepdims=True) + EPSILON)
+            normed_ref[at, :] = (x * inverse * gain_ref[...]).astype(BF16)
+        for g in range(rows // GROUP):
+            at = slice(g * GROUP, (g + 1) * GROUP)
+            sorted_ref[b, at, :] = nn(to_sorted_ref[b, at, :], normed_ref[...]).astype(BF16)
+        if b == 0:
+            relays(1, min(3, n_ctx // 2))
+
+    for copy in mlp_loads:
+        copy.wait()
+    mlp_save = pltpu.make_async_copy(mlp_own, mlp_hbm, mlp_sem.at[2])
+    mlp_save.start()
+    relays(min(3, n_ctx // 2), n_ctx // 2)
+    finish()
+    mlp_save.wait()
+
+
+def begin(inputs, order, lengths, gain, frequency, weights, n_ctx, head, kv_heads, collective):
+    micro_count, rows, width = inputs.shape
+    wq, wk, wv, wo, wg, wu, wd = weights
+    dma = pltpu.SemaphoreType.DMA
     chips = n_ctx // 2
-    dma = pltpu.SemaphoreType.DMA
+    count = 2
+    own, queries, units = wq.shape[0], wq.shape[1], wg.shape[1]
+    some = lambda *dims: jax.ShapeDtypeStruct(dims, BF16)
+    table = lambda *dims: jax.ShapeDtypeStruct(dims, F32)
+    ints = lambda *dims: jax.ShapeDtypeStruct(dims, jnp.int32)
+    inside, lies = pl.BlockSpec(memory_space=VMEM), pl.BlockSpec(memory_space=ANY)
     return pl.pallas_call(
-        functools.partial(gather_kernel, count, n_ctx),
+        functools.partial(begin_kernel, n_ctx, head, kv_heads),
         out_shape=[
-            jax.ShapeDtypeStruct((n_ctx * a.shape[0], a.shape[1]), a.dtype) for a in arrays
+            some(n_ctx * own, queries + 2 * wk.shape[1]),
+            some(n_ctx * own, wo.shape[0]),
+            some(own, 3 * units),
+            some(micro_count, rows, width),
+            some(micro_count, rows, rows),
+            some(micro_count, rows, rows),
+            table(micro_count, rows, head),
+            table(micro_count, rows, head),
+            ints(micro_count * n_ctx, rows),
+            ints(micro_count, rows, 1),
+            ints(micro_count, rows, 1),
         ],
-        in_specs=[pl.BlockSpec(memory_space=ANY)] * count,
-        out_specs=[pl.BlockSpec(memory_space=ANY)] * count,
-        scratch_shapes=[dma((count,))] + [dma((count, chips))] * 4,
-        compiler_params=params(16, collective),
-        name="gather_ctx",
-    )(*arrays)
+        in_specs=[lies, inside, pl.BlockSpec(memory_space=pltpu.SMEM), inside, inside]
+        + [inside, inside, inside, inside, lies, lies, inside],
+        out_specs=[lies] * 3 + [inside] * 8,
+        scratch_shapes=[
+            VMEM(inputs.shape, BF16),
+            VMEM((rows, width), BF16),
+            VMEM((own, queries + 2 * wk.shape[1]), BF16),
+            VMEM((own, wo.shape[0]), BF16),
+            VMEM((own, 3 * units), BF16),
+            dma((micro_count,)),
+            dma((3,)),
+            dma((count,)),
+        ]
+        + [dma((count, chips))] * 4,
+        compiler_params=params(60, collective),
+        name="begin",
+    )(inputs, order, lengths, gain, frequency, wq, wk, wv, wo, wg, wu, wd)
 
 
 def qkv_kernel(heads, kv_heads, x_ref, w_ref, cos_ref, sin_ref, qg_ref, kg_ref, q_ref, kv_ref, raw_ref):
@@ -204,28 +370,29 @@
 
 
 def project_qkv(normed, weight, cosine, sine, query_gain, key_gain, heads, kv_heads):
-    total, width = normed.shape
+    micro_count, total, width = normed.shape
     head = query_gain.shape[1]
     block = 256
-    row = lambda cols: pl.BlockSpec((block, cols), lambda i: (i, 0))
+    of = lambda cols: pl.BlockSpec((None, block, cols), lambda b, i: (b, i, 0))
+    result = lambda cols, dtype: jax.ShapeDtypeStruct((micro_count, total, cols), dtype)
     return pl.pallas_call(
         functools.partial(qkv_kernel, heads, kv_heads),
-        grid=(total // block,),
+        grid=(micro_count, total // block),
         out_shape=[
-            jax.ShapeDtypeStruct((total, heads * head), BF16),
-            jax.ShapeDtypeStruct((total, 2 * kv_heads * head), BF16),
-            jax.ShapeDtypeStruct((total, (heads + kv_heads) * head), F32),
+            result(heads * head, BF16),
+            result(2 * kv_heads * head, BF16),
+            result((heads + kv_heads) * head, F32),
         ],
         in_specs=[
-            row(width),
+            of(width),
             whole(weight.shape),
-            row(head),
-            row(head),
+            of(head),
+            of(head),
             whole((1, head)),
             whole((1, head)),
         ],
-        out_specs=[row(heads * head), row(2 * kv_heads * head), row((heads + kv_heads) * head)],
-        compiler_params=params(40),
+        out_specs=[of(heads * head), of(2 * kv_heads * head), of((heads + kv_heads) * head)],
+        compiler_params=params(60),
         name="project_qkv",
     )(normed, weight, cosine, sine, query_gain, key_gain)
 
@@ -284,9 +451,9 @@
         mass_ref[0, n : n + 1] = jnp.broadcast_to(jnp.log2(mass), (group * rows, 128)).T[0:1]
 
 
-def attend_forward(query, kv, marks, head, kv_heads):
+def attend_forward(query, index, kv, marks, head, kv_heads):
     lo, hi, pk_row, pq_col, sq_col = marks[:5]
-    rows, width = query.shape
+    unused, rows, width = query.shape
     group = width // (kv_heads * head)
     blocks = rows // QROWS
     own = lambda i, *s: (i, 0)
@@ -296,7 +463,7 @@
             num_scalar_prefetch=2,
             grid=(blocks,),
             in_specs=[
-                pl.BlockSpec((QROWS, width), own),
+                pl.BlockSpec((None, QROWS, width), lambda i, *s: (index, i, 0)),
                 whole(kv.shape),
                 whole(pk_row.shape),
                 pl.BlockSpec((QROWS, 1), own),
@@ -311,7 +478,7 @@
             jax.ShapeDtypeStruct((rows, width), F32),
             jax.ShapeDtypeStruct((blocks, kv_heads, group * QROWS), F32),
         ],
-        compiler_params=params(40),
+        compiler_params=params(60),
         name="attend_forward",
     )(lo, hi, query, kv, pk_row, pq_col, sq_col)
 
@@ -405,20 +572,21 @@
             dkv_ref[:, :, value_cols] = acc[:, :, value_cols].astype(BF16)
 
 
-def attend_backward(query, kv, marks, grad, out, mass, raw, cosine, sine, gain, head, kv_heads):
+def attend_backward(query, index, kv, marks, grad, out, mass, raw, cosine, sine, gain, head, kv_heads):
     lo, hi, pk_row, unused, unused_too, pq_row, sq_row = marks
-    rows, width = query.shape
+    unused, rows, width = query.shape
     group = width // (kv_heads * head)
     blocks = rows // QROWS
     own = lambda i, *s: (i, 0)
     line = lambda i, *s: (i, 0, 0)
+    of = lambda cols: pl.BlockSpec((None, QROWS, cols), lambda i, *s: (index, i, 0))
     return pl.pallas_call(
         functools.partial(backward_kernel, head, kv_heads),
         grid_spec=pltpu.PrefetchScalarGridSpec(
             num_scalar_prefetch=2,
             grid=(blocks,),
             in_specs=[
-                pl.BlockSpec((QROWS, width), own),
+                of(width),
                 whole(kv.shape),
                 whole(pk_row.shape),
                 pl.BlockSpec((1, 1, group * QROWS), line),
@@ -426,9 +594,9 @@
                 pl.BlockSpec((QROWS, width), own),
                 pl.BlockSpec((QROWS, width), own),
                 pl.BlockSpec((1, kv_heads, group * QROWS), line),
-                pl.BlockSpec((QROWS, width), own),
-                pl.BlockSpec((QROWS, head), own),
-                pl.BlockSpec((QROWS, head), own),
+                of(width),
+                of(head),
+                of(head),
                 whole((1, head)),
             ],
             out_specs=[pl.BlockSpec((QROWS, width), own), whole(kv.shape), whole((1, head))],
@@ -459,15 +627,18 @@
     dgain_ref[...] = total
 
 
-def key_back(grad, raw, cosine, sine, gain, kv_heads):
+def key_back(grad, index, raw, cosine, sine, gain, kv_heads):
     rows = grad.shape[0]
     head = gain.shape[1]
-    keys = pl.BlockSpec((rows, kv_heads * head), lambda i: (0, raw.shape[1] // (kv_heads * head) - 1))
+    keys = pl.BlockSpec(
+        (None, rows, kv_heads * head), lambda i: (index, 0, raw.shape[2] // (kv_heads * head) - 1)
+    )
+    turns = pl.BlockSpec((None, rows, head), lambda i: (index, 0, 0))
     return pl.pallas_call(
         functools.partial(key_back_kernel, head, kv_heads),
         grid=(1,),
         out_shape=[jax.ShapeDtypeStruct(grad.shape, BF16), jax.ShapeDtypeStruct((1, head), F32)],
-        in_specs=[whole(grad.shape), keys, whole((rows, head)), whole((rows, head)), whole((1, head))],
+        in_specs=[whole(grad.shape), keys, turns, turns, whole((1, head))],
         out_specs=[whole(grad.shape), whole((1, head))],
         compiler_params=params(32),
         name="key_back",
@@ -865,7 +1036,7 @@
     dma = pltpu.SemaphoreType.DMA
 
     def bind(ins, outs, scratch):
-        peers, start, relay, finish = gather_parts(ins, outs, scratch, n_ctx)
+        peers, start, relay, finish = gather_parts([ins[0].at[own.index]], outs, scratch, n_ctx)
 
         def hook(s):
             for d in range(1, chips):
@@ -1160,11 +1331,17 @@
         functools.partial(weight_kernel, starts, len(lefts)),
         grid=(at,),
         out_shape=jax.ShapeDtypeStruct((width, at * tile), BF16),
-        in_specs=[whole((rows, width))] * len(lefts) + specs,
+        in_specs=[
+            pl.BlockSpec((None, rows, width), lambda j, at=left.index: (at, 0, 0))
+            if isinstance(left, One)
+            else whole((rows, width))
+            for left in lefts
+        ]
+        + specs,
         out_specs=pl.BlockSpec((width, tile), lambda j: (0, j)),
         compiler_params=params(60),
         name="weight_grads",
-    )(*lefts, *rights)
+    )(*[source(left) for left in lefts], *rights)
 
 
 def gains_kernel(n_ctx, n_tp, x_ref, out_ref, got, send_sem, recv_sem, line_got, line_send, line_recv):
@@ -1235,52 +1412,19 @@
     )(blocks)
 
 
-def sort_runs(packed_runs):
-    place = jnp.sum((packed_runs[:, None, :] < packed_runs[:, :, None]).astype(jnp.int32), axis=2)
-    slots = jnp.arange(packed_runs.shape[1], dtype=jnp.int32)
-    in_order = jnp.sum(
-        jnp.where(place[:, :, None] == slots[None, None, :], packed_runs[:, :, None], 0), axis=1
-    )
-    return place, in_order
-
-
-def layout(lengths_row, order_row, rank, n_ctx, head, group):
-    runs = order_row.reshape(n_ctx, -1)
-    rows = runs.shape[1]
-    place, in_order = sort_runs(runs)
-    own_place = lax.dynamic_index_in_dim(place, rank, 0, keepdims=False)
-    packed = lax.dynamic_index_in_dim(in_order, rank, 0, keepdims=False)
-    starts = jnp.cumsum(lengths_row) - lengths_row
-    first = jnp.max(jnp.where(starts[None, :] <= packed[:, None], starts[None, :], 0), axis=1)
-    position = packed - first
-    inverse = jnp.exp(jnp.arange(head // 2, dtype=F32) * (-2.0 * math.log(THETA) / head))
-    angles = position.astype(F32)[:, None] * inverse[None, :]
-    cosine, sine = jnp.cos(angles), jnp.sin(angles)
-    cosine = jnp.concatenate([cosine, cosine], axis=1)
-    sine = jnp.concatenate([-sine, sine], axis=1)
-    slots = jnp.arange(rows, dtype=jnp.int32)
-    to_slot = (own_place[:, None] == slots[None, :]).astype(BF16)
-    to_sorted = (own_place[None, :] == slots[:, None]).astype(BF16)
+def attention_marks(in_order, newest, oldest, n_ctx, group):
+    rows = newest.shape[0]
     blocks = rows // SUB
     grouped = in_order.reshape(n_ctx, blocks, SUB)
     smallest = jnp.min(grouped[:, :, 0], axis=0)
     largest = jnp.max(grouped[:, :, SUB - 1], axis=0)
-    oldest = first.reshape(-1, QROWS)[:, 0]
-    newest = packed.reshape(-1, QROWS)[:, QROWS - 1]
-    lo = jnp.sum((largest[None, :] < oldest[:, None]).astype(jnp.int32), axis=1)
-    hi = jnp.sum((smallest[None, :] <= newest[:, None]).astype(jnp.int32), axis=1)
-    keys = grouped.transpose(1, 0, 2).reshape(blocks, n_ctx * SUB)
-    of_group = lambda row: jnp.tile(row.reshape(-1, 1, QROWS), (1, 1, group))
-    marks = (
-        lo,
-        hi,
-        keys[:, None, :],
-        packed[:, None],
-        first[:, None],
-        of_group(packed),
-        of_group(first),
-    )
-    return to_slot, to_sorted, cosine, sine, marks
+    first = oldest.reshape(-1, QROWS)[:, 0]
+    last = newest.reshape(-1, QROWS)[:, QROWS - 1]
+    lo = jnp.sum((largest[None, :] < first[:, None]).astype(jnp.int32), axis=1)
+    hi = jnp.sum((smallest[None, :] <= last[:, None]).astype(jnp.int32), axis=1)
+    keys = grouped.transpose(1, 0, 2).reshape(blocks, 1, n_ctx * SUB)
+    of_group = lambda column: jnp.tile(column.reshape(-1, 1, QROWS), (1, 1, group))
+    return lo, hi, keys, newest, oldest, of_group(newest), of_group(oldest)
 
 
 def on_device(
@@ -1311,35 +1455,57 @@
     q_gain, k_gain = query_gain[None, :], key_gain[None, :]
     a_gain, m_gain = attn_gain[None, :], mlp_gain[None, :]
 
-    pieces = [w_query]
-    for n in range(kv_heads):
-        at = slice(n * head, (n + 1) * head)
-        pieces += [w_key[:, at], w_value[:, at]]
-    qkv_w, out_w = gather_ctx([jnp.concatenate(pieces, axis=1), w_out.T], n_ctx, 0)
-    mlp_own = jnp.concatenate([w_gate, w_up, w_down.T], axis=1)
-    orders = [layout(seq_lengths[b], token_order[b], rank, n_ctx, head, heads // kv_heads) for b in range(micro_count)]
-    inputs = hidden_in.astype(F32)
-    inverse = lax.rsqrt(jnp.mean(inputs * inputs, axis=-1, keepdims=True) + EPSILON)
-    normed = (inputs * inverse * attn_gain).astype(BF16)
+    frequency = jnp.exp(jnp.arange(head // 2, dtype=F32) * (-2.0 * math.log(THETA) / head))
+    one = jnp.ones((head // 2,), F32)
+    frequency = jnp.stack([jnp.tile(frequency, 2), jnp.concatenate([-one, one])])
+    (
+        qkv_w,
+        out_w,
+        mlp_own,
+        sorted_normed,
+        to_slot,
+        to_sorted,
+        cosine,
+        sine,
+        in_order,
+        newest,
+        oldest,
+    ) = begin(
+        hidden_in,
+        token_order.reshape(micro_count * n_ctx, rows),
+        seq_lengths,
+        a_gain,
+        frequency,
+        (w_query, w_key, w_value, w_out, w_gate, w_up, w_down),
+        n_ctx,
+        head,
+        kv_heads,
+        0,
+    )
     both = range(micro_count)
     last = micro_count - 1
-    sorted_normed = [nn(orders[b][1], normed[b]).astype(BF16) for b in both]
-    projected = [
-        project_qkv(
-            sorted_normed[b], qkv_w, orders[b][2], orders[b][3], q_gain, k_gain, heads, kv_heads
+    orders = [
+        (
+            to_slot[b],
+            to_sorted[b],
+            attention_marks(
+                in_order[b * n_ctx : (b + 1) * n_ctx], newest[b], oldest[b], n_ctx, heads // kv_heads
+            ),
         )
         for b in both
     ]
-    kv_own = after([p[1] for p in projected], projected[last][0])
-    (kv_first,) = gather_ctx([kv_own[0]], n_ctx, 1)
+    query, kv_own, raw = project_qkv(
+        sorted_normed, qkv_w, cosine, sine, q_gain, k_gain, heads, kv_heads
+    )
+    kv_first = gather_ctx(kv_own, 0, n_ctx, 1)
     kv_all = [kv_first.reshape(n_ctx, rows, -1)]
     mlp_w = lax.all_gather(after(mlp_own, kv_first), "ctx", axis=0, tiled=True)
 
     def forward(b):
-        return attend_forward(projected[b][0], kv_all[b], orders[b][4], head, kv_heads)
+        return attend_forward(query, b, kv_all[b], orders[b][2], head, kv_heads)
 
     def out_line(b):
-        return attn_out_line(attended[b][0], orders[b][0], out_w, One(hidden_in, b), m_gain)
+        return attn_out_line(attended[b][0], One(to_slot, b), out_w, One(hidden_in, b), m_gain)
 
     def middle_line(b):
         return middle_back_line(fed[b][4], One(cotangent, b), middles[b][1], m_gain, out_w)
@@ -1349,7 +1515,7 @@
 
     attended, middles, fed, mids, backs = [], [], [], [], []
     attended.append(forward(0))
-    results = run_jobs(n_tp, out_line(0), [gather_job(kv_own[1], n_ctx)], 2, 40, "attn_out_gather")
+    results = run_jobs(n_tp, out_line(0), [gather_job(One(kv_own, 1), n_ctx)], 2, 40, "attn_out_gather")
     middles.append(results[:3])
     kv_all.append(results[3].reshape(n_ctx, rows, -1))
     attended.append(forward(1))
@@ -1363,12 +1529,11 @@
     layer_out = jnp.stack(lax.psum([fed[b][3] for b in both], "tp"))
 
     def backward(b, grad):
-        q, unused, raw = projected[b]
-        to_slot, to_sorted, cosine, sine, marks = orders[b]
-        g_mixed = nn(to_sorted, grad).astype(BF16)
+        unused, sorting, marks = orders[b]
+        g_mixed = nn(sorting, grad).astype(BF16)
         mixed_full, mass = attended[b]
         return attend_backward(
-            q, kv_all[b], marks, g_mixed, mixed_full, mass, raw, cosine, sine, q_gain, head, kv_heads
+            query, b, kv_all[b], marks, g_mixed, mixed_full, mass, raw, cosine, sine, q_gain, head, kv_heads
         )
 
     backs.append(backward(0, mids[0][1]))
@@ -1403,11 +1568,11 @@
     backs.append(backward(1, mids[1][1]))
 
     def key_part(b, dkv):
-        return key_back(dkv, projected[b][2], orders[b][2], orders[b][3], k_gain, kv_heads)
+        return key_back(dkv, b, raw, cosine, sine, k_gain, kv_heads)
 
     def in_line(b, gkv):
         return input_back_line(
-            backs[b][0], gkv, orders[b][0], qkv_w, One(hidden_in, b), mids[b][0], a_gain
+            backs[b][0], gkv, One(to_slot, b), qkv_w, One(hidden_in, b), mids[b][0], a_gain
         )
 
     gkv_first, dk_gain_first = key_part(0, after(dkv_first, backs[1][0]))
@@ -1424,7 +1589,7 @@
     tile = min(512, 2 * kv_heads * head, queries)
     gkvs = [gkv_first, gkv_last]
     attn_grads = weight_grads(
-        [sorted_normed[b] for b in both] + [mids[b][0] for b in both],
+        [One(sorted_normed, b) for b in both] + [mids[b][0] for b in both],
         [
             (tuple(both), [backs[b][0] for b in both]),
             (tuple(both), [gkvs[b] for b in both]),

time: 731 us -> 711 us (0.973)
  Pallas kernels: 615 us -> 635 us
  other arithmetic: 35.7 us -> 18.9 us
  local copies, waits for them, and re-layouts: 45.3 us -> 31.7 us
    pallas_call x4 -> x3, Pallas kernels: 61.8 us -> 71.9 us  [the longest x1 38.1 us: begin(): pl.pallas_call(functools.partial(begin_kernel, n_ctx, head, kv_heads), ou...]
    pallas_call x2, Pallas kernels: 26.2 us -> 35.1 us  [attend_forward(): pl.pallas_call(functools.partial(forward_kernel, head, kv_heads), grid_sp...]
    unnamed x140 -> x64, local copies, waits for them, and re-layouts: 25.6 us -> 16.8 us
  transfers between devices with their start and end apart: 3 -> 3, of which waited for: 2 -> 0; matrix products, arithmetic and copies ran while one was open for 4% -> 4% of each run, Pallas kernels for 59% -> 62%
where the time goes in v4:
time: 711 us; the launch traced here: 703 us
  Pallas kernels  635 us (89%)
  local copies, waits for them, and re-layouts  31.7 us (4%)
  other arithmetic  18.9 us (3%)
  between operations  14.7 us (2%)
    pallas_call x6, Pallas kernels, run_jobs(): pl.pallas_call(kernel, out_shape=[out[0] for part in parts for out in par...  441 us
    pallas_call x2, Pallas kernels, attend_backward(): pl.pallas_call(functools.partial(backward_kernel, head, kv_heads), grid_s...  61.9 us
    pallas_call x1, Pallas kernels, begin(): pl.pallas_call(functools.partial(begin_kernel, n_ctx, head, kv_heads), ou...  38.1 us
    pallas_call x2, Pallas kernels, attend_forward(): pl.pallas_call(functools.partial(forward_kernel, head, kv_heads), grid_sp...  35.1 us
    pallas_call x1, Pallas kernels, gather_ctx(): pl.pallas_call(functools.partial(gather_kernel, index, n_ctx), out_shape=...  24 us
    unnamed x64, local copies, waits for them, and re-layouts  16.8 us
  transfers between devices with their start and end apart: 3, of which 0 were waited for; matrix products, arithmetic and copies ran while one was open for 4% of the time, Pallas kernels for 62%

profile of v4, /device:TPU:0, one launch (start us, length us, event | category | flops | bytes accessed | tf_op | source)
XLA Modules:
  0.0 702.8 jit_solution(12632816914259156146)
XLA Ops:
  7.2 1.4 reshape.104.order_ref
  8.7 1.2 pad_maximum_fusion.3.frequency_ref
  10.0 38.1 %begin.1 = (bf16[2048,1024]{1,0:T(8,128)(2,1)}, bf16[2048,512]{1,0:T(8,128)(2,1)}, bf16[256,4608]{1,0:T(8,128)(2,1)}, bf16[2,512,2048]{2,1,0:T(8,128)(2,1)}, bf1...) custom-call(bf16[2,512,2048]{2,1,0:T(8,128)(2,1)} %refs_4_.3, ...), custom_call_target="tpu_custom_call" | custom-call | tf_op jit(solution)/shard_map/begin/pallas_call | solution.py:316
  48.0 9.8 %project_qkv.1 = (bf16[2,512,512]{2,1,0:T(8,128)(2,1)}, bf16[2,512,512]{2,1,0:T(8,128)(2,1)}, f32[2,512,768]{2,1,0:T(8,128)}) custom-call(bf16[2,512,2048]{2,1,0:T(8,128)(2,1)} %get-tuple-element.78.x_ref.refs_0_.refs_1_, bf16[2048,1024]{1,0:T(8,128)(2,1)} %get-tuple-element.79.w_ref.refs_3_, f32[2,512,128]{2,1,0:T(8,128)} %get-tuple-element.80.cos_ref, ...), custom_call_target="tpu_custom_call" | custom-call | tf_op jit(solution)/shard_map/project_qkv/pallas_call | solution.py:378
  57.8 24.0 %gather_ctx.1 = bf16[4096,512]{1,0:T(8,128)(2,1)} custom-call(bf16[2,512,512]{2,1,0:T(8,128)(2,1)} %get-tuple-element.83.source_ref.refs_5_), custom_call_target="tpu_custom_call" | custom-call | tf_op jit(solution)/shard_map/gather_ctx/pallas_call | solution.py:167
  82.2 0.7 copy-done.20
  83.0 1.1 slice_bitcast_fusion.4
  85.0 0.7 reshape.110.pk_ref
  86.2 0.7 fusion.7.hi_ref
  86.9 0.7 fusion.6.lo_ref
  87.6 19.9 %attend_forward.2 = (f32[512,512]{1,0:T(8,128)}, f32[2,2,512]{2,1,0:T(2,128)}) custom-call(s32[2]{0:T(128)} %fusion.6.lo_ref, s32[2]{0:T(128)} %fusion.7.hi_ref, bf16[2,512,512]{2,1,0:T(8,128)(2,1)} %get-tuple-element.82.q_ref, bf16[8,512,512]{2,1,0:T(8,128)(2,1)} %bitcast.61, s32[8,1,512]{2,1,0:T(1,128)} %reshape.108.pk_ref, ...), custom_call_target="tpu_custom_call" | custom-call | tf_op jit(solution)/shard_map/attend_forward/pallas_call | solution.py:460
  107.6 1.2 copy-done.9
  108.8 1.2 copy-done.10
  110.0 64.3 %attn_out_gather.1 = (bf16[512,512]{1,0:T(8,128)(2,1)S(1)}, bf16[512,2048]{1,0:T(8,128)(2,1)S(1)}, bf16[512,2048]{1,0:T(8,128)(2,1)S(1)}, bf16[4096,512]{1,0:T(8,128)(2,1)S(1)}) custom-call(f32[512,512]{1,0:T(8,128)S(1)} %copy-done.9, bf16[2,512,512]{2,1,0:T(8,128)(2,1)S(1)} %copy-done.3, bf16[2048,512]{1,0:T(8,128)(2,1)S(1)} %copy-done.1, ...), custom_call_target="tpu_custom_call" | custom-call | tf_op jit(solution)/shard_map/attn_out_gather/pallas_call | solution.py:746
  174.4 2.0 copy-done.2
  176.4 1.3 copy-done.7
  177.7 1.3 copy-done.8
  179.0 0.8 copy-done.13
  180.3 0.7 fusion.5.hi_ref
  181.0 0.7 fusion.4.lo_ref
  181.7 15.2 %attend_forward.3 = (f32[512,512]{1,0:T(8,128)}, f32[2,2,512]{2,1,0:T(2,128)}) custom-call(s32[2]{0:T(128)} %fusion.4.lo_ref, s32[2]{0:T(128)} %fusion.5.hi_ref, bf16[2,512,512]{2,1,0:T(8,128)(2,1)} %get-tuple-element.82.q_ref, bf16[8,512,512]{2,1,0:T(8,128)(2,1)} %bitcast.52, s32[8,1,512]{2,1,0:T(1,128)} %reshape.110.pk_ref, ...), custom_call_target="tpu_custom_call" | custom-call | tf_op jit(solution)/shard_map/attend_forward/pallas_call | solution.py:460
  196.9 62.8 %attn_out_mlp.1 = (bf16[512,512]{1,0:T(8,128)(2,1)}, bf16[512,2048]{1,0:T(8,128)(2,1)}, bf16[512,2048]{1,0:T(8,128)(2,1)}, bf16[512,1536]{1,0:T(8,128)(2,1)}, bf...) custom-call(f32[512,512]{1,0:T(8,128)} %get-tuple-element.88.refs_0_, ...), custom_call_target="tpu_custom_call" | custom-call | tf_op jit(solution)/shard_map/attn_out_mlp/pallas_call | solution.py:746
  259.7 63.5 %middle_back_mlp.1 = (bf16[512,2048]{1,0:T(8,128)(2,1)}, bf16[512,512]{1,0:T(8,128)(2,1)}, f32[1,2048]{1,0:T(1,128)}, bf16[512,1536]{1,0:T(8,128)(2,1)}, bf16[51...) custom-call(bf16[512,2048]{1,0:T(8,128)(2,1)} %get-tuple-element.94.refs_, ...), custom_call_target="tpu_custom_call" | custom-call | tf_op jit(solution)/shard_map/middle_back_mlp/pallas_call | solution.py:746
  324.6 1.2 convolution_convert_fusion.1.g_ref
  325.8 33.3 %attend_backward.2 = (bf16[512,512]{1,0:T(8,128)(2,1)}, bf16[8,512,512]{2,1,0:T(8,128)(2,1)}, f32[1,128]{1,0:T(1,128)}) custom-call(s32[2]{0:T(128)} %fusion.6.lo_ref, s32[2]{0:T(128)} %fusion.7.hi_ref, bf16[2,512,512]{2,1,0:T(8,128)(2,1)} %get-tuple-element.82.q_ref, bf16[8,512,512]{2,1,0:T(8,128)(2,1)} %bitcast.62, s32[8,1,512]{2,1,0:T(1,128)} %reshape.108.pk_ref, ...), custom_call_target="tpu_custom_call" | custom-call | tf_op jit(solution)/shard_map/attend_backward/pallas_call | solution.py:583
  359.1 123.0 %middle_back_weights.1 = (bf16[512,2048]{1,0:T(8,128)(2,1)}, bf16[512,512]{1,0:T(8,128)(2,1)}, f32[1,2048]{1,0:T(1,128)}, bf16[2048,4608]{1,0:T(8,128)(2,1)}, bf16[512,512]{1,0:T(8,128)(2,1)}) custom-call(bf16[512,2048]{1,0:T(8,128)(2,1)} %get-tuple-element.104.refs_0_, bf16[2,512,2048]{2,1,0:T(8,128)(2,1)} %refs_8_.1, ...), custom_call_target="tpu_custom_call", output_to_operand_aliasing={{3}: (15, {})} | custom-call | tf_op jit(solution)/shard_map/middle_back_weights/pallas_call | solution.py:746
  483.4 1.2 convolution_convert_fusion.g_ref
  484.7 28.6 %attend_backward.3 = (bf16[512,512]{1,0:T(8,128)(2,1)}, bf16[8,512,512]{2,1,0:T(8,128)(2,1)}, f32[1,128]{1,0:T(1,128)}) custom-call(s32[2]{0:T(128)} %fusion.4.lo_ref, s32[2]{0:T(128)} %fusion.5.hi_ref, bf16[2,512,512]{2,1,0:T(8,128)(2,1)} %get-tuple-element.82.q_ref, bf16[8,512,512]{2,1,0:T(8,128)(2,1)} %bitcast.53, s32[8,1,512]{2,1,0:T(1,128)} %reshape.110.pk_ref, ...), custom_call_target="tpu_custom_call" | custom-call | tf_op jit(solution)/shard_map/attend_backward/pallas_call | solution.py:583
  513.9 0.8 copy-done.12
  514.7 62.5 %input_back_keys.1 = (bf16[512,2048]{1,0:T(8,128)(2,1)}, f32[1,2048]{1,0:T(1,128)}, bf16[512,512]{1,0:T(8,128)(2,1)}) custom-call(bf16[512,512]{1,0:T(8,128)(2,1)} %get-tuple-element.102.refs_0_.refs_4_, bf16[512,512]{1,0:T(8,128)(2,1)} %copy-done.12, bf16[2,512,512]{2,1,0:T(8,128)(2,1)} %get-tuple-element.85.refs_1_.refs_2_, ...), custom_call_target="tpu_custom_call" | custom-call | tf_op jit(solution)/shard_map/input_back_keys/pallas_call | solution.py:746
  577.2 1.0 copy-done.6
  578.3 1.1 copy-done.15
  579.9 0.8 copy-done.11
  580.7 13.5 %weight_grads.1.refs_7_ = bf16[2048,1536]{1,0:T(8,128)(2,1)} custom-call(bf16[2,512,2048]{2,1,0:T(8,128)(2,1)} %get-tuple-element.78.x_ref.refs_0_.refs_1_, bf16[2,512,2048]{2,1,0:T(8,128)(2,1)} %get-tuple-element.78.x_ref.refs_0_.refs_1_, bf16[512,2048]{1,0:T(8,128)(2,1)} %get-tuple-element.118.refs_5_.refs_2_, ...), custom_call_target="tpu_custom_call" | custom-call | tf_op jit(solution)/shard_map/weight_grads/pallas_call | solution.py:1330
  594.3 65.2 %input_back_weights.1 = (bf16[512,2048]{1,0:T(8,128)(2,1)}, f32[1,2048]{1,0:T(1,128)}, f32[256,1536]{1,0:T(8,128)}) custom-call(bf16[512,512]{1,0:T(8,128)(2,1)} %get-tuple-element.115.refs_5_.refs_0_, bf16[512,512]{1,0:T(8,128)(2,1)} %copy-done.11, bf16[2,512,512]{2,1,0:T(8,128)(2,1)} %get-tuple-element.85.refs_1_.refs_2_, ...), custom_call_target="tpu_custom_call" | custom-call | tf_op jit(solution)/shard_map/input_back_weights/pallas_call | solution.py:746
  659.6 0.7 add.18
  660.4 9.7 %sum_gains.1 = f32[8,128]{1,0:T(8,128)S(1)} custom-call(f32[8,8,128]{2,1,0:T(8,128)S(1)} %concatenate.9.x_ref), custom_call_target="tpu_custom_call" | custom-call | tf_op jit(solution)/shard_map/sum_gains/pallas_call | solution.py:1397
  670.1 2.1 slice_bitcast_fusion.1
  672.2 1.0 copy.47
  673.2 1.2 fusion.9
  674.4 0.7 pad_maximum_fusion.2
  675.1 0.7 pad_maximum_fusion.1
  676.9 5.5 maximum_convert_fusion
  682.4 4.6 pad_maximum_fusion
  687.1 2.2 convert_element_type.31
  689.3 1.3 slice_bitcast_fusion
  690.5 3.2 copy.48
  693.7 2.1 fusion.8
  (98 shorter events, 7.4 us)
Async XLA Ops:
  7.2 189.7 %all-gather.2.cloned.1.call-start = ((), (), s32[]{:S(2)}) async-start(), calls=%async_computation.1 | async-start | bytes 21233664 | tf_op jit(solution)/shard_map/all_gather | solution.py:1502
  81.8 1.0 copy-start.20
  81.8 1.2 copy-start.21
  81.9 2.3 copy-start.22
  81.9 600.5 %all-reduce.3.cloned.1.call-start = ((), (), s32[]{:S(2)}) async-start(), calls=%async_computation.3 | async-start | bytes 8388608 | tf_op jit(solution)/shard_map/psum | solution.py:1529
  87.6 19.9 %copy-start.1 = (bf16[2048,512]{1,0:T(8,128)(2,1)S(1)}, bf16[2048,512]{1,0:T(8,128)(2,1)}, u32[]{:S(2)}) copy-start(bf16[2048,512]{1,0:T(8,128)(2,1)} %get-tuple-element.86.refs_2_.refs_4_) | copy-start | bytes 6291460
  87.6 19.9 %copy-start.3 = (bf16[2,512,512]{2,1,0:T(8,128)(2,1)S(1)}, bf16[2,512,512]{2,1,0:T(8,128)(2,1)}, u32[]{:S(2)}) copy-start(bf16[2,512,512]{2,1,0:T(8,128)(2,1)} %get-tuple-element.85.refs_1_.refs_2_) | copy-start | bytes 3145732
  87.6 19.9 %copy-start.16 = (f32[2048]{0:T(1024)S(1)}, f32[2048]{0:T(1024)}, u32[]{:S(2)}) copy-start(f32[2048]{0:T(1024)} %param.25) | copy-start | bytes 24580
  107.6 1.2 copy-start.9
  108.8 1.2 copy-start.10
  174.4 2.0 copy-start.2
  176.4 1.3 copy-start.7
  177.7 1.3 copy-start.8
  179.0 0.8 copy-start.13
  323.3 1.3 copy-start.26
  323.3 1.4 copy-start.28
  323.3 363.8 %reduce-scatter.2.cloned.1.call-start = ((), (), s32[]{:S(2)}) async-start(), calls=%async_computation.2 | async-start | bytes 21233664 | tf_op jit(solution)/shard_map/reduce_scatter | solution.py:1566
  482.2 1.3 copy-start.27
  484.7 28.7 %copy-start = (f32[2,512,768]{2,1,0:T(8,128)S(1)}, f32[2,512,768]{2,1,0:T(8,128)}, u32[]{:S(2)}) copy-start(f32[2,512,768]{2,1,0:T(8,128)} %get-tuple-element.101.raw_ref) | copy-start | bytes 9437188
  484.7 28.7 %copy-start.4 = (f32[2,512,128]{2,1,0:T(8,128)S(1)}, f32[2,512,128]{2,1,0:T(8,128)}, u32[]{:S(2)}) copy-start(f32[2,512,128]{2,1,0:T(8,128)} %get-tuple-element.80.cos_ref) | copy-start | bytes 1572868
  484.7 28.7 %copy-start.5 = (f32[2,512,128]{2,1,0:T(8,128)S(1)}, f32[2,512,128]{2,1,0:T(8,128)}, u32[]{:S(2)}) copy-start(f32[2,512,128]{2,1,0:T(8,128)} %get-tuple-element.81.sin_ref) | copy-start | bytes 1572868
  484.7 28.7 %copy-start.14 = (bf16[512,512]{1,0:T(8,128)(2,1)S(1)}, bf16[512,512]{1,0:T(8,128)(2,1)}, u32[]{:S(2)}) copy-start(bf16[512,512]{1,0:T(8,128)(2,1)} %get-tuple-element.116.grad_ref) | copy-start | bytes 1572868
  484.7 28.7 %copy-start.17 = (f32[128]{0:T(128)S(1)}, f32[128]{0:T(128)}, u32[]{:S(2)}) copy-start(f32[128]{0:T(128)} %param.23) | copy-start | bytes 1540
  513.9 0.8 copy-start.12
  577.2 1.0 copy-start.6
  578.3 1.1 copy-start.15
  579.9 0.8 copy-start.11
  594.2 65.3 %copy-start.23 = (f32[1,2048]{1,0:T(1,128)S(1)}, f32[1,2048]{1,0:T(1,128)}, u32[]{:S(2)}) copy-start(f32[1,2048]{1,0:T(1,128)} %get-tuple-element.129) | copy-start | bytes 24580
  594.2 65.3 %copy-start.24 = (f32[1,2048]{1,0:T(1,128)S(1)}, f32[1,2048]{1,0:T(1,128)}, u32[]{:S(2)}) copy-start(f32[1,2048]{1,0:T(1,128)} %get-tuple-element.130) | copy-start | bytes 24580
  594.2 65.3 %copy-start.25 = (f32[1,2048]{1,0:T(1,128)S(1)}, f32[1,2048]{1,0:T(1,128)}, u32[]{:S(2)}) copy-start(f32[1,2048]{1,0:T(1,128)} %get-tuple-element.127) | copy-start | bytes 24580
  594.2 66.1 %copy-start.29 = (f32[1,128]{1,0:T(1,128)S(1)}, f32[1,128]{1,0:T(1,128)}, u32[]{:S(2)}) copy-start(f32[1,128]{1,0:T(1,128)} %get-tuple-element.131) | copy-start | bytes 1540
  594.2 66.1 %copy-start.30 = (f32[1,128]{1,0:T(1,128)S(1)}, f32[1,128]{1,0:T(1,128)}, u32[]{:S(2)}) copy-start(f32[1,128]{1,0:T(1,128)} %get-tuple-element.132) | copy-start | bytes 1540
  672.2 4.7 copy-start.19
  690.5 3.2 copy-start.18
Sparse Core Ops, SparseCore 0:
  82.0 112.1 all-gather.1
  323.4 200.3 all-reduce.2
  527.9 157.6 reduce-scatter.1

commit v5 on v4

--- a/solution.py
+++ b/solution.py
@@ -1342,6 +1342,52 @@
         compiler_params=params(60),
         name="weight_grads",
     )(*[source(left) for left in lefts], *rights)
+
+
+def mlp_results_kernel(grads_ref, gate_ref, up_ref, down_ref):
+    units = gate_ref.shape[1]
+    gate_ref[...] = grads_ref[:, :units].astype(F32)
+    up_ref[...] = grads_ref[:, units : 2 * units].astype(F32)
+    down_ref[...] = grads_ref[:, 2 * units :].astype(F32).T
+
+
+def mlp_results(grads):
+    rows, units = grads.shape[0], grads.shape[1] // 3
+    shapes = [(rows, units), (rows, units), (units, rows)]
+    return pl.pallas_call(
+        mlp_results_kernel,
+        grid=(1,),
+        out_shape=[jax.ShapeDtypeStruct(item, F32) for item in shapes],
+        in_specs=[whole(grads.shape)],
+        out_specs=[whole(item) for item in shapes],
+        compiler_params=params(60),
+        name="mlp_results",
+    )(grads)
+
+
+def attn_results_kernel(head, grads_ref, query_ref, key_ref, value_ref, out_ref):
+    at = query_ref.shape[1]
+    query_ref[...] = grads_ref[:, :at]
+    for n in range(key_ref.shape[1] // head):
+        own = slice(n * head, (n + 1) * head)
+        key_ref[:, own] = grads_ref[:, at : at + head]
+        value_ref[:, own] = grads_ref[:, at + head : at + 2 * head]
+        at += 2 * head
+    out_ref[...] = grads_ref[:, at:].T
+
+
+def attn_results(grads, head, queries, keys):
+    rows = grads.shape[0]
+    shapes = [(rows, queries), (rows, keys), (rows, keys), (queries, rows)]
+    return pl.pallas_call(
+        functools.partial(attn_results_kernel, head),
+        grid=(1,),
+        out_shape=[jax.ShapeDtypeStruct(item, F32) for item in shapes],
+        in_specs=[whole(grads.shape)],
+        out_specs=[whole(item) for item in shapes],
+        compiler_params=params(60),
+        name="attn_results",
+    )(grads)
 
 
 def gains_kernel(n_ctx, n_tp, x_ref, out_ref, got, send_sem, recv_sem, line_got, line_send, line_recv):
@@ -1515,7 +1561,7 @@
 
     attended, middles, fed, mids, backs = [], [], [], [], []
     attended.append(forward(0))
-    results = run_jobs(n_tp, out_line(0), [gather_job(One(kv_own, 1), n_ctx)], 2, 40, "attn_out_gather")
+    results = run_jobs(n_tp, out_line(0), [gather_job(One(kv_own, 1), n_ctx)], 2, 60, "attn_out_gather")
     middles.append(results[:3])
     kv_all.append(results[3].reshape(n_ctx, rows, -1))
     attended.append(forward(1))
@@ -1632,27 +1678,24 @@
         8,
     )
 
-    mlp_grads = mlp_grads.astype(F32)
-    at = queries
-    keys, values = [], []
-    for n in range(kv_heads):
-        keys.append(attn_grads[:, at : at + head])
-        values.append(attn_grads[:, at + head : at + 2 * head])
-        at += 2 * head
+    grad_query, grad_key, grad_value, grad_out = attn_results(
+        attn_grads, head, queries, kv_heads * head
+    )
+    grad_gate, grad_up, grad_down = mlp_results(mlp_grads)
     return (
         layer_out,
         jnp.stack(grads_in).astype(F32),
         gains[:share].reshape(-1),
-        attn_grads[:, :queries],
-        jnp.concatenate(keys, axis=1),
-        jnp.concatenate(values, axis=1),
+        grad_query,
+        grad_key,
+        grad_value,
         gains[4],
         gains[5],
-        attn_grads[:, at:].T,
+        grad_out,
         gains[share : 2 * share].reshape(-1),
-        mlp_grads[:, :units],
-        mlp_grads[:, units : 2 * units],
-        mlp_grads[:, 2 * units :].T,
+        grad_gate,
+        grad_up,
+        grad_down,
     )
 
 

time: 711 us -> 703 us (0.989)
  local copies, waits for them, and re-layouts: 31.7 us -> 13 us
  Pallas kernels: 635 us -> 647 us
    unnamed x64 -> x42, local copies, waits for them, and re-layouts: 16.8 us -> 4.63 us
  transfers between devices with their start and end apart: 3 -> 3, of which waited for: 0 -> 0; matrix products, arithmetic and copies ran while one was open for 4% -> 3% of each run, Pallas kernels for 62% -> 64%
where the time goes in v5:
time: 703 us; the launch traced here: 693 us
  Pallas kernels  647 us (92%)
  other arithmetic  15.3 us (2%)
  between operations  14.7 us (2%)
  local copies, waits for them, and re-layouts  13 us (2%)
    pallas_call x6, Pallas kernels, run_jobs(): pl.pallas_call(kernel, out_shape=[out[0] for part in parts for out in par...  442 us
    pallas_call x2, Pallas kernels, attend_backward(): pl.pallas_call(functools.partial(backward_kernel, head, kv_heads), grid_s...  66.1 us
    pallas_call x1, Pallas kernels, begin(): pl.pallas_call(functools.partial(begin_kernel, n_ctx, head, kv_heads), ou...  38 us
    pallas_call x2, Pallas kernels, attend_forward(): pl.pallas_call(functools.partial(forward_kernel, head, kv_heads), grid_sp...  36.7 us
    pallas_call x1, Pallas kernels, gather_ctx(): pl.pallas_call(functools.partial(gather_kernel, index, n_ctx), out_shape=...  24 us
  transfers between devices with their start and end apart: 3, of which 0 were waited for; matrix products, arithmetic and copies ran while one was open for 3% of the time, Pallas kernels for 64%

profile of v5, /device:TPU:0, one launch (start us, length us, event | category | flops | bytes accessed | tf_op | source)
XLA Modules:
  0.0 693.0 jit_solution(7128873157694149655)
XLA Ops:
  7.2 1.4 reshape.104.order_ref
  8.7 1.2 pad_maximum_fusion.1.frequency_ref
  10.0 38.0 %begin.1 = (bf16[2048,1024]{1,0:T(8,128)(2,1)}, bf16[2048,512]{1,0:T(8,128)(2,1)}, bf16[256,4608]{1,0:T(8,128)(2,1)}, bf16[2,512,2048]{2,1,0:T(8,128)(2,1)}, bf1...) custom-call(bf16[2,512,2048]{2,1,0:T(8,128)(2,1)} %refs_4_.3, ...), custom_call_target="tpu_custom_call" | custom-call | tf_op jit(solution)/shard_map/begin/pallas_call | solution.py:316
  48.0 9.7 %project_qkv.1 = (bf16[2,512,512]{2,1,0:T(8,128)(2,1)}, bf16[2,512,512]{2,1,0:T(8,128)(2,1)}, f32[2,512,768]{2,1,0:T(8,128)}) custom-call(bf16[2,512,2048]{2,1,0:T(8,128)(2,1)} %get-tuple-element.85.x_ref.refs_0_.refs_1_, bf16[2048,1024]{1,0:T(8,128)(2,1)} %get-tuple-element.86.w_ref.refs_3_, f32[2,512,128]{2,1,0:T(8,128)} %get-tuple-element.87.cos_ref, ...), custom_call_target="tpu_custom_call" | custom-call | tf_op jit(solution)/shard_map/project_qkv/pallas_call | solution.py:378
  57.7 24.0 %gather_ctx.1 = bf16[4096,512]{1,0:T(8,128)(2,1)} custom-call(bf16[2,512,512]{2,1,0:T(8,128)(2,1)} %get-tuple-element.90.source_ref.refs_5_), custom_call_target="tpu_custom_call" | custom-call | tf_op jit(solution)/shard_map/gather_ctx/pallas_call | solution.py:167
  81.8 0.3 all-reduce.3.cloned.1.call-start
  82.1 0.7 copy-done.10
  83.0 1.1 slice_bitcast_fusion.2
  84.2 0.7 reshape.108.pk_ref
  85.0 0.7 reshape.110.pk_ref
  86.0 0.2 slice_reduce_fusion.4
  86.2 0.7 fusion.7.hi_ref
  86.9 0.7 fusion.6.lo_ref
  87.6 19.2 %attend_forward.2 = (f32[512,512]{1,0:T(8,128)}, f32[2,2,512]{2,1,0:T(2,128)}) custom-call(s32[2]{0:T(128)} %fusion.6.lo_ref, s32[2]{0:T(128)} %fusion.7.hi_ref, bf16[2,512,512]{2,1,0:T(8,128)(2,1)} %get-tuple-element.89.q_ref, bf16[8,512,512]{2,1,0:T(8,128)(2,1)} %bitcast.51, s32[8,1,512]{2,1,0:T(1,128)} %reshape.108.pk_ref, ...), custom_call_target="tpu_custom_call" | custom-call | tf_op jit(solution)/shard_map/attend_forward/pallas_call | solution.py:460
  106.8 69.2 %attn_out_gather.1 = (bf16[512,512]{1,0:T(8,128)(2,1)}, bf16[512,2048]{1,0:T(8,128)(2,1)}, bf16[512,2048]{1,0:T(8,128)(2,1)}, bf16[4096,512]{1,0:T(8,128)(2,1)}) custom-call(f32[512,512]{1,0:T(8,128)} %get-tuple-element.91.refs_0_.out_ref, bf16[2,512,512]{2,1,0:T(8,128)(2,1)} %get-tuple-element.92.refs_1_.refs_2_, ...), custom_call_target="tpu_custom_call" | custom-call | tf_op jit(solution)/shard_map/attn_out_gather/pallas_call | solution.py:746
  176.0 0.2 slice_reduce_fusion.10
  176.3 0.2 slice_reduce_fusion.6
  176.5 0.7 fusion.5.hi_ref
  177.2 0.7 fusion.4.lo_ref
  177.9 17.5 %attend_forward.3 = (f32[512,512]{1,0:T(8,128)}, f32[2,2,512]{2,1,0:T(2,128)}) custom-call(s32[2]{0:T(128)} %fusion.4.lo_ref, s32[2]{0:T(128)} %fusion.5.hi_ref, bf16[2,512,512]{2,1,0:T(8,128)(2,1)} %get-tuple-element.89.q_ref, bf16[8,512,512]{2,1,0:T(8,128)(2,1)} %bitcast.53, s32[8,1,512]{2,1,0:T(1,128)} %reshape.110.pk_ref, ...), custom_call_target="tpu_custom_call" | custom-call | tf_op jit(solution)/shard_map/attend_forward/pallas_call | solution.py:460
  195.4 63.2 %attn_out_mlp.1 = (bf16[512,512]{1,0:T(8,128)(2,1)}, bf16[512,2048]{1,0:T(8,128)(2,1)}, bf16[512,2048]{1,0:T(8,128)(2,1)}, bf16[512,1536]{1,0:T(8,128)(2,1)}, bf...) custom-call(f32[512,512]{1,0:T(8,128)} %get-tuple-element.95.refs_0_, ...), custom_call_target="tpu_custom_call" | custom-call | tf_op jit(solution)/shard_map/attn_out_mlp/pallas_call | solution.py:746
  258.6 63.5 %middle_back_mlp.1 = (bf16[512,2048]{1,0:T(8,128)(2,1)}, bf16[512,512]{1,0:T(8,128)(2,1)}, f32[1,2048]{1,0:T(1,128)}, bf16[512,1536]{1,0:T(8,128)(2,1)}, bf16[51...) custom-call(bf16[512,2048]{1,0:T(8,128)(2,1)} %get-tuple-element.101.refs, ...), custom_call_target="tpu_custom_call" | custom-call | tf_op jit(solution)/shard_map/middle_back_mlp/pallas_call | solution.py:746
  322.1 0.6 tile.40.pq_ref
  322.7 0.6 tile.42.sq_ref
  323.4 1.2 convolution_convert_fusion.1.g_ref
  324.6 33.8 %attend_backward.2 = (bf16[512,512]{1,0:T(8,128)(2,1)}, bf16[8,512,512]{2,1,0:T(8,128)(2,1)}, f32[1,128]{1,0:T(1,128)}) custom-call(s32[2]{0:T(128)} %fusion.6.lo_ref, s32[2]{0:T(128)} %fusion.7.hi_ref, bf16[2,512,512]{2,1,0:T(8,128)(2,1)} %get-tuple-element.89.q_ref, bf16[8,512,512]{2,1,0:T(8,128)(2,1)} %bitcast.52, s32[8,1,512]{2,1,0:T(1,128)} %reshape.108.pk_ref, ...), custom_call_target="tpu_custom_call" | custom-call | tf_op jit(solution)/shard_map/attend_backward/pallas_call | solution.py:583
  358.4 118.2 %middle_back_weights.1 = (bf16[512,2048]{1,0:T(8,128)(2,1)}, bf16[512,512]{1,0:T(8,128)(2,1)}, f32[1,2048]{1,0:T(1,128)}, bf16[2048,4608]{1,0:T(8,128)(2,1)}, bf16[512,512]{1,0:T(8,128)(2,1)}) custom-call(bf16[512,2048]{1,0:T(8,128)(2,1)} %get-tuple-element.111.refs_0_, bf16[2,512,2048]{2,1,0:T(8,128)(2,1)} %refs_8_.1, ...), custom_call_target="tpu_custom_call", output_to_operand_aliasing={{3}: (15, {})} | custom-call | tf_op jit(solution)/shard_map/middle_back_weights/pallas_call | solution.py:746
  476.7 0.6 tile.44.pq_ref
  477.3 0.6 tile.46.sq_ref
  477.9 1.2 convolution_convert_fusion.g_ref
  479.1 32.3 %attend_backward.3 = (bf16[512,512]{1,0:T(8,128)(2,1)}, bf16[8,512,512]{2,1,0:T(8,128)(2,1)}, f32[1,128]{1,0:T(1,128)}) custom-call(s32[2]{0:T(128)} %fusion.4.lo_ref, s32[2]{0:T(128)} %fusion.5.hi_ref, bf16[2,512,512]{2,1,0:T(8,128)(2,1)} %get-tuple-element.89.q_ref, bf16[8,512,512]{2,1,0:T(8,128)(2,1)} %bitcast.54, s32[8,1,512]{2,1,0:T(1,128)} %reshape.110.pk_ref, ...), custom_call_target="tpu_custom_call" | custom-call | tf_op jit(solution)/shard_map/attend_backward/pallas_call | solution.py:583
  511.4 0.6 key_back.2
  512.0 0.8 copy-done.5
  512.8 64.5 %input_back_keys.1 = (bf16[512,2048]{1,0:T(8,128)(2,1)}, f32[1,2048]{1,0:T(1,128)}, bf16[512,512]{1,0:T(8,128)(2,1)}) custom-call(bf16[512,512]{1,0:T(8,128)(2,1)} %get-tuple-element.109.refs_0_.refs_4_, bf16[512,512]{1,0:T(8,128)(2,1)} %copy-done.5, bf16[2,512,512]{2,1,0:T(8,128)(2,1)} %get-tuple-element.92.refs_1_.refs_2_, ...), custom_call_target="tpu_custom_call" | custom-call | tf_op jit(solution)/shard_map/input_back_keys/pallas_call | solution.py:746
  577.3 1.0 copy-done.3
  578.4 1.0 copy-done.7
  579.4 0.6 key_back.3
  580.0 0.8 copy-done.4
  580.8 13.3 %weight_grads.1.refs_7_ = bf16[2048,1536]{1,0:T(8,128)(2,1)} custom-call(bf16[2,512,2048]{2,1,0:T(8,128)(2,1)} %get-tuple-element.85.x_ref.refs_0_.refs_1_, bf16[2,512,2048]{2,1,0:T(8,128)(2,1)} %get-tuple-element.85.x_ref.refs_0_.refs_1_, bf16[512,2048]{1,0:T(8,128)(2,1)} %get-tuple-element.125.refs_5_.refs_2_, ...), custom_call_target="tpu_custom_call" | custom-call | tf_op jit(solution)/shard_map/weight_grads/pallas_call | solution.py:1330
  594.1 63.1 %input_back_weights.1 = (bf16[512,2048]{1,0:T(8,128)(2,1)}, f32[1,2048]{1,0:T(1,128)}, f32[256,1536]{1,0:T(8,128)}) custom-call(bf16[512,512]{1,0:T(8,128)(2,1)} %get-tuple-element.122.refs_5_.refs_0_, bf16[512,512]{1,0:T(8,128)(2,1)} %copy-done.4, bf16[2,512,512]{2,1,0:T(8,128)(2,1)} %get-tuple-element.92.refs_1_.refs_2_, ...), custom_call_target="tpu_custom_call" | custom-call | tf_op jit(solution)/shard_map/input_back_weights/pallas_call | solution.py:746
  657.3 0.7 add.18
  658.2 9.6 %sum_gains.1 = f32[8,128]{1,0:T(8,128)S(1)} custom-call(f32[8,8,128]{2,1,0:T(8,128)S(1)} %concatenate.3.x_ref), custom_call_target="tpu_custom_call" | custom-call | tf_op jit(solution)/shard_map/sum_gains/pallas_call | solution.py:1443
  667.8 2.7 attn_results.1
  670.5 0.5 slice_bitcast_fusion.6
  671.0 0.6 slice_bitcast_fusion.4
  671.6 5.5 maximum_convert_fusion
  677.1 4.6 pad_maximum_fusion
  681.7 4.2 mlp_results.1
  (71 shorter events, 1.2 us)
Async XLA Ops:
  7.2 188.2 %all-gather.2.cloned.1.call-start = ((), (), s32[]{:S(2)}) async-start(), calls=%async_computation.1 | async-start | bytes 21233664 | tf_op jit(solution)/shard_map/all_gather | solution.py:1548
  81.8 1.0 copy-start.10
  81.8 1.2 copy-start.11
  81.8 2.3 copy-start.12
  81.8 595.3 %all-reduce.3.cloned.1.call-start = ((), (), s32[]{:S(2)}) async-start(), calls=%async_computation.3 | async-start | bytes 8388608 | tf_op jit(solution)/shard_map/psum | solution.py:1575
  322.0 1.3 copy-start.16
  322.0 1.4 copy-start.18
  322.1 359.7 %reduce-scatter.2.cloned.1.call-start = ((), (), s32[]{:S(2)}) async-start(), calls=%async_computation.2 | async-start | bytes 21233664 | tf_op jit(solution)/shard_map/reduce_scatter | solution.py:1612
  476.6 1.3 copy-start.17
  479.1 32.3 %copy-start = (f32[2,512,768]{2,1,0:T(8,128)S(1)}, f32[2,512,768]{2,1,0:T(8,128)}, u32[]{:S(2)}) copy-start(f32[2,512,768]{2,1,0:T(8,128)} %get-tuple-element.108.raw_ref) | copy-start | bytes 9437188
  479.1 32.3 %copy-start.1 = (f32[2,512,128]{2,1,0:T(8,128)S(1)}, f32[2,512,128]{2,1,0:T(8,128)}, u32[]{:S(2)}) copy-start(f32[2,512,128]{2,1,0:T(8,128)} %get-tuple-element.87.cos_ref) | copy-start | bytes 1572868
  479.1 32.3 %copy-start.2 = (f32[2,512,128]{2,1,0:T(8,128)S(1)}, f32[2,512,128]{2,1,0:T(8,128)}, u32[]{:S(2)}) copy-start(f32[2,512,128]{2,1,0:T(8,128)} %get-tuple-element.88.sin_ref) | copy-start | bytes 1572868
  479.1 32.3 %copy-start.6 = (bf16[512,512]{1,0:T(8,128)(2,1)S(1)}, bf16[512,512]{1,0:T(8,128)(2,1)}, u32[]{:S(2)}) copy-start(bf16[512,512]{1,0:T(8,128)(2,1)} %get-tuple-element.123.grad_ref) | copy-start | bytes 1572868
  479.1 32.3 %copy-start.8 = (f32[128]{0:T(128)S(1)}, f32[128]{0:T(128)}, u32[]{:S(2)}) copy-start(f32[128]{0:T(128)} %param.23) | copy-start | bytes 1540
  512.0 0.8 copy-start.5
  577.3 1.0 copy-start.3
  578.4 1.0 copy-start.7
  580.0 0.8 copy-start.4
  594.1 63.2 %copy-start.13 = (f32[1,2048]{1,0:T(1,128)S(1)}, f32[1,2048]{1,0:T(1,128)}, u32[]{:S(2)}) copy-start(f32[1,2048]{1,0:T(1,128)} %get-tuple-element.136) | copy-start | bytes 24580
  594.1 63.2 %copy-start.14 = (f32[1,2048]{1,0:T(1,128)S(1)}, f32[1,2048]{1,0:T(1,128)}, u32[]{:S(2)}) copy-start(f32[1,2048]{1,0:T(1,128)} %get-tuple-element.137) | copy-start | bytes 24580
  594.1 63.2 %copy-start.15 = (f32[1,2048]{1,0:T(1,128)S(1)}, f32[1,2048]{1,0:T(1,128)}, u32[]{:S(2)}) copy-start(f32[1,2048]{1,0:T(1,128)} %get-tuple-element.134) | copy-start | bytes 24580
  594.1 64.0 %copy-start.19 = (f32[1,128]{1,0:T(1,128)S(1)}, f32[1,128]{1,0:T(1,128)}, u32[]{:S(2)}) copy-start(f32[1,128]{1,0:T(1,128)} %get-tuple-element.138) | copy-start | bytes 1540
  594.1 64.0 %copy-start.20 = (f32[1,128]{1,0:T(1,128)S(1)}, f32[1,128]{1,0:T(1,128)}, u32[]{:S(2)}) copy-start(f32[1,128]{1,0:T(1,128)} %get-tuple-element.139) | copy-start | bytes 1540
  594.1 77.5 %copy-start.9 = (bf16[512,2048]{1,0:T(8,128)(2,1)S(1)}, bf16[512,2048]{1,0:T(8,128)(2,1)}, u32[]{:S(2)}) copy-start(bf16[512,2048]{1,0:T(8,128)(2,1)} %get-tuple-element.127) | copy-start | bytes 6291460
Sparse Core Ops, SparseCore 0:
  82.0 112.3 all-gather.1
  322.2 196.8 all-reduce.2
  523.1 153.9 reduce-scatter.1

commit v6 on v5

--- a/solution.py
+++ b/solution.py
@@ -1041,7 +1041,7 @@
         def hook(s):
             for d in range(1, chips):
 
-                @pl.when(s == CHUNKS - 2 * chips + 2 * d)
+                @pl.when(s == (CHUNKS + d if d > 2 else CHUNKS - 5 + d))
                 def _(d=d):
                     relay(0, d)
 

time: 703 us -> 701 us (level)
  waiting for transfers between devices: 0.06 us -> 13 us
  Pallas kernels: 647 us -> 635 us
    all_gather x1, waiting for transfers between devices: 0.01 us -> 11.6 us  [on_device(): mlp_w = lax.all_gather(after(mlp_own, kv_first), 'ctx', axis=0, tiled=True)]
    pallas_call x2, Pallas kernels: 66.1 us -> 58.9 us  [attend_backward(): pl.pallas_call(functools.partial(backward_kernel, head, kv_heads), grid_s...]
  transfers between devices with their start and end apart: 3 -> 3, of which waited for: 0 -> 2; matrix products, arithmetic and copies ran while one was open for 3% -> 3% of each run, Pallas kernels for 64% -> 62%
where the time goes in v6:
time: 701 us; the launch traced here: 694 us
  Pallas kernels  635 us (91%)
  other arithmetic  15.3 us (2%)
  between operations  14.7 us (2%)
  local copies, waits for them, and re-layouts  13 us (2%)
  waiting for transfers between devices  13 us (2%)
    pallas_call x6, Pallas kernels, run_jobs(): pl.pallas_call(kernel, out_shape=[out[0] for part in parts for out in par...  441 us
    pallas_call x2, Pallas kernels, attend_backward(): pl.pallas_call(functools.partial(backward_kernel, head, kv_heads), grid_s...  58.9 us
    pallas_call x1, Pallas kernels, begin(): pl.pallas_call(functools.partial(begin_kernel, n_ctx, head, kv_heads), ou...  38 us
    pallas_call x2, Pallas kernels, attend_forward(): pl.pallas_call(functools.partial(forward_kernel, head, kv_heads), grid_sp...  32.6 us
    pallas_call x1, Pallas kernels, gather_ctx(): pl.pallas_call(functools.partial(gather_kernel, index, n_ctx), out_shape=...  24 us
  transfers between devices with their start and end apart: 3, of which 2 were waited for; matrix products, arithmetic and copies ran while one was open for 3% of the time, Pallas kernels for 62%

profile of v6, /device:TPU:0, one launch (start us, length us, event | category | flops | bytes accessed | tf_op | source)
XLA Modules:
  0.0 693.8 jit_solution(14143346110813750812)
XLA Ops:
  7.2 1.4 reshape.104.order_ref
  8.7 1.2 pad_maximum_fusion.1.frequency_ref
  10.0 38.0 %begin.1 = (bf16[2048,1024]{1,0:T(8,128)(2,1)}, bf16[2048,512]{1,0:T(8,128)(2,1)}, bf16[256,4608]{1,0:T(8,128)(2,1)}, bf16[2,512,2048]{2,1,0:T(8,128)(2,1)}, bf1...) custom-call(bf16[2,512,2048]{2,1,0:T(8,128)(2,1)} %refs_4_.3, ...), custom_call_target="tpu_custom_call" | custom-call | tf_op jit(solution)/shard_map/begin/pallas_call | solution.py:316
  48.0 9.7 %project_qkv.1 = (bf16[2,512,512]{2,1,0:T(8,128)(2,1)}, bf16[2,512,512]{2,1,0:T(8,128)(2,1)}, f32[2,512,768]{2,1,0:T(8,128)}) custom-call(bf16[2,512,2048]{2,1,0:T(8,128)(2,1)} %get-tuple-element.85.x_ref.refs_0_.refs_1_, bf16[2048,1024]{1,0:T(8,128)(2,1)} %get-tuple-element.86.w_ref.refs_3_, f32[2,512,128]{2,1,0:T(8,128)} %get-tuple-element.87.cos_ref, ...), custom_call_target="tpu_custom_call" | custom-call | tf_op jit(solution)/shard_map/project_qkv/pallas_call | solution.py:378
  57.7 24.0 %gather_ctx.1 = bf16[4096,512]{1,0:T(8,128)(2,1)} custom-call(bf16[2,512,512]{2,1,0:T(8,128)(2,1)} %get-tuple-element.90.source_ref.refs_5_), custom_call_target="tpu_custom_call" | custom-call | tf_op jit(solution)/shard_map/gather_ctx/pallas_call | solution.py:167
  81.8 0.3 all-reduce.3.cloned.1.call-start
  82.1 0.7 copy-done.10
  83.0 1.1 slice_bitcast_fusion.2
  84.2 0.7 reshape.108.pk_ref
  85.0 0.7 reshape.110.pk_ref
  86.2 0.7 fusion.7.hi_ref
  86.9 0.7 fusion.6.lo_ref
  87.6 16.1 %attend_forward.2 = (f32[512,512]{1,0:T(8,128)}, f32[2,2,512]{2,1,0:T(2,128)}) custom-call(s32[2]{0:T(128)} %fusion.6.lo_ref, s32[2]{0:T(128)} %fusion.7.hi_ref, bf16[2,512,512]{2,1,0:T(8,128)(2,1)} %get-tuple-element.89.q_ref, bf16[8,512,512]{2,1,0:T(8,128)(2,1)} %bitcast.51, s32[8,1,512]{2,1,0:T(1,128)} %reshape.108.pk_ref, ...), custom_call_target="tpu_custom_call" | custom-call | tf_op jit(solution)/shard_map/attend_forward/pallas_call | solution.py:460
  103.7 63.4 %attn_out_gather.1 = (bf16[512,512]{1,0:T(8,128)(2,1)}, bf16[512,2048]{1,0:T(8,128)(2,1)}, bf16[512,2048]{1,0:T(8,128)(2,1)}, bf16[4096,512]{1,0:T(8,128)(2,1)}) custom-call(f32[512,512]{1,0:T(8,128)} %get-tuple-element.91.refs_0_.out_ref, bf16[2,512,512]{2,1,0:T(8,128)(2,1)} %get-tuple-element.92.refs_1_.refs_2_, ...), custom_call_target="tpu_custom_call" | custom-call | tf_op jit(solution)/shard_map/attn_out_gather/pallas_call | solution.py:746
  167.4 0.2 slice_reduce_fusion.6
  167.6 0.7 fusion.5.hi_ref
  168.3 0.7 fusion.4.lo_ref
  169.0 16.5 %attend_forward.3 = (f32[512,512]{1,0:T(8,128)}, f32[2,2,512]{2,1,0:T(2,128)}) custom-call(s32[2]{0:T(128)} %fusion.4.lo_ref, s32[2]{0:T(128)} %fusion.5.hi_ref, bf16[2,512,512]{2,1,0:T(8,128)(2,1)} %get-tuple-element.89.q_ref, bf16[8,512,512]{2,1,0:T(8,128)(2,1)} %bitcast.53, s32[8,1,512]{2,1,0:T(1,128)} %reshape.110.pk_ref, ...), custom_call_target="tpu_custom_call" | custom-call | tf_op jit(solution)/shard_map/attend_forward/pallas_call | solution.py:460
  185.5 11.6 %all-gather.2.cloned.1.call-done.refs_8_.refs_15_ = bf16[2048,4608]{1,0:T(8,128)(2,1)} async-done(((bf16[256,4608]{1,0:T(8,128)(2,1)}), bf16[2048,4608]{1,0:T(8,128)(2,1)}) %all-gather.2.cloned.1.call-update) | async-done | bytes 18874384 | tf_op jit(solution)/shard_map/all_gather | solution.py:1548
  197.1 63.5 %attn_out_mlp.1 = (bf16[512,512]{1,0:T(8,128)(2,1)}, bf16[512,2048]{1,0:T(8,128)(2,1)}, bf16[512,2048]{1,0:T(8,128)(2,1)}, bf16[512,1536]{1,0:T(8,128)(2,1)}, bf...) custom-call(f32[512,512]{1,0:T(8,128)} %get-tuple-element.95.refs_0_, ...), custom_call_target="tpu_custom_call" | custom-call | tf_op jit(solution)/shard_map/attn_out_mlp/pallas_call | solution.py:746
  260.5 63.5 %middle_back_mlp.1 = (bf16[512,2048]{1,0:T(8,128)(2,1)}, bf16[512,512]{1,0:T(8,128)(2,1)}, f32[1,2048]{1,0:T(1,128)}, bf16[512,1536]{1,0:T(8,128)(2,1)}, bf16[51...) custom-call(bf16[512,2048]{1,0:T(8,128)(2,1)} %get-tuple-element.101.refs, ...), custom_call_target="tpu_custom_call" | custom-call | tf_op jit(solution)/shard_map/middle_back_mlp/pallas_call | solution.py:746
  324.1 0.6 tile.40.pq_ref
  324.7 0.6 tile.42.sq_ref
  325.4 1.2 convolution_convert_fusion.1.g_ref
  326.6 28.5 %attend_backward.2 = (bf16[512,512]{1,0:T(8,128)(2,1)}, bf16[8,512,512]{2,1,0:T(8,128)(2,1)}, f32[1,128]{1,0:T(1,128)}) custom-call(s32[2]{0:T(128)} %fusion.6.lo_ref, s32[2]{0:T(128)} %fusion.7.hi_ref, bf16[2,512,512]{2,1,0:T(8,128)(2,1)} %get-tuple-element.89.q_ref, bf16[8,512,512]{2,1,0:T(8,128)(2,1)} %bitcast.52, s32[8,1,512]{2,1,0:T(1,128)} %reshape.108.pk_ref, ...), custom_call_target="tpu_custom_call" | custom-call | tf_op jit(solution)/shard_map/attend_backward/pallas_call | solution.py:583
  355.2 120.6 %middle_back_weights.1 = (bf16[512,2048]{1,0:T(8,128)(2,1)}, bf16[512,512]{1,0:T(8,128)(2,1)}, f32[1,2048]{1,0:T(1,128)}, bf16[2048,4608]{1,0:T(8,128)(2,1)}, bf16[512,512]{1,0:T(8,128)(2,1)}) custom-call(bf16[512,2048]{1,0:T(8,128)(2,1)} %get-tuple-element.111.refs_0_, bf16[2,512,2048]{2,1,0:T(8,128)(2,1)} %refs_8_.1, ...), custom_call_target="tpu_custom_call", output_to_operand_aliasing={{3}: (15, {})} | custom-call | tf_op jit(solution)/shard_map/middle_back_weights/pallas_call | solution.py:746
  475.8 0.6 tile.44.pq_ref
  476.4 0.6 tile.46.sq_ref
  477.0 1.2 convolution_convert_fusion.g_ref
  478.3 30.4 %attend_backward.3 = (bf16[512,512]{1,0:T(8,128)(2,1)}, bf16[8,512,512]{2,1,0:T(8,128)(2,1)}, f32[1,128]{1,0:T(1,128)}) custom-call(s32[2]{0:T(128)} %fusion.4.lo_ref, s32[2]{0:T(128)} %fusion.5.hi_ref, bf16[2,512,512]{2,1,0:T(8,128)(2,1)} %get-tuple-element.89.q_ref, bf16[8,512,512]{2,1,0:T(8,128)(2,1)} %bitcast.54, s32[8,1,512]{2,1,0:T(1,128)} %reshape.110.pk_ref, ...), custom_call_target="tpu_custom_call" | custom-call | tf_op jit(solution)/shard_map/attend_backward/pallas_call | solution.py:583
  508.7 0.6 key_back.2
  509.3 0.8 copy-done.5
  510.1 65.0 %input_back_keys.1 = (bf16[512,2048]{1,0:T(8,128)(2,1)}, f32[1,2048]{1,0:T(1,128)}, bf16[512,512]{1,0:T(8,128)(2,1)}) custom-call(bf16[512,512]{1,0:T(8,128)(2,1)} %get-tuple-element.109.refs_0_.refs_4_, bf16[512,512]{1,0:T(8,128)(2,1)} %copy-done.5, bf16[2,512,512]{2,1,0:T(8,128)(2,1)} %get-tuple-element.92.refs_1_.refs_2_, ...), custom_call_target="tpu_custom_call" | custom-call | tf_op jit(solution)/shard_map/input_back_keys/pallas_call | solution.py:746
  575.1 1.0 copy-done.3
  576.1 1.1 copy-done.7
  577.2 0.6 key_back.3
  577.8 0.8 copy-done.4
  578.6 13.5 %weight_grads.1.refs_7_ = bf16[2048,1536]{1,0:T(8,128)(2,1)} custom-call(bf16[2,512,2048]{2,1,0:T(8,128)(2,1)} %get-tuple-element.85.x_ref.refs_0_.refs_1_, bf16[2,512,2048]{2,1,0:T(8,128)(2,1)} %get-tuple-element.85.x_ref.refs_0_.refs_1_, bf16[512,2048]{1,0:T(8,128)(2,1)} %get-tuple-element.125.refs_5_.refs_2_, ...), custom_call_target="tpu_custom_call" | custom-call | tf_op jit(solution)/shard_map/weight_grads/pallas_call | solution.py:1330
  592.2 65.1 %input_back_weights.1 = (bf16[512,2048]{1,0:T(8,128)(2,1)}, f32[1,2048]{1,0:T(1,128)}, f32[256,1536]{1,0:T(8,128)}) custom-call(bf16[512,512]{1,0:T(8,128)(2,1)} %get-tuple-element.122.refs_5_.refs_0_, bf16[512,512]{1,0:T(8,128)(2,1)} %copy-done.4, bf16[2,512,512]{2,1,0:T(8,128)(2,1)} %get-tuple-element.92.refs_1_.refs_2_, ...), custom_call_target="tpu_custom_call" | custom-call | tf_op jit(solution)/shard_map/input_back_weights/pallas_call | solution.py:746
  657.4 0.7 add.18
  658.2 9.1 %sum_gains.1 = f32[8,128]{1,0:T(8,128)S(1)} custom-call(f32[8,8,128]{2,1,0:T(8,128)S(1)} %concatenate.3.x_ref), custom_call_target="tpu_custom_call" | custom-call | tf_op jit(solution)/shard_map/sum_gains/pallas_call | solution.py:1443
  667.3 2.7 attn_results.1
  670.0 0.5 slice_bitcast_fusion.6
  670.5 0.6 slice_bitcast_fusion.4
  671.1 5.5 maximum_convert_fusion
  676.6 4.6 pad_maximum_fusion
  681.2 1.4 reduce-scatter.2.cloned.1.call-done.grads_ref
  682.6 4.2 mlp_results.1
  (71 shorter events, 1.6 us)
Async XLA Ops:
  7.2 189.9 %all-gather.2.cloned.1.call-start = ((), (), s32[]{:S(2)}) async-start(), calls=%async_computation.1 | async-start | bytes 21233664 | tf_op jit(solution)/shard_map/all_gather | solution.py:1548
  81.8 1.0 copy-start.10
  81.8 1.2 copy-start.11
  81.8 2.3 copy-start.12
  81.8 594.8 %all-reduce.3.cloned.1.call-start = ((), (), s32[]{:S(2)}) async-start(), calls=%async_computation.3 | async-start | bytes 8388608 | tf_op jit(solution)/shard_map/psum | solution.py:1575
  324.0 1.3 copy-start.16
  324.0 1.4 copy-start.18
  324.1 358.5 %reduce-scatter.2.cloned.1.call-start = ((), (), s32[]{:S(2)}) async-start(), calls=%async_computation.2 | async-start | bytes 21233664 | tf_op jit(solution)/shard_map/reduce_scatter | solution.py:1612
  475.7 1.3 copy-start.17
  478.2 30.4 %copy-start = (f32[2,512,768]{2,1,0:T(8,128)S(1)}, f32[2,512,768]{2,1,0:T(8,128)}, u32[]{:S(2)}) copy-start(f32[2,512,768]{2,1,0:T(8,128)} %get-tuple-element.108.raw_ref) | copy-start | bytes 9437188
  478.2 30.4 %copy-start.1 = (f32[2,512,128]{2,1,0:T(8,128)S(1)}, f32[2,512,128]{2,1,0:T(8,128)}, u32[]{:S(2)}) copy-start(f32[2,512,128]{2,1,0:T(8,128)} %get-tuple-element.87.cos_ref) | copy-start | bytes 1572868
  478.2 30.4 %copy-start.2 = (f32[2,512,128]{2,1,0:T(8,128)S(1)}, f32[2,512,128]{2,1,0:T(8,128)}, u32[]{:S(2)}) copy-start(f32[2,512,128]{2,1,0:T(8,128)} %get-tuple-element.88.sin_ref) | copy-start | bytes 1572868
  478.2 30.4 %copy-start.6 = (bf16[512,512]{1,0:T(8,128)(2,1)S(1)}, bf16[512,512]{1,0:T(8,128)(2,1)}, u32[]{:S(2)}) copy-start(bf16[512,512]{1,0:T(8,128)(2,1)} %get-tuple-element.123.grad_ref) | copy-start | bytes 1572868
  478.2 30.4 %copy-start.8 = (f32[128]{0:T(128)S(1)}, f32[128]{0:T(128)}, u32[]{:S(2)}) copy-start(f32[128]{0:T(128)} %param.23) | copy-start | bytes 1540
  509.3 0.8 copy-start.5
  575.1 1.0 copy-start.3
  576.1 1.1 copy-start.7
  577.8 0.8 copy-start.4
  592.1 65.2 %copy-start.13 = (f32[1,2048]{1,0:T(1,128)S(1)}, f32[1,2048]{1,0:T(1,128)}, u32[]{:S(2)}) copy-start(f32[1,2048]{1,0:T(1,128)} %get-tuple-element.136) | copy-start | bytes 24580
  592.1 65.2 %copy-start.14 = (f32[1,2048]{1,0:T(1,128)S(1)}, f32[1,2048]{1,0:T(1,128)}, u32[]{:S(2)}) copy-start(f32[1,2048]{1,0:T(1,128)} %get-tuple-element.137) | copy-start | bytes 24580
  592.1 65.2 %copy-start.15 = (f32[1,2048]{1,0:T(1,128)S(1)}, f32[1,2048]{1,0:T(1,128)}, u32[]{:S(2)}) copy-start(f32[1,2048]{1,0:T(1,128)} %get-tuple-element.134) | copy-start | bytes 24580
  592.1 65.9 %copy-start.19 = (f32[1,128]{1,0:T(1,128)S(1)}, f32[1,128]{1,0:T(1,128)}, u32[]{:S(2)}) copy-start(f32[1,128]{1,0:T(1,128)} %get-tuple-element.138) | copy-start | bytes 1540
  592.2 65.9 %copy-start.20 = (f32[1,128]{1,0:T(1,128)S(1)}, f32[1,128]{1,0:T(1,128)}, u32[]{:S(2)}) copy-start(f32[1,128]{1,0:T(1,128)} %get-tuple-element.139) | copy-start | bytes 1540
  592.2 78.9 %copy-start.9 = (bf16[512,2048]{1,0:T(8,128)(2,1)S(1)}, bf16[512,2048]{1,0:T(8,128)(2,1)}, u32[]{:S(2)}) copy-start(bf16[512,2048]{1,0:T(8,128)(2,1)} %get-tuple-element.127) | copy-start | bytes 6291460
Sparse Core Ops, SparseCore 0:
  82.0 115.0 all-gather.1
  324.2 197.2 all-reduce.2
  525.6 156.9 reduce-scatter.1
